TPU v7x, 32 devices: a whole 2x2x4 slice. The times are simulated.
32 devices in a mesh: seq: 16 (over z, y, x), dp: 2 (over core).
Axes of the slice: x: 2, y: 2, z: 4, core: 2. Of those that a mesh axis runs over, the one named last changes fastest.
Arguments:
- tokens: bfloat16 [4096, 4096], P(('dp', 'seq')), parts along dimension 0, may hold values from -6 to 6
- sign_in: int32 [4096, 256], P(('dp', 'seq')), parts along dimension 0, may hold values from 0 to 65535
- sign_out: int32 [4096, 32], P(('dp', 'seq')), parts along dimension 0, may hold values from 0 to 65535
- w_value: bfloat16 [4096, 512], P('seq'), may hold values from -0.09375 to 0.09375
- w_noise: bfloat16 [4096, 512], P('seq'), may hold values from -0.046875 to 0.046875
- w_gate: bfloat16 [4096, 512], replicated, may hold values from -0.09375 to 0.09375
- conv_taps: float32 [3, 1024], replicated, may hold values from -3.5 to 3.5
- long_filter: float32 [2048, 512], P('seq'), may hold values from -1.5 to 1.5, as said below
- w_out: bfloat16 [512, 4096], replicated, may hold values from -0.25 to 0.25
Outputs:
- mixed: bfloat16 [4096, 4096], P(('dp', 'seq')), parts along dimension 0
There are 2 independent parts, one for each index of `dp`. A program takes and returns all parts, laid end to end along the dimension named above; an argument that names none is the same for every part. Nothing has to cross between parts.
Inputs may be any that keep to these rules, and one draw needn't show every extreme that they name: `long_filter`: filter taps are real and finite.
All inputs are finite; a program needn't handle non-finite values.
Results may differ from a plain program's by a relative error of at most 0.0064.
Values may be sent and summed in bfloat16 or wider, within the bound.
No kernel may reach another device: no remote copies, remote signals or barrier semaphores. Data moves between devices by JAX's collectives and lax.ppermute only.
A program may use at most 64 MiB of HBM per device.

v0:
```python
import functools

import jax
import jax.numpy as jnp
from jax import lax
from jax.experimental import pallas as pl
from jax.experimental.pallas import tpu as pltpu
from jax.sharding import Mesh, PartitionSpec as P

F32 = jnp.float32
BF16 = jnp.bfloat16
LANES = 128
GROUP = 8
BLOCK = 32
SLOTS = LANES // BLOCK
MIB = 1 << 20
VMEM = pl.BlockSpec(memory_space=pltpu.VMEM)
SMEM = pl.BlockSpec(memory_space=pltpu.SMEM)
HBM = pl.BlockSpec(memory_space=pltpu.HBM)
ANY = pl.BlockSpec(memory_space=pl.ANY)


def params(mib):
    return pltpu.CompilerParams(vmem_limit_bytes=mib * MIB)


def cost(flops, accessed):
    return pl.CostEstimate(flops=flops, bytes_accessed=accessed, transcendentals=0)


def in_hbm(*arrays):
    return [pltpu.with_memory_space_constraint(array, pltpu.HBM) for array in arrays]


def sign_bytes(packed):
    parts = jnp.concatenate([packed & 255, packed >> 8], axis=1)
    return parts.astype(F32).astype(BF16)


def one_hot(rows, columns, source_of):
    at = lax.broadcasted_iota(jnp.int32, (rows, columns), 0)
    column = lax.broadcasted_iota(jnp.int32, (1, columns), 1)
    return (at == source_of(column)).astype(F32).astype(BF16)


def weights_kernel(value_ref, noise_ref, weight_ref, sems):
    half = weight_ref.shape[1] // 2
    columns = pl.ds(pl.multiple_of(lax.axis_index("dp") * half, half), half)
    copies = []
    for at, source in enumerate((value_ref, noise_ref)):
        target = weight_ref.at[:, at * half : (at + 1) * half]
        copies.append(pltpu.make_async_copy(source.at[:, columns], target, sems.at[at]))
        copies[-1].start()
    for copy in copies:
        copy.wait()


def pack_kernel(
    near, far, tokens_ref, in_ref, sent_ref, lags_ref, value_ref, noise_ref, weight_ref, *refs
):
    outs, (in_held, sent_held, lags_held, read_sems, weight_sems, token_sems) = refs[:near], refs[near:]
    core, far_at, near_at = lax.axis_index("dp"), lax.axis_index("far"), lax.axis_index("near")
    half = weight_ref.shape[1] // 2
    share = weight_ref.shape[0]
    depth = share * far
    words = in_ref.shape[1]
    per_part = words // (near * far)
    own_words = per_part * far

    copies = []
    for at, source in enumerate((value_ref, noise_ref)):
        columns = pl.ds(pl.multiple_of(core * half, half), half)
        target = weight_ref.at[:, at * half : (at + 1) * half]
        copies.append(pltpu.make_async_copy(source.at[:, columns], target, weight_sems.at[at]))
    reads = [
        pltpu.make_async_copy(in_ref, in_held, read_sems.at[0]),
        pltpu.make_async_copy(sent_ref, sent_held, read_sems.at[1]),
        pltpu.make_async_copy(
            lags_ref.at[:, pl.ds(pl.multiple_of(core * half, half), half)], lags_held, read_sems.at[2]
        ),
    ]
    for step, out in enumerate(outs):
        for turn in range(far):
            start = ((far_at ^ turn) * near + (near_at ^ step)) * share
            columns = pl.ds(pl.multiple_of(start, share), share)
            target = out.at[:, turn * share : (turn + 1) * share]
            copies.append(
                pltpu.make_async_copy(tokens_ref.at[:, columns], target, token_sems.at[step * far + turn])
            )
    for copy in reads + copies:
        copy.start()

    def word_of(column):
        step, rest = column // (2 * own_words), column % (2 * own_words)
        part, word = rest // own_words, rest % own_words
        plane = (word // per_part) ^ far_at
        return part * words + (plane * near + (step ^ near_at)) * per_part + word % per_part

    by_word = one_hot(2 * words, 2 * words, word_of)
    reads[0].wait()
    moved = jnp.dot(sign_bytes(in_held[...]), by_word, preferred_element_type=F32).astype(BF16)
    reads[1].wait()
    sent = sign_bytes(sent_held[...].astype(F32).T.astype(jnp.int32))
    held = half // (near * far)

    def channel_of(column):
        step, rest = column // (far * held), column % (far * held)
        return (rest // held * near + (step ^ near_at)) * held + rest % held

    reads[2].wait()
    lags = jnp.dot(
        lags_held[...].astype(BF16), one_hot(half, half, channel_of), preferred_element_type=F32
    ).astype(BF16)
    width, own_lags = 2 * own_words, far * held
    for step, out in enumerate(outs):
        out[:, depth : depth + width] = moved[:, step * width : (step + 1) * width]
        out[:, depth + width :] = jnp.concatenate(
            [sent, lags[:, step * own_lags : (step + 1) * own_lags]], axis=1
        )
    for copy in copies:
        copy.wait()


def spread_signs(pair, byte_of, columns):
    spread = jnp.dot(pair, one_hot(pair.shape[1], columns, byte_of), preferred_element_type=F32)
    mask = 1 << (lax.broadcasted_iota(jnp.int32, (1, columns), 1) & 7)
    return jnp.where((spread.astype(jnp.int32) & mask) != 0, 1.0, -1.0)


def spaced(lines, held):
    if held >= GROUP:
        return lines
    spare = jnp.zeros((GROUP - held, lines.shape[1]), F32)
    split = [lines[at : at + held] for at in range(0, lines.shape[0], held)]
    return jnp.concatenate([part for own in split for part in (own, spare)], axis=0)


def project_kernel(near, far, cores, depth, *refs):
    outs, (out_lags_ref, whole_ref) = refs[-2 - near : -2], refs[-2:]
    chunks, pieces = refs[: near * cores][::-1], refs[near * cores : -2 - near]
    core, near_at = lax.axis_index("dp"), lax.axis_index("near")
    rows = chunks[0].shape[0]
    half = pieces[0].shape[1] // 2
    words = depth // 16
    sent_words = cores * half // 16
    sent_start = depth + 2 * words

    def in_byte(column):
        return (column >> 4) + words * ((column >> 3) & 1)

    def out_byte(column):
        return core * (half // 16) + (column >> 4) + sent_words * ((column >> 3) & 1)

    def joined(start, stop):
        return jnp.concatenate([chunk[:, start:stop] for chunk in chunks], axis=0)

    flip_in = spread_signs(joined(depth, sent_start), in_byte, depth).astype(BF16)
    flip_out = spread_signs(joined(sent_start, sent_start + 2 * sent_words), out_byte, half)
    mean_part, noise_part = 0.0, 0.0
    step = depth // len(pieces)
    for at, piece in enumerate(pieces):
        tokens = joined(at * step, (at + 1) * step)
        flipped = tokens * flip_in[:, at * step : (at + 1) * step]
        mean_part += jnp.dot(tokens, piece[:, :half], preferred_element_type=F32)
        noise_part += jnp.dot(flipped, piece[:, half:], preferred_element_type=F32)
    held = half // (near * far)
    stride = max(held, GROUP)
    value = spaced((mean_part + flip_out * noise_part).T, held)
    for part in range(cores):
        for turn in range(near):
            at = part * near + turn
            target = ((core ^ part) * near + (near_at ^ turn)) * rows
            whole_ref[:, pl.ds(pl.multiple_of(target, rows), rows)] = value[:, at * rows : (at + 1) * rows]
    for turn in range(near):
        own_lags = chunks[turn][:, sent_start + 2 * sent_words :].astype(F32).T
        at = pl.multiple_of((near_at ^ turn) * rows, rows)
        out_lags_ref[:, pl.ds(at, rows)] = own_lags
    for turn, out in enumerate(outs):
        for plane in range(far):
            at = pl.multiple_of((plane * near + (near_at ^ turn)) * stride, stride)
            out[plane * held : (plane + 1) * held, :] = whole_ref[pl.ds(at, held), :].astype(BF16)


def sum_kernel(near, far, lags_ref, *refs):
    parts, outs, whole_ref = refs[:near], refs[near : near + far], refs[-1]
    far_at = lax.axis_index("far")
    held = outs[0].shape[0]
    stride = max(held, GROUP)
    span = parts[0].shape[1]
    total = 0.0
    for part in parts:
        total += part[...].astype(F32)
    whole_ref[:, :span] = spaced(total, held)
    whole_ref[:, span:] = spaced(lags_ref[...], held)
    for turn, out in enumerate(outs):
        at = pl.multiple_of((far_at ^ turn) * stride, stride)
        out[...] = whole_ref[pl.ds(at, held), :].astype(BF16)


def shifted(values, steps):
    moved = pltpu.roll(values, steps, 1)
    at = lax.broadcasted_iota(jnp.int32, values.shape, 1)
    return jnp.where(at >= steps, moved, 0.0)


def lane_roll(values, steps):
    return pltpu.roll(values, steps % LANES, values.ndim - 1) if steps % LANES else values


def mix_kernel(near, far, cores, held, taps_ref, *refs):
    parts, (out_ref, left_ref, sums_ref, done_ref, table_ref, lines_ref) = refs[:-6][::-1], refs[-6:]
    tiles = out_ref.shape[0] // cores
    block_rows = cores * GROUP
    tile_rows = SLOTS * block_rows
    rows = tiles * tile_rows
    lane = lax.broadcasted_iota(jnp.int32, (1, LANES), 1)
    pair = 2 * LANES
    span = near * LANES

    def padded(lines):
        if held >= GROUP:
            return lines
        return jnp.concatenate([lines, jnp.zeros((GROUP - held, lines.shape[1]), F32)], axis=0)

    for turn, part in enumerate(parts):
        for plane in range(far // len(parts)):
            own = slice(plane * held, (plane + 1) * held)
            target = pl.multiple_of(((lax.axis_index("far") if len(parts) > 1 else plane) ^ turn) * span, span)
            for line in range(cores + 1):
                piece = part[own, line * span : (line + 1) * span]
                lines_ref[line, :, pl.ds(target, span)] = piece.astype(F32)
    half = held * near * far
    position = lax.axis_index("far") * near + lax.axis_index("near")
    first = lax.axis_index("dp") * half + position * held
    channel = lax.broadcasted_iota(jnp.int32, (held, cores * half), 1) - first
    chosen = channel == lax.broadcasted_iota(jnp.int32, (held, cores * half), 0)
    taps = [
        jnp.sum(jnp.where(chosen, taps_ref[lag : lag + 1, : cores * half], 0.0), axis=1, keepdims=True)
        for lag in range(3)
    ]
    signals = []
    for part in range(cores):
        value = lines_ref[part]
        signal = taps[0] * value
        for lag in range(1, 3):
            signal += taps[lag] * shifted(value, lag)
        signals.append(padded(signal))
    lags = padded(lines_ref[cores])

    for group in range(max(held, GROUP) // GROUP):
        own = slice(group * GROUP, (group + 1) * GROUP)
        for at in range(GROUP):
            row = lags[group * GROUP + at : group * GROUP + at + 1, :]
            repeated = jnp.broadcast_to(row, (BLOCK, row.shape[1]))
            turned = pltpu.roll(repeated, 0, 1, stride=1, stride_axis=0)
            column = lax.broadcasted_iota(jnp.int32, repeated.shape, 1)
            lag = lax.broadcasted_iota(jnp.int32, repeated.shape, 0)
            kept = jnp.where(column >= lag, turned, 0.0).astype(BF16)
            table_ref[at * BLOCK : (at + 1) * BLOCK, :] = kept

        stacked = jnp.concatenate(
            [
                signal[own, a * LANES : (a + 1) * LANES]
                for a in range(tiles)
                for signal in signals
            ],
            axis=0,
        )
        slot_of = lax.broadcasted_iota(jnp.int32, stacked.shape, 0) % SLOTS
        turned = stacked
        for slot in range(1, SLOTS):
            turned = jnp.where(slot_of == slot, lane_roll(stacked, BLOCK * slot), turned)
        spread = jnp.stack(
            [
                lane_roll(turned, -BLOCK * slot).reshape(tiles, block_rows, LANES)
                for slot in range(SLOTS)
            ],
            axis=1,
        ).reshape(rows, LANES)
        owner = lax.broadcasted_iota(jnp.int32, (rows, LANES), 0) % GROUP
        for half in range(GROUP // SLOTS):
            kept = jnp.where(owner == lane // BLOCK + half * SLOTS, spread, 0.0)
            left_ref[:, half * LANES : (half + 1) * LANES] = kept.astype(BF16)

        sums_ref[...] = jnp.zeros_like(sums_ref)
        if tiles <= 16:
            for at in range(tiles // 2):
                start = 2 * at * tile_rows
                partial = jnp.dot(
                    left_ref[: rows - start, :],
                    table_ref[:, at * pair : (at + 1) * pair],
                    preferred_element_type=F32,
                )
                sums_ref[start:rows, :] += partial[:, :LANES]
                sums_ref[start + tile_rows : rows, :] += partial[: rows - start - tile_rows, LANES:]
        else:

            def add(at, _):
                partial = jnp.dot(
                    left_ref[...],
                    table_ref[:, pl.ds(pl.multiple_of(at * pair, pair), pair)],
                    preferred_element_type=F32,
                )
                start = pl.multiple_of(2 * at * tile_rows, tile_rows)
                sums_ref[pl.ds(start, rows), :] += partial[:, :LANES]
                sums_ref[pl.ds(start + tile_rows, rows), :] += partial[:, LANES:]
                return 0

            lax.fori_loop(0, tiles // 2, add, 0)

        sums = sums_ref[:rows, :]
        landed = [0.0] * SLOTS
        for part in range(SLOTS):
            late = sums
            if part:
                ahead = jnp.zeros((part * block_rows, LANES), F32)
                late = jnp.concatenate([ahead, sums[: rows - part * block_rows]], axis=0)
            late = late.reshape(tiles, SLOTS, block_rows, LANES)
            for slot in range(SLOTS):
                moved = late[:, slot].reshape(tiles * block_rows, LANES)
                landed[slot] += lane_roll(moved, BLOCK * (slot - part))
        result = 0.0
        for slot in range(SLOTS):
            result += jnp.where(lane // BLOCK == slot, landed[slot], 0.0)
        result = result.reshape(tiles, cores, GROUP, LANES)
        for part in range(cores):
            done_ref[part * tiles : (part + 1) * tiles, own, :] = result[:, part]

    out_ref[...] = done_ref[:, :held, :].astype(BF16)


def out_kernel(
    gate_ref, before_ref, taps_ref, mixed_ref, source_ref, target_ref,
    gate_held, before_held, taps_held, mixed_held, weight_ref, held_ref, small_sems, read_sems, write_sems,
):
    chunks, channels, step = weight_ref.shape
    small = [
        pltpu.make_async_copy(source, target, small_sems.at[at])
        for at, (source, target) in enumerate(
            (
                (gate_ref, gate_held),
                (before_ref, before_held),
                (taps_ref, taps_held),
                (mixed_ref, mixed_held),
            )
        )
    ]
    reads = [
        pltpu.make_async_copy(
            source_ref.at[:, pl.ds(at * step, step)], weight_ref.at[at], read_sems.at[at]
        )
        for at in range(chunks)
    ]
    for copy in small + reads:
        copy.start()
    for copy in small:
        copy.wait()
    gate = gate_held[...].astype(F32)
    extended = jnp.concatenate([before_held[...].astype(F32), gate], axis=0)
    gate_short = taps_held[0:1, channels:] * gate
    for lag in range(1, 3):
        gate_short += taps_held[lag : lag + 1, channels:] * extended[2 - lag : 2 - lag + gate.shape[0]]
    gated = (gate_short * mixed_held[...].astype(F32).T).astype(BF16)
    writes = []
    for at in range(chunks):
        reads[at].wait()
        held_ref[at] = jnp.dot(gated, weight_ref[at], preferred_element_type=F32).astype(BF16)
        columns = target_ref.at[:, pl.ds(at * step, step)]
        writes.append(pltpu.make_async_copy(held_ref.at[at], columns, write_sems.at[at]))
        writes[-1].start()
    for write in writes:
        write.wait()


def exchanged(value, axis, step):
    return lax.ppermute(value, axis, [(i, i ^ step) for i in range(lax.axis_size(axis))])


def all_exchanged(values, axis):
    result = list(values)
    for step in reversed(range(1, len(values))):
        result[step] = exchanged(values[step], axis, step)
    return result


def on_device(near, far, tokens, sign_in, sign_out, w_value, w_noise, w_gate, conv_taps, long_filter, w_out):
    rows, width = tokens.shape
    channels = w_gate.shape[1]
    cores = lax.axis_size("dp")
    count = near * far
    half = channels // cores
    held = half // count
    share = w_value.shape[0]
    depth = share * far
    length = count * rows
    near_at, core = lax.axis_index("near"), lax.axis_index("dp")

    lags_start = depth + depth // 8 + channels // 8
    packed_width = lags_start + far * held
    if share % LANES == 0 and far == 4:
        first = pl.pallas_call(
            weights_kernel,
            in_specs=[HBM] * 2,
            out_specs=VMEM,
            out_shape=jax.ShapeDtypeStruct((share, 2 * half), BF16),
            scratch_shapes=[pltpu.SemaphoreType.DMA((2,))],
            compiler_params=params(2),
            cost_estimate=cost(0, MIB // 2),
            name="weights",
        )(*in_hbm(w_value, w_noise))
        far_weights = exchanged(first, "far", 2)
        late_tokens, first = lax.optimization_barrier((tokens, first))
        weights, *chunks = pl.pallas_call(
            functools.partial(pack_kernel, near, far),
            in_specs=[HBM] * 6,
            out_specs=[VMEM] * (1 + near),
            out_shape=[jax.ShapeDtypeStruct((share, 2 * half), BF16)]
            + [jax.ShapeDtypeStruct((rows, packed_width), BF16)] * near,
            scratch_shapes=[
                pltpu.VMEM(sign_in.shape, jnp.int32),
                pltpu.VMEM(sign_out.shape[::-1], jnp.int32),
                pltpu.VMEM((rows, half), F32),
                pltpu.SemaphoreType.DMA((3,)),
                pltpu.SemaphoreType.DMA((2,)),
                pltpu.SemaphoreType.DMA((near * far,)),
            ],
            compiler_params=params(16),
            cost_estimate=cost(2 * rows * 512 * 512, 3 * MIB),
            name="pack",
        )(*in_hbm(late_tokens, sign_in, sign_out.T, long_filter, w_value, w_noise))
        pieces = [weights, exchanged(weights, "far", 1), far_weights, None]
    else:
        own = lax.dynamic_slice_in_dim(jnp.stack([w_value, w_noise]), core * half, half, axis=2)
        own = own.transpose(1, 0, 2).reshape(share, 2 * half)
        pieces = [lax.all_gather(own, "far", axis=0, tiled=True)]
        order = jnp.arange(near) ^ near_at

        def by_owner(array):
            parts = array.reshape(rows, far, near, -1).transpose(2, 0, 1, 3).reshape(near, rows, -1)
            return jnp.take(parts, order, axis=0)

        words = by_owner(sign_in)
        sent = jnp.broadcast_to(sign_out[None], (near, *sign_out.shape))
        own_lags = lax.dynamic_slice_in_dim(long_filter, core * half, half, axis=1)
        signs = [words & 255, words >> 8, sent & 255, sent >> 8, by_owner(own_lags)]
        packed = [by_owner(tokens)] + [part.astype(BF16) for part in signs]
        chunks = list(jnp.concatenate(packed, axis=2))
    chunks = all_exchanged(chunks, "near")

    late_tokens = tokens
    if len(pieces) > 1:
        pieces[1], chunks[0] = lax.optimization_barrier((pieces[1], chunks[0]))
        late_tokens, pieces[2] = lax.optimization_barrier((tokens, pieces[2]))
        pieces[3] = exchanged(pieces[2], "far", 1)
    gate_rows = jnp.dot(late_tokens, w_gate, preferred_element_type=F32).astype(BF16)
    *chunks[:0:-1], gate_rows = lax.optimization_barrier((*chunks[:0:-1], gate_rows))
    pieces[-1], chunks[-1] = lax.optimization_barrier((pieces[-1], chunks[-1]))
    chunks += [exchanged(chunk, "dp", 1) for chunk in chunks]

    near_shape = jax.ShapeDtypeStruct((far * held, cores * near * rows), BF16)
    partial = pl.pallas_call(
        functools.partial(project_kernel, near, far, cores, depth),
        in_specs=[VMEM] * (len(chunks) + len(pieces)),
        out_specs=[VMEM] * (near + 1),
        out_shape=[near_shape] * near + [jax.ShapeDtypeStruct((far * held, near * rows), F32)],
        scratch_shapes=[pltpu.VMEM((count * max(held, GROUP), near_shape.shape[1]), F32)],
        compiler_params=params(40),
        cost_estimate=cost(4 * cores * near * rows * depth * half, 6 * MIB),
        name="project",
    )(*chunks[::-1], *pieces)
    *partial, lags = partial
    last_rows, partial[0] = lax.optimization_barrier((gate_rows[rows - 2 :], partial[0]))
    before = lax.ppermute(last_rows, ("far", "near"), [(i, i + 1) for i in range(count - 1)])
    partial = all_exchanged(partial, "near")
    *partial[::-1], before = lax.optimization_barrier((*partial[::-1], before))

    far_shape = (held, (cores + 1) * near * rows)
    parts = pl.pallas_call(
        functools.partial(sum_kernel, near, far),
        in_specs=[VMEM] * (1 + near),
        out_specs=[VMEM] * far,
        out_shape=[jax.ShapeDtypeStruct(far_shape, BF16)] * far,
        scratch_shapes=[pltpu.VMEM((far * max(held, GROUP), far_shape[1]), F32)],
        compiler_params=params(16),
        cost_estimate=cost(MIB, MIB),
        name="sum",
    )(lags, *partial[::-1])
    if far == 4:
        parts = all_exchanged(parts, "far")
    else:
        order = jnp.arange(far) ^ lax.axis_index("far")
        parts = lax.all_to_all(jnp.take(jnp.stack(parts), order, axis=0), "far", 0, 0, tiled=True)
        parts = [parts.reshape(far * held, far_shape[1])]

    tiles = length // LANES
    all_rows = tiles * SLOTS * cores * GROUP
    held_rows = max(held, GROUP)
    mixed = pl.pallas_call(
        functools.partial(mix_kernel, near, far, cores, held),
        in_specs=[VMEM] * (1 + len(parts)),
        out_specs=VMEM,
        out_shape=jax.ShapeDtypeStruct((cores * tiles, held, LANES), BF16),
        scratch_shapes=[
            pltpu.VMEM((all_rows, GROUP * BLOCK), BF16),
            pltpu.VMEM((all_rows * (1 if tiles <= 16 else 2), LANES), F32),
            pltpu.VMEM((cores * tiles, held_rows, LANES), F32),
            pltpu.VMEM((GROUP * BLOCK, length), BF16),
            pltpu.VMEM((cores + 1, held, length), F32),
        ],
        compiler_params=params(48),
        cost_estimate=cost(cores * held_rows * BLOCK * length * 256, 2 * MIB),
        name="mix",
    )(conv_taps, *parts[::-1])

    landed = lax.all_to_all(mixed, ("dp", "far", "near"), 0, 0, tiled=True).reshape(channels, rows)
    chunks = 8
    return pl.pallas_call(
        out_kernel,
        in_specs=[ANY] * 4 + [HBM],
        out_specs=HBM,
        out_shape=jax.ShapeDtypeStruct((rows, width), BF16),
        scratch_shapes=[
            pltpu.VMEM(gate_rows.shape, BF16),
            pltpu.VMEM(before.shape, BF16),
            pltpu.VMEM(conv_taps.shape, F32),
            pltpu.VMEM(landed.shape, BF16),
            pltpu.VMEM((chunks, channels, width // chunks), BF16),
            pltpu.VMEM((chunks, rows, width // chunks), BF16),
            pltpu.SemaphoreType.DMA((4,)),
            pltpu.SemaphoreType.DMA((chunks,)),
            pltpu.SemaphoreType.DMA((chunks,)),
        ],
        compiler_params=params(16),
        cost_estimate=cost(2 * rows * width * channels, 5 * MIB),
        name="project_out",
    )(gate_rows, before, conv_taps, landed, *in_hbm(w_out))


def solution(mesh):
    count = mesh.shape["seq"]
    near = 4 if count % 4 == 0 else 1
    far = count // near
    seq_at = mesh.axis_names.index("seq")
    shape = list(mesh.devices.shape)
    shape[seq_at : seq_at + 1] = [far, near]
    names = list(mesh.axis_names)
    names[seq_at : seq_at + 1] = ["far", "near"]
    inner = Mesh(mesh.devices.reshape(shape), tuple(names))
    by_token = P(("dp", "far", "near"), None)
    by_row = P(("far", "near"), None)
    placed = (by_token, by_token, by_token, by_row, by_row, P(), P(), by_row, P())
    return jax.shard_map(
        functools.partial(on_device, near, far),
        mesh=inner,
        in_specs=placed,
        out_specs=by_token,
        check_vma=False,
    )
```

profile of v0, /device:TPU:0, one launch (start us, length us, event | category | flops | bytes accessed | tf_op | source)
XLA Modules:
  0.0 65.7 jit_solution(18197263660138269390)
XLA Ops:
  0.0 1.0 %weights.1 = bf16[256,512]{1,0:T(8,128)(2,1)S(1)} custom-call(bf16[256,512]{1,0:T(8,128)(2,1)} %value_ref.3, bf16[256,512]{1,0:T(8,128)(2,1)} %noise_ref.3), custom_call_target="tpu_custom_call" | custom-call | bytes 524288 | tf_op jit(solution)/shard_map/weights/pallas_call | solution.py:401
  1.0 4.1 %collective-permute-start.3 = (bf16[256,512]{1,0:T(8,128)(2,1)S(1)}, bf16[256,512]{1,0:T(8,128)(2,1)S(1)}, u32[]{:S(2)}, u32[]{:S(2)}) collective-permute-start(bf16[256,512]{1,0:T(8,128)(2,1)S(1)} %weights.1), channel_id=1, source_target_pairs={{0,16},{8,24},{16,0},{24,8},{1,17},{9,25},{17,1},{25,9},{2,18},{10... | collective-permute-start | bytes 786440 | tf_op jit(solution)/shard_map/ppermute | solution.py:376
  5.1 2.2 %pack.1 = (bf16[256,512]{1,0:T(8,128)(2,1)S(1)}, bf16[128,1280]{1,0:T(8,128)(2,1)S(1)}, bf16[128,1280]{1,0:T(8,128)(2,1)S(1)}, bf16[128,1280]{1,0:T(8,128)(2,1)S(1)}, bf16[128,1280]{1,0:T(8,128)(2,1)S(1)}) custom-call(bf16[128,4096]{1,0:T(8,128)(2,1)} %tokens_ref, s32[128,256]{1,0:T(8,128)} %in_ref.1, s32[32,128]{1,0:T(8,128)} %bitcast.5, ...), custom_call_target="tpu_custom_call" | custom-call | flops 67108864 | bytes 3145728 | tf_op jit(solution)/shard_map/pack/pallas_call | solution.py:413
  7.3 1.6 %collective-permute-start.8 = (bf16[256,512]{1,0:T(8,128)(2,1)S(1)}, bf16[256,512]{1,0:T(8,128)(2,1)S(1)}, u32[]{:S(2)}, u32[]{:S(2)}) collective-permute-start(bf16[256,512]{1,0:T(8,128)(2,1)S(1)} %get-tuple-element.48.refs_8_), channel_id=1, source_target_pairs={{0,8},{8,0},{16,24},{24,16},{1,9},{9,1},{17,25},{25,17},{2,10},{10... | collective-permute-start | bytes 786440 | tf_op jit(solution)/shard_map/ppermute | solution.py:376
  8.9 2.4 %collective-permute-start = (bf16[128,1280]{1,0:T(8,128)(2,1)S(1)}, bf16[128,1280]{1,0:T(8,128)(2,1)S(1)}, u32[]{:S(2)}, u32[]{:S(2)}) collective-permute-start(bf16[128,1280]{1,0:T(8,128)(2,1)S(1)} %get-tuple-element.38), channel_id=1, source_target_pairs={{0,6},{2,4},{4,2},{6,0},{1,7},{3,5},{5,3},{7,1},{8,14},{10,12},{12... | collective-permute-start | bytes 983048 | tf_op jit(solution)/shard_map/ppermute | solution.py:376
  12.4 4.7 %collective-permute-done.3.refs_10_ = bf16[256,512]{1,0:T(8,128)(2,1)S(1)} collective-permute-done((bf16[256,512]{1,0:T(8,128)(2,1)S(1)}, bf16[256,512]{1,0:T(8,128)(2,1)S(1)}, u32[]{:S(2)}, u32[]{:S(2)}) %collective-permute-start.3) | collective-permute-done | bytes 262176 | tf_op jit(solution)/shard_map/ppermute | solution.py:376
  17.1 0.7 %collective-permute-start.4 = (bf16[256,512]{1,0:T(8,128)(2,1)S(1)}, bf16[256,512]{1,0:T(8,128)(2,1)S(1)}, u32[]{:S(2)}, u32[]{:S(2)}) collective-permute-start(bf16[256,512]{1,0:T(8,128)(2,1)S(1)} %collective-permute-done.3.refs_10_), channel_id=1, source_target_pairs={{0,8},{8,0},{16,24},{24,16},{1,9},{9,1},{17,25},{25,17},{2,10},{10... | collective-permute-start | bytes 786440 | tf_op jit(solution)/shard_map/ppermute | solution.py:376
  17.8 2.3 %collective-permute-done.8.refs_9_ = bf16[256,512]{1,0:T(8,128)(2,1)S(1)} collective-permute-done((bf16[256,512]{1,0:T(8,128)(2,1)S(1)}, bf16[256,512]{1,0:T(8,128)(2,1)S(1)}, u32[]{:S(2)}, u32[]{:S(2)}) %collective-permute-start.8) | collective-permute-done | bytes 262176 | tf_op jit(solution)/shard_map/ppermute | solution.py:376
  20.1 3.2 %convolution_convert_fusion.gate_ref = bf16[128,512]{1,0:T(8,128)(2,1)S(1)} fusion(bf16[128,4096]{1,0:T(8,128)(2,1)} %tokens_ref, bf16[4096,512]{1,0:T(8,128)(2,1)} %param.14), kind=kOutput, calls=%fused_computation | convolution fusion | flops 536936448 | bytes 5373952 | tf_op jit(solution)/shard_map/dot_general | solution.py:455
  23.4 2.3 %collective-permute-done.1.refs_5_ = bf16[128,1280]{1,0:T(8,128)(2,1)S(1)} collective-permute-done((bf16[128,1280]{1,0:T(8,128)(2,1)S(1)}, bf16[128,1280]{1,0:T(8,128)(2,1)S(1)}, u32[]{:S(2)}, u32[]{:S(2)}) %collective-permute-start.1) | collective-permute-done | bytes 327712 | tf_op jit(solution)/shard_map/ppermute | solution.py:376
  26.3 1.1 %collective-permute-done.6.refs_1_ = bf16[128,1280]{1,0:T(8,128)(2,1)S(1)} collective-permute-done((bf16[128,1280]{1,0:T(8,128)(2,1)S(1)}, bf16[128,1280]{1,0:T(8,128)(2,1)S(1)}, u32[]{:S(2)}, u32[]{:S(2)}) %collective-permute-start.6) | collective-permute-done | bytes 327712 | tf_op jit(solution)/shard_map/ppermute | solution.py:376
  28.4 2.2 %project.1 = (bf16[64,1024]{1,0:T(8,128)(2,1)S(1)}, bf16[64,1024]{1,0:T(8,128)(2,1)S(1)}, bf16[64,1024]{1,0:T(8,128)(2,1)S(1)}, bf16[64,1024]{1,0:T(8,128)(2,1)S(1)}, f32[64,512]{1,0:T(8,128)S(1)}) custom-call(bf16[128,1280]{1,0:T(8,128)(2,1)S(1)} %collective-permute-done.5.refs_0_, bf16[128,1280]{1,0:T(8,128)(2,1)S(1)} %collective-permute-done.6.refs_1_, ...), custom_call_target="tpu_custom_call" | custom-call | flops 1073741824 | bytes 6291456 | tf_op jit(solution)/shard_map/project/pallas_call | solution.py:461
  30.5 1.7 %collective-permute-start.10 = (bf16[64,1024]{1,0:T(8,128)(2,1)S(1)}, bf16[64,1024]{1,0:T(8,128)(2,1)S(1)}, u32[]{:S(2)}, u32[]{:S(2)}) collective-permute-start(bf16[64,1024]{1,0:T(8,128)(2,1)S(1)} %get-tuple-element.53), channel_id=1, source_target_pairs={{0,6},{2,4},{4,2},{6,0},{1,7},{3,5},{5,3},{7,1},{8,14},{10,12},{12... | collective-permute-start | bytes 393224 | tf_op jit(solution)/shard_map/ppermute | solution.py:376
  32.3 1.3 %collective-permute-start.11 = (bf16[64,1024]{1,0:T(8,128)(2,1)S(1)}, bf16[64,1024]{1,0:T(8,128)(2,1)S(1)}, u32[]{:S(2)}, u32[]{:S(2)}) collective-permute-start(bf16[64,1024]{1,0:T(8,128)(2,1)S(1)} %get-tuple-element.54), channel_id=1, source_target_pairs={{0,4},{2,6},{4,0},{6,2},{1,5},{3,7},{5,1},{7,3},{8,12},{10,14},{12... | collective-permute-start | bytes 393224 | tf_op jit(solution)/shard_map/ppermute | solution.py:376
  34.1 3.4 %collective-permute-start.13 = (bf16[2,512]{1,0:T(2,128)(2,1)S(1)}, bf16[2,512]{1,0:T(2,128)(2,1)S(1)}, u32[]{:S(2)}, u32[]{:S(2)}) collective-permute-start(bf16[2,512]{1,0:T(2,128)(2,1)S(1)} %slice.3), channel_id=1, source_target_pairs={{0,2},{2,4},{4,6},{6,8},{8,10},{10,12},{12,14},{14,16},{16,18},{18... | collective-permute-start | bytes 6152 | tf_op jit(solution)/shard_map/ppermute | solution.py:473
  37.5 1.3 %collective-permute-done.13.before_ref = bf16[2,512]{1,0:T(2,128)(2,1)S(1)} collective-permute-done((bf16[2,512]{1,0:T(2,128)(2,1)S(1)}, bf16[2,512]{1,0:T(2,128)(2,1)S(1)}, u32[]{:S(2)}, u32[]{:S(2)}) %collective-permute-start.13) | collective-permute-done | bytes 2080 | tf_op jit(solution)/shard_map/ppermute | solution.py:473
  38.8 1.1 %collective-permute-done.11.refs_1_ = bf16[64,1024]{1,0:T(8,128)(2,1)S(1)} collective-permute-done((bf16[64,1024]{1,0:T(8,128)(2,1)S(1)}, bf16[64,1024]{1,0:T(8,128)(2,1)S(1)}, u32[]{:S(2)}, u32[]{:S(2)}) %collective-permute-start.11) | collective-permute-done | bytes 131104 | tf_op jit(solution)/shard_map/ppermute | solution.py:376
  40.0 3.7 %collective-permute-start.14 = (bf16[16,1536]{1,0:T(8,128)(2,1)S(1)}, bf16[16,1536]{1,0:T(8,128)(2,1)S(1)}, u32[]{:S(2)}, u32[]{:S(2)}) collective-permute-start(bf16[16,1536]{1,0:T(8,128)(2,1)S(1)} %get-tuple-element.65), channel_id=1, source_target_pairs={{0,24},{8,16},{16,8},{24,0},{1,25},{9,17},{17,9},{25,1},{2,26},{10... | collective-permute-start | bytes 147464 | tf_op jit(solution)/shard_map/ppermute | solution.py:376
  43.7 0.8 %collective-permute-start.16 = (bf16[16,1536]{1,0:T(8,128)(2,1)S(1)}, bf16[16,1536]{1,0:T(8,128)(2,1)S(1)}, u32[]{:S(2)}, u32[]{:S(2)}) collective-permute-start(bf16[16,1536]{1,0:T(8,128)(2,1)S(1)} %get-tuple-element.67), channel_id=1, source_target_pairs={{0,8},{8,0},{16,24},{24,16},{1,9},{9,1},{17,25},{25,17},{2,10},{10... | collective-permute-start | bytes 147464 | tf_op jit(solution)/shard_map/ppermute | solution.py:376
  44.4 1.7 %collective-permute-done.14.refs_0_ = bf16[16,1536]{1,0:T(8,128)(2,1)S(1)} collective-permute-done((bf16[16,1536]{1,0:T(8,128)(2,1)S(1)}, bf16[16,1536]{1,0:T(8,128)(2,1)S(1)}, u32[]{:S(2)}, u32[]{:S(2)}) %collective-permute-start.14) | collective-permute-done | bytes 49184 | tf_op jit(solution)/shard_map/ppermute | solution.py:376
  46.1 2.5 %collective-permute-done.15.refs_1_ = bf16[16,1536]{1,0:T(8,128)(2,1)S(1)} collective-permute-done((bf16[16,1536]{1,0:T(8,128)(2,1)S(1)}, bf16[16,1536]{1,0:T(8,128)(2,1)S(1)}, u32[]{:S(2)}, u32[]{:S(2)}) %collective-permute-start.15) | collective-permute-done | bytes 49184 | tf_op jit(solution)/shard_map/ppermute | solution.py:376
  48.6 2.5 %mix.1 = bf16[32,16,128]{2,1,0:T(8,128)(2,1)S(1)} custom-call(f32[3,1024]{1,0:T(4,128)S(1)} %copy-done, bf16[16,1536]{1,0:T(8,128)(2,1)S(1)} %collective-permute-done.14.refs_0_, bf16[16,1536]{1,0:T(8,128)(2,1)S(1)} %collective-permute-done.15.refs_1_, bf16[16,1536]{1,0:T(8,128)(2,1)S(1)} %collective-permute-done.16.refs_2_, ...), custom_call_target="tpu_custom_call" | custom-call | flops 536870912 | bytes 2097152 | tf_op jit(solution)/shard_map/mix/pallas_call | solution.py:498
  51.2 10.4 %all_to_all.5 = bf16[32,16,128]{2,1,0:T(8,128)(2,1)S(1)} all-to-all(bf16[32,16,128]{2,1,0:T(8,128)(2,1)S(1)} %mix.1), channel_id=1, replica_groups=mesh['far'=4,'near'=4,'dp'=2] {'dp','far','near'}, dimensions={0} | all-to-all | bytes 262144 | tf_op jit(solution)/shard_map/all_to_all | solution.py:515
  61.6 4.1 %project_out.1 = bf16[128,4096]{1,0:T(8,128)(2,1)} custom-call(bf16[128,512]{1,0:T(8,128)(2,1)S(1)} %convolution_convert_fusion.gate_ref, bf16[2,512]{1,0:T(2,128)(2,1)S(1)} %collective-permute-done.13.before_ref, f32[3,1024]{1,0:T(4,128)S(1)} %copy-done, bf16[512,128]{1,0:T(8,128)(2,1)S(1)} %bitcast.4, bf16[512,4096]{1,0:T(8,128)(2,1)} %source_ref.1), custom_call_target="tpu_custom_call" | custom-call | flops 536870912 | bytes 5242880 | tf_op jit(solution)/shard_map/project_out/pallas_call | solution.py:517
  (21 shorter events, 3.3 us)
Async XLA Ops:
  1.0 16.1 %collective-permute-start.3 = (bf16[256,512]{1,0:T(8,128)(2,1)S(1)}, bf16[256,512]{1,0:T(8,128)(2,1)S(1)}, u32[]{:S(2)}, u32[]{:S(2)}) collective-permute-start(bf16[256,512]{1,0:T(8,128)(2,1)S(1)} %weights.1), channel_id=1, source_target_pairs={{0,16},{8,24},{16,0},{24,8},{1,17},{9,25},{17,1},{25,9},{2,18},{10... | collective-permute-start | bytes 786440 | tf_op jit(solution)/shard_map/ppermute | solution.py:376
  7.3 12.8 %collective-permute-start.8 = (bf16[256,512]{1,0:T(8,128)(2,1)S(1)}, bf16[256,512]{1,0:T(8,128)(2,1)S(1)}, u32[]{:S(2)}, u32[]{:S(2)}) collective-permute-start(bf16[256,512]{1,0:T(8,128)(2,1)S(1)} %get-tuple-element.48.refs_8_), channel_id=1, source_target_pairs={{0,8},{8,0},{16,24},{24,16},{1,9},{9,1},{17,25},{25,17},{2,10},{10... | collective-permute-start | bytes 786440 | tf_op jit(solution)/shard_map/ppermute | solution.py:376
  8.9 14.5 %collective-permute-start = (bf16[128,1280]{1,0:T(8,128)(2,1)S(1)}, bf16[128,1280]{1,0:T(8,128)(2,1)S(1)}, u32[]{:S(2)}, u32[]{:S(2)}) collective-permute-start(bf16[128,1280]{1,0:T(8,128)(2,1)S(1)} %get-tuple-element.38), channel_id=1, source_target_pairs={{0,6},{2,4},{4,2},{6,0},{1,7},{3,5},{5,3},{7,1},{8,14},{10,12},{12... | collective-permute-start | bytes 983048 | tf_op jit(solution)/shard_map/ppermute | solution.py:376
  11.4 14.4 %collective-permute-start.1 = (bf16[128,1280]{1,0:T(8,128)(2,1)S(1)}, bf16[128,1280]{1,0:T(8,128)(2,1)S(1)}, u32[]{:S(2)}, u32[]{:S(2)}) collective-permute-start(bf16[128,1280]{1,0:T(8,128)(2,1)S(1)} %get-tuple-element.39), channel_id=1, source_target_pairs={{0,4},{2,6},{4,0},{6,2},{1,5},{3,7},{5,1},{7,3},{8,12},{10,14},{12... | collective-permute-start | bytes 983048 | tf_op jit(solution)/shard_map/ppermute | solution.py:376
  11.9 14.0 %collective-permute-start.2 = (bf16[128,1280]{1,0:T(8,128)(2,1)S(1)}, bf16[128,1280]{1,0:T(8,128)(2,1)S(1)}, u32[]{:S(2)}, u32[]{:S(2)}) collective-permute-start(bf16[128,1280]{1,0:T(8,128)(2,1)S(1)} %get-tuple-element.40), channel_id=1, source_target_pairs={{0,2},{2,0},{4,6},{6,4},{1,3},{3,1},{5,7},{7,5},{8,10},{10,8},{12,... | collective-permute-start | bytes 983048 | tf_op jit(solution)/shard_map/ppermute | solution.py:376
  17.1 9.2 %collective-permute-start.4 = (bf16[256,512]{1,0:T(8,128)(2,1)S(1)}, bf16[256,512]{1,0:T(8,128)(2,1)S(1)}, u32[]{:S(2)}, u32[]{:S(2)}) collective-permute-start(bf16[256,512]{1,0:T(8,128)(2,1)S(1)} %collective-permute-done.3.refs_10_), channel_id=1, source_target_pairs={{0,8},{8,0},{16,24},{24,16},{1,9},{9,1},{17,25},{25,17},{2,10},{10... | collective-permute-start | bytes 786440 | tf_op jit(solution)/shard_map/ppermute | solution.py:376
  20.1 28.5 %copy-start = (f32[3,1024]{1,0:T(4,128)S(1)}, f32[3,1024]{1,0:T(4,128)}, u32[]{:S(2)}) copy-start(f32[3,1024]{1,0:T(4,128)} %taps_ref.3) | copy-start | bytes 36868
  20.1 6.2 %collective-permute-start.9 = (bf16[128,1280]{1,0:T(8,128)(2,1)S(1)}, bf16[128,1280]{1,0:T(8,128)(2,1)S(1)}, u32[]{:S(2)}, u32[]{:S(2)}) collective-permute-start(bf16[128,1280]{1,0:T(8,128)(2,1)S(1)} %get-tuple-element.50.refs_7_), channel_id=1, source_target_pairs={{0,1},{1,0},{2,3},{3,2},{4,5},{5,4},{6,7},{7,6},{8,9},{9,8},{10,11... | collective-permute-start | bytes 983048 | tf_op jit(solution)/shard_map/ppermute | solution.py:376
  25.8 1.6 %collective-permute-start.6 = (bf16[128,1280]{1,0:T(8,128)(2,1)S(1)}, bf16[128,1280]{1,0:T(8,128)(2,1)S(1)}, u32[]{:S(2)}, u32[]{:S(2)}) collective-permute-start(bf16[128,1280]{1,0:T(8,128)(2,1)S(1)} %collective-permute-done.1.refs_5_), channel_id=1, source_target_pairs={{0,1},{1,0},{2,3},{3,2},{4,5},{5,4},{6,7},{7,6},{8,9},{9,8},{10,11... | collective-permute-start | bytes 983048 | tf_op jit(solution)/shard_map/ppermute | solution.py:376
  25.8 2.1 %collective-permute-start.7 = (bf16[128,1280]{1,0:T(8,128)(2,1)S(1)}, bf16[128,1280]{1,0:T(8,128)(2,1)S(1)}, u32[]{:S(2)}, u32[]{:S(2)}) collective-permute-start(bf16[128,1280]{1,0:T(8,128)(2,1)S(1)} %collective-permute-done.2.refs_6_), channel_id=1, source_target_pairs={{0,1},{1,0},{2,3},{3,2},{4,5},{5,4},{6,7},{7,6},{8,9},{9,8},{10,11... | collective-permute-start | bytes 983048 | tf_op jit(solution)/shard_map/ppermute | solution.py:376
  26.3 2.1 %collective-permute-start.5 = (bf16[128,1280]{1,0:T(8,128)(2,1)S(1)}, bf16[128,1280]{1,0:T(8,128)(2,1)S(1)}, u32[]{:S(2)}, u32[]{:S(2)}) collective-permute-start(bf16[128,1280]{1,0:T(8,128)(2,1)S(1)} %collective-permute-done.refs_4_), channel_id=1, source_target_pairs={{0,1},{1,0},{2,3},{3,2},{4,5},{5,4},{6,7},{7,6},{8,9},{9,8},{10,11... | collective-permute-start | bytes 983048 | tf_op jit(solution)/shard_map/ppermute | solution.py:376
  30.5 8.2 %collective-permute-start.10 = (bf16[64,1024]{1,0:T(8,128)(2,1)S(1)}, bf16[64,1024]{1,0:T(8,128)(2,1)S(1)}, u32[]{:S(2)}, u32[]{:S(2)}) collective-permute-start(bf16[64,1024]{1,0:T(8,128)(2,1)S(1)} %get-tuple-element.53), channel_id=1, source_target_pairs={{0,6},{2,4},{4,2},{6,0},{1,7},{3,5},{5,3},{7,1},{8,14},{10,12},{12... | collective-permute-start | bytes 393224 | tf_op jit(solution)/shard_map/ppermute | solution.py:376
  32.3 7.6 %collective-permute-start.11 = (bf16[64,1024]{1,0:T(8,128)(2,1)S(1)}, bf16[64,1024]{1,0:T(8,128)(2,1)S(1)}, u32[]{:S(2)}, u32[]{:S(2)}) collective-permute-start(bf16[64,1024]{1,0:T(8,128)(2,1)S(1)} %get-tuple-element.54), channel_id=1, source_target_pairs={{0,4},{2,6},{4,0},{6,2},{1,5},{3,7},{5,1},{7,3},{8,12},{10,14},{12... | collective-permute-start | bytes 393224 | tf_op jit(solution)/shard_map/ppermute | solution.py:376
  33.6 6.3 %collective-permute-start.12 = (bf16[64,1024]{1,0:T(8,128)(2,1)S(1)}, bf16[64,1024]{1,0:T(8,128)(2,1)S(1)}, u32[]{:S(2)}, u32[]{:S(2)}) collective-permute-start(bf16[64,1024]{1,0:T(8,128)(2,1)S(1)} %get-tuple-element.55), channel_id=1, source_target_pairs={{0,2},{2,0},{4,6},{6,4},{1,3},{3,1},{5,7},{7,5},{8,10},{10,8},{12,... | collective-permute-start | bytes 393224 | tf_op jit(solution)/shard_map/ppermute | solution.py:376
  34.1 4.7 %collective-permute-start.13 = (bf16[2,512]{1,0:T(2,128)(2,1)S(1)}, bf16[2,512]{1,0:T(2,128)(2,1)S(1)}, u32[]{:S(2)}, u32[]{:S(2)}) collective-permute-start(bf16[2,512]{1,0:T(2,128)(2,1)S(1)} %slice.3), channel_id=1, source_target_pairs={{0,2},{2,4},{4,6},{6,8},{8,10},{10,12},{12,14},{14,16},{16,18},{18... | collective-permute-start | bytes 6152 | tf_op jit(solution)/shard_map/ppermute | solution.py:473
  40.0 6.2 %collective-permute-start.14 = (bf16[16,1536]{1,0:T(8,128)(2,1)S(1)}, bf16[16,1536]{1,0:T(8,128)(2,1)S(1)}, u32[]{:S(2)}, u32[]{:S(2)}) collective-permute-start(bf16[16,1536]{1,0:T(8,128)(2,1)S(1)} %get-tuple-element.65), channel_id=1, source_target_pairs={{0,24},{8,16},{16,8},{24,0},{1,25},{9,17},{17,9},{25,1},{2,26},{10... | collective-permute-start | bytes 147464 | tf_op jit(solution)/shard_map/ppermute | solution.py:376
  43.7 5.0 %collective-permute-start.15 = (bf16[16,1536]{1,0:T(8,128)(2,1)S(1)}, bf16[16,1536]{1,0:T(8,128)(2,1)S(1)}, u32[]{:S(2)}, u32[]{:S(2)}) collective-permute-start(bf16[16,1536]{1,0:T(8,128)(2,1)S(1)} %get-tuple-element.66), channel_id=1, source_target_pairs={{0,16},{8,24},{16,0},{24,8},{1,17},{9,25},{17,1},{25,9},{2,18},{10... | collective-permute-start | bytes 147464 | tf_op jit(solution)/shard_map/ppermute | solution.py:376
  43.7 5.0 %collective-permute-start.16 = (bf16[16,1536]{1,0:T(8,128)(2,1)S(1)}, bf16[16,1536]{1,0:T(8,128)(2,1)S(1)}, u32[]{:S(2)}, u32[]{:S(2)}) collective-permute-start(bf16[16,1536]{1,0:T(8,128)(2,1)S(1)} %get-tuple-element.67), channel_id=1, source_target_pairs={{0,8},{8,0},{16,24},{24,16},{1,9},{9,1},{17,25},{25,17},{2,10},{10... | collective-permute-start | bytes 147464 | tf_op jit(solution)/shard_map/ppermute | solution.py:376
where the time goes:
time: 65.9 us; the launch traced here: 65.7 us
  starting transfers between devices  21.8 us (33%)
  waiting for transfers between devices  18.1 us (27%)
  Pallas kernels  12 us (18%)
  blocking collectives  10.4 us (16%)
  matrix products  3.24 us (5%)
    ppermute x16, starting transfers between devices, exchanged(): lax.ppermute(value, axis, [(i, i ^ step) for i in range(lax.axis_size(axi...  18.4 us
    ppermute x16, waiting for transfers between devices, exchanged(): lax.ppermute(value, axis, [(i, i ^ step) for i in range(lax.axis_size(axi...  16.8 us
    all_to_all x1, blocking collectives, on_device(): lax.all_to_all(mixed, ('dp', 'far', 'near'), 0, 0, tiled=True)  10.4 us
    pallas_call x1, Pallas kernels, on_device(): pl.pallas_call(out_kernel, in_specs=[ANY] * 4 + [HBM], out_specs=HBM, out...  4.08 us
    ppermute x1, starting transfers between devices, on_device(): lax.ppermute(last_rows, ('far', 'near'), [(i, i + 1) for i in range(count...  3.38 us
    dot_general x1, matrix products, on_device(): jnp.dot(late_tokens, w_gate, preferred_element_type=F32).astype(BF16)  3.24 us
    pallas_call x1, Pallas kernels, on_device(): pl.pallas_call(functools.partial(mix_kernel, near, far, cores, held), in_...  2.51 us
    pallas_call x1, Pallas kernels, on_device(): pl.pallas_call(functools.partial(pack_kernel, near, far), in_specs=[HBM]...  2.16 us
  transfers between devices with their start and end apart: 17, of which 11 were waited for; matrix products, arithmetic and copies ran while one was open for 5% of the time, Pallas kernels for 3%

commit v1 on v0

--- a/solution.py
+++ b/solution.py
@@ -136,8 +136,9 @@
 
 
 def project_kernel(near, far, cores, depth, *refs):
-    outs, (out_lags_ref, whole_ref) = refs[-2 - near : -2], refs[-2:]
-    chunks, pieces = refs[: near * cores][::-1], refs[near * cores : -2 - near]
+    whole_ref, lines_ref = refs[-2:]
+    outs, lag_outs = refs[-2 - near - far : -2 - far], refs[-2 - far : -2]
+    chunks, pieces = refs[: near * cores][::-1], refs[near * cores : -2 - near - far]
     core, near_at = lax.axis_index("dp"), lax.axis_index("near")
     rows = chunks[0].shape[0]
     half = pieces[0].shape[1] // 2
@@ -174,24 +175,25 @@
     for turn in range(near):
         own_lags = chunks[turn][:, sent_start + 2 * sent_words :].astype(F32).T
         at = pl.multiple_of((near_at ^ turn) * rows, rows)
-        out_lags_ref[:, pl.ds(at, rows)] = own_lags
+        lines_ref[:, pl.ds(at, rows)] = spaced(own_lags, held)
+    for turn, out in enumerate(lag_outs):
+        at = pl.multiple_of((lax.axis_index("far") ^ turn) * stride, stride)
+        out[...] = lines_ref[pl.ds(at, held), :].astype(BF16)
     for turn, out in enumerate(outs):
         for plane in range(far):
             at = pl.multiple_of((plane * near + (near_at ^ turn)) * stride, stride)
             out[plane * held : (plane + 1) * held, :] = whole_ref[pl.ds(at, held), :].astype(BF16)
 
 
-def sum_kernel(near, far, lags_ref, *refs):
+def sum_kernel(near, far, *refs):
     parts, outs, whole_ref = refs[:near], refs[near : near + far], refs[-1]
     far_at = lax.axis_index("far")
     held = outs[0].shape[0]
     stride = max(held, GROUP)
-    span = parts[0].shape[1]
     total = 0.0
     for part in parts:
         total += part[...].astype(F32)
-    whole_ref[:, :span] = spaced(total, held)
-    whole_ref[:, span:] = spaced(lags_ref[...], held)
+    whole_ref[...] = spaced(total, held)
     for turn, out in enumerate(outs):
         at = pl.multiple_of((far_at ^ turn) * stride, stride)
         out[...] = whole_ref[pl.ds(at, held), :].astype(BF16)
@@ -207,28 +209,46 @@
     return pltpu.roll(values, steps % LANES, values.ndim - 1) if steps % LANES else values
 
 
-def mix_kernel(near, far, cores, held, taps_ref, *refs):
-    parts, (out_ref, left_ref, sums_ref, done_ref, table_ref, lines_ref) = refs[:-6][::-1], refs[-6:]
+def laid_out(far, held, parts, lines_ref):
+    span = lines_ref.shape[2] // far
+    for turn, part in enumerate(parts):
+        for plane in range(far // len(parts)):
+            own = slice(plane * held, (plane + 1) * held)
+            target = ((lax.axis_index("far") if len(parts) > 1 else plane) ^ turn) * span
+            for line in range(lines_ref.shape[0]):
+                piece = part[own, line * span : (line + 1) * span]
+                lines_ref[line, :, pl.ds(pl.multiple_of(target, span), span)] = piece.astype(F32)
+
+
+def padded(lines):
+    if lines.shape[0] >= GROUP:
+        return lines
+    spare = jnp.zeros((GROUP - lines.shape[0], lines.shape[1]), F32)
+    return jnp.concatenate([lines, spare], axis=0)
+
+
+def table_kernel(far, held, *refs):
+    parts, (out_ref, lines_ref) = refs[:-2][::-1], refs[-2:]
+    laid_out(far, held, parts, lines_ref)
+    lags = padded(lines_ref[0])
+    for at in range(lags.shape[0]):
+        repeated = jnp.broadcast_to(lags[at : at + 1, :], (BLOCK, lags.shape[1]))
+        turned = pltpu.roll(repeated, 0, 1, stride=1, stride_axis=0)
+        column = lax.broadcasted_iota(jnp.int32, repeated.shape, 1)
+        lag = lax.broadcasted_iota(jnp.int32, repeated.shape, 0)
+        kept = jnp.where(column >= lag, turned, 0.0).astype(BF16)
+        out_ref[at * BLOCK : (at + 1) * BLOCK, :] = kept
+
+
+def mix_kernel(near, far, cores, held, taps_ref, full_ref, *refs):
+    parts, (out_ref, left_ref, sums_ref, done_ref, lines_ref) = refs[:-5][::-1], refs[-5:]
     tiles = out_ref.shape[0] // cores
     block_rows = cores * GROUP
     tile_rows = SLOTS * block_rows
     rows = tiles * tile_rows
     lane = lax.broadcasted_iota(jnp.int32, (1, LANES), 1)
     pair = 2 * LANES
-    span = near * LANES
-
-    def padded(lines):
-        if held >= GROUP:
-            return lines
-        return jnp.concatenate([lines, jnp.zeros((GROUP - held, lines.shape[1]), F32)], axis=0)
-
-    for turn, part in enumerate(parts):
-        for plane in range(far // len(parts)):
-            own = slice(plane * held, (plane + 1) * held)
-            target = pl.multiple_of(((lax.axis_index("far") if len(parts) > 1 else plane) ^ turn) * span, span)
-            for line in range(cores + 1):
-                piece = part[own, line * span : (line + 1) * span]
-                lines_ref[line, :, pl.ds(target, span)] = piece.astype(F32)
+    laid_out(far, held, parts, lines_ref)
     half = held * near * far
     position = lax.axis_index("far") * near + lax.axis_index("near")
     first = lax.axis_index("dp") * half + position * held
@@ -245,19 +265,10 @@
         for lag in range(1, 3):
             signal += taps[lag] * shifted(value, lag)
         signals.append(padded(signal))
-    lags = padded(lines_ref[cores])
 
     for group in range(max(held, GROUP) // GROUP):
         own = slice(group * GROUP, (group + 1) * GROUP)
-        for at in range(GROUP):
-            row = lags[group * GROUP + at : group * GROUP + at + 1, :]
-            repeated = jnp.broadcast_to(row, (BLOCK, row.shape[1]))
-            turned = pltpu.roll(repeated, 0, 1, stride=1, stride_axis=0)
-            column = lax.broadcasted_iota(jnp.int32, repeated.shape, 1)
-            lag = lax.broadcasted_iota(jnp.int32, repeated.shape, 0)
-            kept = jnp.where(column >= lag, turned, 0.0).astype(BF16)
-            table_ref[at * BLOCK : (at + 1) * BLOCK, :] = kept
-
+        table_ref = full_ref.at[group * GROUP * BLOCK : (group + 1) * GROUP * BLOCK]
         stacked = jnp.concatenate(
             [
                 signal[own, a * LANES : (a + 1) * LANES]
@@ -376,6 +387,14 @@
     return lax.ppermute(value, axis, [(i, i ^ step) for i in range(lax.axis_size(axis))])
 
 
+def over_far(values):
+    if len(values) == 4:
+        return all_exchanged(values, "far")
+    order = jnp.arange(len(values)) ^ lax.axis_index("far")
+    moved = lax.all_to_all(jnp.take(jnp.stack(values), order, axis=0), "far", 0, 0, tiled=True)
+    return [moved.reshape(-1, moved.shape[2])]
+
+
 def all_exchanged(values, axis):
     result = list(values)
     for step in reversed(range(1, len(values))):
@@ -461,56 +480,64 @@
     partial = pl.pallas_call(
         functools.partial(project_kernel, near, far, cores, depth),
         in_specs=[VMEM] * (len(chunks) + len(pieces)),
-        out_specs=[VMEM] * (near + 1),
-        out_shape=[near_shape] * near + [jax.ShapeDtypeStruct((far * held, near * rows), F32)],
-        scratch_shapes=[pltpu.VMEM((count * max(held, GROUP), near_shape.shape[1]), F32)],
+        out_specs=[VMEM] * (near + far),
+        out_shape=[near_shape] * near + [jax.ShapeDtypeStruct((held, near * rows), BF16)] * far,
+        scratch_shapes=[
+            pltpu.VMEM((count * max(held, GROUP), near_shape.shape[1]), F32),
+            pltpu.VMEM((far * max(held, GROUP), near * rows), F32),
+        ],
         compiler_params=params(40),
         cost_estimate=cost(4 * cores * near * rows * depth * half, 6 * MIB),
         name="project",
     )(*chunks[::-1], *pieces)
-    *partial, lags = partial
+    partial, lags = list(partial[:near]), partial[near:]
+    lags = over_far(lags)
     last_rows, partial[0] = lax.optimization_barrier((gate_rows[rows - 2 :], partial[0]))
     before = lax.ppermute(last_rows, ("far", "near"), [(i, i + 1) for i in range(count - 1)])
     partial = all_exchanged(partial, "near")
     *partial[::-1], before = lax.optimization_barrier((*partial[::-1], before))
 
-    far_shape = (held, (cores + 1) * near * rows)
+    far_shape = (held, cores * near * rows)
     parts = pl.pallas_call(
         functools.partial(sum_kernel, near, far),
-        in_specs=[VMEM] * (1 + near),
+        in_specs=[VMEM] * near,
         out_specs=[VMEM] * far,
         out_shape=[jax.ShapeDtypeStruct(far_shape, BF16)] * far,
         scratch_shapes=[pltpu.VMEM((far * max(held, GROUP), far_shape[1]), F32)],
         compiler_params=params(16),
         cost_estimate=cost(MIB, MIB),
         name="sum",
-    )(lags, *partial[::-1])
-    if far == 4:
-        parts = all_exchanged(parts, "far")
-    else:
-        order = jnp.arange(far) ^ lax.axis_index("far")
-        parts = lax.all_to_all(jnp.take(jnp.stack(parts), order, axis=0), "far", 0, 0, tiled=True)
-        parts = [parts.reshape(far * held, far_shape[1])]
+    )(*partial[::-1])
+    parts = over_far(parts)
+    held_rows = max(held, GROUP)
+    table = pl.pallas_call(
+        functools.partial(table_kernel, far, held),
+        in_specs=[VMEM] * len(lags),
+        out_specs=VMEM,
+        out_shape=jax.ShapeDtypeStruct((held_rows * BLOCK, length), BF16),
+        scratch_shapes=[pltpu.VMEM((1, held, length), F32)],
+        compiler_params=params(16),
+        cost_estimate=cost(held_rows * BLOCK * length * 4, 3 * MIB),
+        name="table",
+    )(*lags[::-1])
 
     tiles = length // LANES
     all_rows = tiles * SLOTS * cores * GROUP
-    held_rows = max(held, GROUP)
     mixed = pl.pallas_call(
         functools.partial(mix_kernel, near, far, cores, held),
-        in_specs=[VMEM] * (1 + len(parts)),
+        in_specs=[VMEM] * (2 + len(parts)),
         out_specs=VMEM,
         out_shape=jax.ShapeDtypeStruct((cores * tiles, held, LANES), BF16),
         scratch_shapes=[
             pltpu.VMEM((all_rows, GROUP * BLOCK), BF16),
             pltpu.VMEM((all_rows * (1 if tiles <= 16 else 2), LANES), F32),
             pltpu.VMEM((cores * tiles, held_rows, LANES), F32),
-            pltpu.VMEM((GROUP * BLOCK, length), BF16),
-            pltpu.VMEM((cores + 1, held, length), F32),
+            pltpu.VMEM((cores, held, length), F32),
         ],
         compiler_params=params(48),
         cost_estimate=cost(cores * held_rows * BLOCK * length * 256, 2 * MIB),
         name="mix",
-    )(conv_taps, *parts[::-1])
+    )(conv_taps, table, *parts[::-1])
 
     landed = lax.all_to_all(mixed, ("dp", "far", "near"), 0, 0, tiled=True).reshape(channels, rows)
     chunks = 8

time: 65.9 us -> 67.9 us (1.030)
  starting transfers between devices: 21.8 us -> 28.1 us
  waiting for transfers between devices: 18.1 us -> 13.5 us
    ppermute x16 -> x19, starting transfers between devices: 18.4 us -> 24.7 us  [exchanged(): lax.ppermute(value, axis, [(i, i ^ step) for i in range(lax.axis_size(axi...]
    ppermute x16 -> x19, waiting for transfers between devices: 16.8 us -> 13.5 us  [exchanged(): lax.ppermute(value, axis, [(i, i ^ step) for i in range(lax.axis_size(axi...]
    ppermute x1, waiting for transfers between devices: 1.29 us -> 0.01 us  [on_device(): lax.ppermute(last_rows, ('far', 'near'), [(i, i + 1) for i in range(count...]
  transfers between devices with their start and end apart: 17 -> 20, of which waited for: 11 -> 10; matrix products, arithmetic and copies ran while one was open for 5% -> 5% of each run, Pallas kernels for 3% -> 4%
where the time goes in v1:
time: 67.9 us; the launch traced here: 67.7 us
  starting transfers between devices  28.1 us (41%)
  waiting for transfers between devices  13.5 us (20%)
  Pallas kernels  12.2 us (18%)
  blocking collectives  10.5 us (15%)
  matrix products  3.23 us (5%)
    ppermute x19, starting transfers between devices, exchanged(): lax.ppermute(value, axis, [(i, i ^ step) for i in range(lax.axis_size(axi...  24.7 us
    ppermute x19, waiting for transfers between devices, exchanged(): lax.ppermute(value, axis, [(i, i ^ step) for i in range(lax.axis_size(axi...  13.5 us
    all_to_all x1, blocking collectives, on_device(): lax.all_to_all(mixed, ('dp', 'far', 'near'), 0, 0, tiled=True)  10.5 us
    pallas_call x1, Pallas kernels, on_device(): pl.pallas_call(out_kernel, in_specs=[ANY] * 4 + [HBM], out_specs=HBM, out...  4.09 us
    ppermute x1, starting transfers between devices, on_device(): lax.ppermute(last_rows, ('far', 'near'), [(i, i + 1) for i in range(count...  3.38 us
    dot_general x1, matrix products, on_device(): jnp.dot(late_tokens, w_gate, preferred_element_type=F32).astype(BF16)  3.23 us
    pallas_call x1, Pallas kernels, on_device(): pl.pallas_call(functools.partial(project_kernel, near, far, cores, depth)...  2.16 us
    pallas_call x1, Pallas kernels, on_device(): pl.pallas_call(functools.partial(pack_kernel, near, far), in_specs=[HBM]...  2.16 us
  transfers between devices with their start and end apart: 20, of which 10 were waited for; matrix products, arithmetic and copies ran while one was open for 5% of the time, Pallas kernels for 4%

profile of v1, /device:TPU:0, one launch (start us, length us, event | category | flops | bytes accessed | tf_op | source)
XLA Modules:
  0.0 67.7 jit_solution(4810673620219948824)
XLA Ops:
  0.0 1.0 %weights.1 = bf16[256,512]{1,0:T(8,128)(2,1)S(1)} custom-call(bf16[256,512]{1,0:T(8,128)(2,1)} %value_ref.3, bf16[256,512]{1,0:T(8,128)(2,1)} %noise_ref.3), custom_call_target="tpu_custom_call" | custom-call | bytes 524288 | tf_op jit(solution)/shard_map/weights/pallas_call | solution.py:420
  1.0 4.1 %collective-permute-start.3 = (bf16[256,512]{1,0:T(8,128)(2,1)S(1)}, bf16[256,512]{1,0:T(8,128)(2,1)S(1)}, u32[]{:S(2)}, u32[]{:S(2)}) collective-permute-start(bf16[256,512]{1,0:T(8,128)(2,1)S(1)} %weights.1), channel_id=1, source_target_pairs={{0,16},{8,24},{16,0},{24,8},{1,17},{9,25},{17,1},{25,9},{2,18},{10... | collective-permute-start | bytes 786440 | tf_op jit(solution)/shard_map/ppermute | solution.py:387
  5.1 2.2 %pack.1 = (bf16[256,512]{1,0:T(8,128)(2,1)S(1)}, bf16[128,1280]{1,0:T(8,128)(2,1)S(1)}, bf16[128,1280]{1,0:T(8,128)(2,1)S(1)}, bf16[128,1280]{1,0:T(8,128)(2,1)S(1)}, bf16[128,1280]{1,0:T(8,128)(2,1)S(1)}) custom-call(bf16[128,4096]{1,0:T(8,128)(2,1)} %tokens_ref, s32[128,256]{1,0:T(8,128)} %in_ref.1, s32[32,128]{1,0:T(8,128)} %bitcast.5, ...), custom_call_target="tpu_custom_call" | custom-call | flops 67108864 | bytes 3145728 | tf_op jit(solution)/shard_map/pack/pallas_call | solution.py:432
  7.3 1.6 %collective-permute-start.8 = (bf16[256,512]{1,0:T(8,128)(2,1)S(1)}, bf16[256,512]{1,0:T(8,128)(2,1)S(1)}, u32[]{:S(2)}, u32[]{:S(2)}) collective-permute-start(bf16[256,512]{1,0:T(8,128)(2,1)S(1)} %get-tuple-element.51.refs_8_), channel_id=1, source_target_pairs={{0,8},{8,0},{16,24},{24,16},{1,9},{9,1},{17,25},{25,17},{2,10},{10... | collective-permute-start | bytes 786440 | tf_op jit(solution)/shard_map/ppermute | solution.py:387
  8.9 2.4 %collective-permute-start = (bf16[128,1280]{1,0:T(8,128)(2,1)S(1)}, bf16[128,1280]{1,0:T(8,128)(2,1)S(1)}, u32[]{:S(2)}, u32[]{:S(2)}) collective-permute-start(bf16[128,1280]{1,0:T(8,128)(2,1)S(1)} %get-tuple-element.41), channel_id=1, source_target_pairs={{0,6},{2,4},{4,2},{6,0},{1,7},{3,5},{5,3},{7,1},{8,14},{10,12},{12... | collective-permute-start | bytes 983048 | tf_op jit(solution)/shard_map/ppermute | solution.py:387
  12.4 4.7 %collective-permute-done.3.refs_10_ = bf16[256,512]{1,0:T(8,128)(2,1)S(1)} collective-permute-done((bf16[256,512]{1,0:T(8,128)(2,1)S(1)}, bf16[256,512]{1,0:T(8,128)(2,1)S(1)}, u32[]{:S(2)}, u32[]{:S(2)}) %collective-permute-start.3) | collective-permute-done | bytes 262176 | tf_op jit(solution)/shard_map/ppermute | solution.py:387
  17.1 0.7 collective-permute-start.4
  17.8 2.3 %collective-permute-done.8.refs_9_ = bf16[256,512]{1,0:T(8,128)(2,1)S(1)} collective-permute-done((bf16[256,512]{1,0:T(8,128)(2,1)S(1)}, bf16[256,512]{1,0:T(8,128)(2,1)S(1)}, u32[]{:S(2)}, u32[]{:S(2)}) %collective-permute-start.8) | collective-permute-done | bytes 262176 | tf_op jit(solution)/shard_map/ppermute | solution.py:387
  20.1 3.2 %convolution_convert_fusion.gate_ref = bf16[128,512]{1,0:T(8,128)(2,1)S(1)} fusion(bf16[128,4096]{1,0:T(8,128)(2,1)} %tokens_ref, bf16[4096,512]{1,0:T(8,128)(2,1)} %param.14), kind=kOutput, calls=%fused_computation | convolution fusion | flops 536936448 | bytes 5373952 | tf_op jit(solution)/shard_map/dot_general | solution.py:474
  23.4 2.4 %collective-permute-done.1.refs_5_ = bf16[128,1280]{1,0:T(8,128)(2,1)S(1)} collective-permute-done((bf16[128,1280]{1,0:T(8,128)(2,1)S(1)}, bf16[128,1280]{1,0:T(8,128)(2,1)S(1)}, u32[]{:S(2)}, u32[]{:S(2)}) %collective-permute-start.1) | collective-permute-done | bytes 327712 | tf_op jit(solution)/shard_map/ppermute | solution.py:387
  26.3 1.1 %collective-permute-done.6.refs_1_ = bf16[128,1280]{1,0:T(8,128)(2,1)S(1)} collective-permute-done((bf16[128,1280]{1,0:T(8,128)(2,1)S(1)}, bf16[128,1280]{1,0:T(8,128)(2,1)S(1)}, u32[]{:S(2)}, u32[]{:S(2)}) %collective-permute-start.6) | collective-permute-done | bytes 327712 | tf_op jit(solution)/shard_map/ppermute | solution.py:387
  28.4 2.2 %project.1 = (bf16[64,1024]{1,0:T(8,128)(2,1)S(1)}, bf16[64,1024]{1,0:T(8,128)(2,1)S(1)}, bf16[64,1024]{1,0:T(8,128)(2,1)S(1)}, bf16[64,1024]{1,0:T(8,128)(2,1)S...) custom-call(bf16[128,1280]{1,0:T(8,128)(2,1)S(1)} %collective-permut, ...), custom_call_target="tpu_custom_call" | custom-call | flops 1073741824 | bytes 6291456 | tf_op jit(solution)/shard_map/project/pallas_call | solution.py:480
  30.6 1.7 %collective-permute-start.10 = (bf16[64,1024]{1,0:T(8,128)(2,1)S(1)}, bf16[64,1024]{1,0:T(8,128)(2,1)S(1)}, u32[]{:S(2)}, u32[]{:S(2)}) collective-permute-start(bf16[64,1024]{1,0:T(8,128)(2,1)S(1)} %get-tuple-element.56), channel_id=1, source_target_pairs={{0,6},{2,4},{4,2},{6,0},{1,7},{3,5},{5,3},{7,1},{8,14},{10,12},{12... | collective-permute-start | bytes 393224 | tf_op jit(solution)/shard_map/ppermute | solution.py:387
  32.3 1.3 %collective-permute-start.11 = (bf16[64,1024]{1,0:T(8,128)(2,1)S(1)}, bf16[64,1024]{1,0:T(8,128)(2,1)S(1)}, u32[]{:S(2)}, u32[]{:S(2)}) collective-permute-start(bf16[64,1024]{1,0:T(8,128)(2,1)S(1)} %get-tuple-element.57), channel_id=1, source_target_pairs={{0,4},{2,6},{4,0},{6,2},{1,5},{3,7},{5,1},{7,3},{8,12},{10,14},{12... | collective-permute-start | bytes 393224 | tf_op jit(solution)/shard_map/ppermute | solution.py:387
  34.1 3.4 %collective-permute-start.13 = (bf16[2,512]{1,0:T(2,128)(2,1)S(1)}, bf16[2,512]{1,0:T(2,128)(2,1)S(1)}, u32[]{:S(2)}, u32[]{:S(2)}) collective-permute-start(bf16[2,512]{1,0:T(2,128)(2,1)S(1)} %slice.3), channel_id=1, source_target_pairs={{0,2},{2,4},{4,6},{6,8},{8,10},{10,12},{12,14},{14,16},{16,18},{18... | collective-permute-start | bytes 6152 | tf_op jit(solution)/shard_map/ppermute | solution.py:496
  37.5 2.1 %collective-permute-start.14 = (bf16[16,512]{1,0:T(8,128)(2,1)S(1)}, bf16[16,512]{1,0:T(8,128)(2,1)S(1)}, u32[]{:S(2)}, u32[]{:S(2)}) collective-permute-start(bf16[16,512]{1,0:T(8,128)(2,1)S(1)} %get-tuple-element.63), channel_id=1, source_target_pairs={{0,24},{8,16},{16,8},{24,0},{1,25},{9,17},{17,9},{25,1},{2,26},{10... | collective-permute-start | bytes 49160 | tf_op jit(solution)/shard_map/ppermute | solution.py:387
  40.0 3.7 %collective-permute-start.17 = (bf16[16,1024]{1,0:T(8,128)(2,1)S(1)}, bf16[16,1024]{1,0:T(8,128)(2,1)S(1)}, u32[]{:S(2)}, u32[]{:S(2)}) collective-permute-start(bf16[16,1024]{1,0:T(8,128)(2,1)S(1)} %get-tuple-element.71), channel_id=1, source_target_pairs={{0,24},{8,16},{16,8},{24,0},{1,25},{9,17},{17,9},{25,1},{2,26},{10... | collective-permute-start | bytes 98312 | tf_op jit(solution)/shard_map/ppermute | solution.py:387
  43.7 0.8 %collective-permute-start.19 = (bf16[16,1024]{1,0:T(8,128)(2,1)S(1)}, bf16[16,1024]{1,0:T(8,128)(2,1)S(1)}, u32[]{:S(2)}, u32[]{:S(2)}) collective-permute-start(bf16[16,1024]{1,0:T(8,128)(2,1)S(1)} %get-tuple-element.73), channel_id=1, source_target_pairs={{0,8},{8,0},{16,24},{24,16},{1,9},{9,1},{17,25},{25,17},{2,10},{10... | collective-permute-start | bytes 98312 | tf_op jit(solution)/shard_map/ppermute | solution.py:387
  44.4 2.1 %collective-permute-start.15 = (bf16[16,512]{1,0:T(8,128)(2,1)S(1)}, bf16[16,512]{1,0:T(8,128)(2,1)S(1)}, u32[]{:S(2)}, u32[]{:S(2)}) collective-permute-start(bf16[16,512]{1,0:T(8,128)(2,1)S(1)} %get-tuple-element.64), channel_id=1, source_target_pairs={{0,16},{8,24},{16,0},{24,8},{1,17},{9,25},{17,1},{25,9},{2,18},{10... | collective-permute-start | bytes 49160 | tf_op jit(solution)/shard_map/ppermute | solution.py:387
  46.6 2.0 %collective-permute-start.16 = (bf16[16,512]{1,0:T(8,128)(2,1)S(1)}, bf16[16,512]{1,0:T(8,128)(2,1)S(1)}, u32[]{:S(2)}, u32[]{:S(2)}) collective-permute-start(bf16[16,512]{1,0:T(8,128)(2,1)S(1)} %get-tuple-element.65), channel_id=1, source_target_pairs={{0,8},{8,0},{16,24},{24,16},{1,9},{9,1},{17,25},{25,17},{2,10},{10... | collective-permute-start | bytes 49160 | tf_op jit(solution)/shard_map/ppermute | solution.py:387
  49.1 1.3 %collective-permute-done.16.refs_2_ = bf16[16,512]{1,0:T(8,128)(2,1)S(1)} collective-permute-done((bf16[16,512]{1,0:T(8,128)(2,1)S(1)}, bf16[16,512]{1,0:T(8,128)(2,1)S(1)}, u32[]{:S(2)}, u32[]{:S(2)}) %collective-permute-start.16) | collective-permute-done | bytes 16416 | tf_op jit(solution)/shard_map/ppermute | solution.py:387
  51.0 2.1 %mix.1 = bf16[32,16,128]{2,1,0:T(8,128)(2,1)S(1)} custom-call(f32[3,1024]{1,0:T(4,128)S(1)} %copy-done, bf16[512,2048]{1,0:T(8,128)(2,1)S(1)} %table.1.full_ref, bf16[16,1024]{1,0:T(8,128)(2,1)S(1)} %collective-permute-done.17.refs_0_, bf16[16,1024]{1,0:T(8,128)(2,1)S(1)} %collective-permute-done.18.refs_1_, ...), custom_call_target="tpu_custom_call" | custom-call | flops 536870912 | bytes 2097152 | tf_op jit(solution)/shard_map/mix/pallas_call | solution.py:526
  53.1 10.5 %all_to_all.5 = bf16[32,16,128]{2,1,0:T(8,128)(2,1)S(1)} all-to-all(bf16[32,16,128]{2,1,0:T(8,128)(2,1)S(1)} %mix.1), channel_id=1, replica_groups=mesh['far'=4,'near'=4,'dp'=2] {'dp','far','near'}, dimensions={0} | all-to-all | bytes 262144 | tf_op jit(solution)/shard_map/all_to_all | solution.py:542
  63.6 4.1 %project_out.1 = bf16[128,4096]{1,0:T(8,128)(2,1)} custom-call(bf16[128,512]{1,0:T(8,128)(2,1)S(1)} %convolution_convert_fusion.gate_ref, bf16[2,512]{1,0:T(2,128)(2,1)S(1)} %collective-permute-done.13.before_ref, f32[3,1024]{1,0:T(4,128)S(1)} %copy-done, bf16[512,128]{1,0:T(8,128)(2,1)S(1)} %bitcast.4, bf16[512,4096]{1,0:T(8,128)(2,1)} %source_ref.1), custom_call_target="tpu_custom_call" | custom-call | flops 536870912 | bytes 5242880 | tf_op jit(solution)/shard_map/project_out/pallas_call | solution.py:544
  (28 shorter events, 4.6 us)
Async XLA Ops:
  1.0 16.1 %collective-permute-start.3 = (bf16[256,512]{1,0:T(8,128)(2,1)S(1)}, bf16[256,512]{1,0:T(8,128)(2,1)S(1)}, u32[]{:S(2)}, u32[]{:S(2)}) collective-permute-start(bf16[256,512]{1,0:T(8,128)(2,1)S(1)} %weights.1), channel_id=1, source_target_pairs={{0,16},{8,24},{16,0},{24,8},{1,17},{9,25},{17,1},{25,9},{2,18},{10... | collective-permute-start | bytes 786440 | tf_op jit(solution)/shard_map/ppermute | solution.py:387
  7.3 12.8 %collective-permute-start.8 = (bf16[256,512]{1,0:T(8,128)(2,1)S(1)}, bf16[256,512]{1,0:T(8,128)(2,1)S(1)}, u32[]{:S(2)}, u32[]{:S(2)}) collective-permute-start(bf16[256,512]{1,0:T(8,128)(2,1)S(1)} %get-tuple-element.51.refs_8_), channel_id=1, source_target_pairs={{0,8},{8,0},{16,24},{24,16},{1,9},{9,1},{17,25},{25,17},{2,10},{10... | collective-permute-start | bytes 786440 | tf_op jit(solution)/shard_map/ppermute | solution.py:387
  8.9 14.4 %collective-permute-start = (bf16[128,1280]{1,0:T(8,128)(2,1)S(1)}, bf16[128,1280]{1,0:T(8,128)(2,1)S(1)}, u32[]{:S(2)}, u32[]{:S(2)}) collective-permute-start(bf16[128,1280]{1,0:T(8,128)(2,1)S(1)} %get-tuple-element.41), channel_id=1, source_target_pairs={{0,6},{2,4},{4,2},{6,0},{1,7},{3,5},{5,3},{7,1},{8,14},{10,12},{12... | collective-permute-start | bytes 983048 | tf_op jit(solution)/shard_map/ppermute | solution.py:387
  11.4 14.4 %collective-permute-start.1 = (bf16[128,1280]{1,0:T(8,128)(2,1)S(1)}, bf16[128,1280]{1,0:T(8,128)(2,1)S(1)}, u32[]{:S(2)}, u32[]{:S(2)}) collective-permute-start(bf16[128,1280]{1,0:T(8,128)(2,1)S(1)} %get-tuple-element.42), channel_id=1, source_target_pairs={{0,4},{2,6},{4,0},{6,2},{1,5},{3,7},{5,1},{7,3},{8,12},{10,14},{12... | collective-permute-start | bytes 983048 | tf_op jit(solution)/shard_map/ppermute | solution.py:387
  11.9 14.0 %collective-permute-start.2 = (bf16[128,1280]{1,0:T(8,128)(2,1)S(1)}, bf16[128,1280]{1,0:T(8,128)(2,1)S(1)}, u32[]{:S(2)}, u32[]{:S(2)}) collective-permute-start(bf16[128,1280]{1,0:T(8,128)(2,1)S(1)} %get-tuple-element.43), channel_id=1, source_target_pairs={{0,2},{2,0},{4,6},{6,4},{1,3},{3,1},{5,7},{7,5},{8,10},{10,8},{12,... | collective-permute-start | bytes 983048 | tf_op jit(solution)/shard_map/ppermute | solution.py:387
  17.1 9.2 %collective-permute-start.4 = (bf16[256,512]{1,0:T(8,128)(2,1)S(1)}, bf16[256,512]{1,0:T(8,128)(2,1)S(1)}, u32[]{:S(2)}, u32[]{:S(2)}) collective-permute-start(bf16[256,512]{1,0:T(8,128)(2,1)S(1)} %collective-permute-done.3.refs_10_), channel_id=1, source_target_pairs={{0,8},{8,0},{16,24},{24,16},{1,9},{9,1},{17,25},{25,17},{2,10},{10... | collective-permute-start | bytes 786440 | tf_op jit(solution)/shard_map/ppermute | solution.py:387
  20.1 6.2 %collective-permute-start.9 = (bf16[128,1280]{1,0:T(8,128)(2,1)S(1)}, bf16[128,1280]{1,0:T(8,128)(2,1)S(1)}, u32[]{:S(2)}, u32[]{:S(2)}) collective-permute-start(bf16[128,1280]{1,0:T(8,128)(2,1)S(1)} %get-tuple-element.53.refs_7_), channel_id=1, source_target_pairs={{0,1},{1,0},{2,3},{3,2},{4,5},{5,4},{6,7},{7,6},{8,9},{9,8},{10,11... | collective-permute-start | bytes 983048 | tf_op jit(solution)/shard_map/ppermute | solution.py:387
  23.3 27.6 %copy-start = (f32[3,1024]{1,0:T(4,128)S(1)}, f32[3,1024]{1,0:T(4,128)}, u32[]{:S(2)}) copy-start(f32[3,1024]{1,0:T(4,128)} %taps_ref.3) | copy-start | bytes 36868
  25.8 1.6 %collective-permute-start.6 = (bf16[128,1280]{1,0:T(8,128)(2,1)S(1)}, bf16[128,1280]{1,0:T(8,128)(2,1)S(1)}, u32[]{:S(2)}, u32[]{:S(2)}) collective-permute-start(bf16[128,1280]{1,0:T(8,128)(2,1)S(1)} %collective-permute-done.1.refs_5_), channel_id=1, source_target_pairs={{0,1},{1,0},{2,3},{3,2},{4,5},{5,4},{6,7},{7,6},{8,9},{9,8},{10,11... | collective-permute-start | bytes 983048 | tf_op jit(solution)/shard_map/ppermute | solution.py:387
  25.8 2.1 %collective-permute-start.7 = (bf16[128,1280]{1,0:T(8,128)(2,1)S(1)}, bf16[128,1280]{1,0:T(8,128)(2,1)S(1)}, u32[]{:S(2)}, u32[]{:S(2)}) collective-permute-start(bf16[128,1280]{1,0:T(8,128)(2,1)S(1)} %collective-permute-done.2.refs_6_), channel_id=1, source_target_pairs={{0,1},{1,0},{2,3},{3,2},{4,5},{5,4},{6,7},{7,6},{8,9},{9,8},{10,11... | collective-permute-start | bytes 983048 | tf_op jit(solution)/shard_map/ppermute | solution.py:387
  26.3 2.1 %collective-permute-start.5 = (bf16[128,1280]{1,0:T(8,128)(2,1)S(1)}, bf16[128,1280]{1,0:T(8,128)(2,1)S(1)}, u32[]{:S(2)}, u32[]{:S(2)}) collective-permute-start(bf16[128,1280]{1,0:T(8,128)(2,1)S(1)} %collective-permute-done.refs_4_), channel_id=1, source_target_pairs={{0,1},{1,0},{2,3},{3,2},{4,5},{5,4},{6,7},{7,6},{8,9},{9,8},{10,11... | collective-permute-start | bytes 983048 | tf_op jit(solution)/shard_map/ppermute | solution.py:387
  30.6 9.1 %collective-permute-start.10 = (bf16[64,1024]{1,0:T(8,128)(2,1)S(1)}, bf16[64,1024]{1,0:T(8,128)(2,1)S(1)}, u32[]{:S(2)}, u32[]{:S(2)}) collective-permute-start(bf16[64,1024]{1,0:T(8,128)(2,1)S(1)} %get-tuple-element.56), channel_id=1, source_target_pairs={{0,6},{2,4},{4,2},{6,0},{1,7},{3,5},{5,3},{7,1},{8,14},{10,12},{12... | collective-permute-start | bytes 393224 | tf_op jit(solution)/shard_map/ppermute | solution.py:387
  32.3 7.6 %collective-permute-start.11 = (bf16[64,1024]{1,0:T(8,128)(2,1)S(1)}, bf16[64,1024]{1,0:T(8,128)(2,1)S(1)}, u32[]{:S(2)}, u32[]{:S(2)}) collective-permute-start(bf16[64,1024]{1,0:T(8,128)(2,1)S(1)} %get-tuple-element.57), channel_id=1, source_target_pairs={{0,4},{2,6},{4,0},{6,2},{1,5},{3,7},{5,1},{7,3},{8,12},{10,14},{12... | collective-permute-start | bytes 393224 | tf_op jit(solution)/shard_map/ppermute | solution.py:387
  33.6 6.3 %collective-permute-start.12 = (bf16[64,1024]{1,0:T(8,128)(2,1)S(1)}, bf16[64,1024]{1,0:T(8,128)(2,1)S(1)}, u32[]{:S(2)}, u32[]{:S(2)}) collective-permute-start(bf16[64,1024]{1,0:T(8,128)(2,1)S(1)} %get-tuple-element.58), channel_id=1, source_target_pairs={{0,2},{2,0},{4,6},{6,4},{1,3},{3,1},{5,7},{7,5},{8,10},{10,8},{12,... | collective-permute-start | bytes 393224 | tf_op jit(solution)/shard_map/ppermute | solution.py:387
  34.1 5.5 %collective-permute-start.13 = (bf16[2,512]{1,0:T(2,128)(2,1)S(1)}, bf16[2,512]{1,0:T(2,128)(2,1)S(1)}, u32[]{:S(2)}, u32[]{:S(2)}) collective-permute-start(bf16[2,512]{1,0:T(2,128)(2,1)S(1)} %slice.3), channel_id=1, source_target_pairs={{0,2},{2,4},{4,6},{6,8},{8,10},{10,12},{12,14},{14,16},{16,18},{18... | collective-permute-start | bytes 6152 | tf_op jit(solution)/shard_map/ppermute | solution.py:496
  37.5 9.1 %collective-permute-start.14 = (bf16[16,512]{1,0:T(8,128)(2,1)S(1)}, bf16[16,512]{1,0:T(8,128)(2,1)S(1)}, u32[]{:S(2)}, u32[]{:S(2)}) collective-permute-start(bf16[16,512]{1,0:T(8,128)(2,1)S(1)} %get-tuple-element.63), channel_id=1, source_target_pairs={{0,24},{8,16},{16,8},{24,0},{1,25},{9,17},{17,9},{25,1},{2,26},{10... | collective-permute-start | bytes 49160 | tf_op jit(solution)/shard_map/ppermute | solution.py:387
  40.0 11.0 %collective-permute-start.17 = (bf16[16,1024]{1,0:T(8,128)(2,1)S(1)}, bf16[16,1024]{1,0:T(8,128)(2,1)S(1)}, u32[]{:S(2)}, u32[]{:S(2)}) collective-permute-start(bf16[16,1024]{1,0:T(8,128)(2,1)S(1)} %get-tuple-element.71), channel_id=1, source_target_pairs={{0,24},{8,16},{16,8},{24,0},{1,25},{9,17},{17,9},{25,1},{2,26},{10... | collective-permute-start | bytes 98312 | tf_op jit(solution)/shard_map/ppermute | solution.py:387
  43.6 7.3 %collective-permute-start.18 = (bf16[16,1024]{1,0:T(8,128)(2,1)S(1)}, bf16[16,1024]{1,0:T(8,128)(2,1)S(1)}, u32[]{:S(2)}, u32[]{:S(2)}) collective-permute-start(bf16[16,1024]{1,0:T(8,128)(2,1)S(1)} %get-tuple-element.72), channel_id=1, source_target_pairs={{0,16},{8,24},{16,0},{24,8},{1,17},{9,25},{17,1},{25,9},{2,18},{10... | collective-permute-start | bytes 98312 | tf_op jit(solution)/shard_map/ppermute | solution.py:387
  43.7 7.3 %collective-permute-start.19 = (bf16[16,1024]{1,0:T(8,128)(2,1)S(1)}, bf16[16,1024]{1,0:T(8,128)(2,1)S(1)}, u32[]{:S(2)}, u32[]{:S(2)}) collective-permute-start(bf16[16,1024]{1,0:T(8,128)(2,1)S(1)} %get-tuple-element.73), channel_id=1, source_target_pairs={{0,8},{8,0},{16,24},{24,16},{1,9},{9,1},{17,25},{25,17},{2,10},{10... | collective-permute-start | bytes 98312 | tf_op jit(solution)/shard_map/ppermute | solution.py:387
  44.4 4.6 %collective-permute-start.15 = (bf16[16,512]{1,0:T(8,128)(2,1)S(1)}, bf16[16,512]{1,0:T(8,128)(2,1)S(1)}, u32[]{:S(2)}, u32[]{:S(2)}) collective-permute-start(bf16[16,512]{1,0:T(8,128)(2,1)S(1)} %get-tuple-element.64), channel_id=1, source_target_pairs={{0,16},{8,24},{16,0},{24,8},{1,17},{9,25},{17,1},{25,9},{2,18},{10... | collective-permute-start | bytes 49160 | tf_op jit(solution)/shard_map/ppermute | solution.py:387
  46.6 3.7 %collective-permute-start.16 = (bf16[16,512]{1,0:T(8,128)(2,1)S(1)}, bf16[16,512]{1,0:T(8,128)(2,1)S(1)}, u32[]{:S(2)}, u32[]{:S(2)}) collective-permute-start(bf16[16,512]{1,0:T(8,128)(2,1)S(1)} %get-tuple-element.65), channel_id=1, source_target_pairs={{0,8},{8,0},{16,24},{24,16},{1,9},{9,1},{17,25},{25,17},{2,10},{10... | collective-permute-start | bytes 49160 | tf_op jit(solution)/shard_map/ppermute | solution.py:387

commit v2 on v0

--- a/solution.py
+++ b/solution.py
@@ -330,8 +330,8 @@
 
 
 def out_kernel(
-    gate_ref, before_ref, taps_ref, mixed_ref, source_ref, target_ref,
-    gate_held, before_held, taps_held, mixed_held, weight_ref, held_ref, small_sems, read_sems, write_sems,
+    gate_ref, even_ref, odd_ref, taps_ref, mixed_ref, source_ref, target_ref,
+    gate_held, even_held, odd_held, taps_held, mixed_held, weight_ref, held_ref, small_sems, read_sems, write_sems,
 ):
     chunks, channels, step = weight_ref.shape
     small = [
@@ -339,7 +339,8 @@
         for at, (source, target) in enumerate(
             (
                 (gate_ref, gate_held),
-                (before_ref, before_held),
+                (even_ref, even_held),
+                (odd_ref, odd_held),
                 (taps_ref, taps_held),
                 (mixed_ref, mixed_held),
             )
@@ -356,7 +357,10 @@
     for copy in small:
         copy.wait()
     gate = gate_held[...].astype(F32)
-    extended = jnp.concatenate([before_held[...].astype(F32), gate], axis=0)
+    position = lax.axis_index("far") * lax.axis_size("near") + lax.axis_index("near")
+    odd = jnp.full((1, 1), position & 1, jnp.int32) != 0
+    before = jnp.where(odd, odd_held[...].astype(F32), even_held[...].astype(F32))
+    extended = jnp.concatenate([before, gate], axis=0)
     gate_short = taps_held[0:1, channels:] * gate
     for lag in range(1, 3):
         gate_short += taps_held[lag : lag + 1, channels:] * extended[2 - lag : 2 - lag + gate.shape[0]]
@@ -470,7 +474,13 @@
     )(*chunks[::-1], *pieces)
     *partial, lags = partial
     last_rows, partial[0] = lax.optimization_barrier((gate_rows[rows - 2 :], partial[0]))
-    before = lax.ppermute(last_rows, ("far", "near"), [(i, i + 1) for i in range(count - 1)])
+    pairs = [(i, i + 1) for i in range(count - 1)]
+    before = [
+        lax.ppermute(
+            last_rows, ("far", "near"), [pair for i, j in pairs[first::2] for pair in ((i, j), (j, i))]
+        )
+        for first in (1, 0)
+    ]
     partial = all_exchanged(partial, "near")
     *partial[::-1], before = lax.optimization_barrier((*partial[::-1], before))
 
@@ -516,24 +526,25 @@
     chunks = 8
     return pl.pallas_call(
         out_kernel,
-        in_specs=[ANY] * 4 + [HBM],
+        in_specs=[ANY] * 5 + [HBM],
         out_specs=HBM,
         out_shape=jax.ShapeDtypeStruct((rows, width), BF16),
         scratch_shapes=[
             pltpu.VMEM(gate_rows.shape, BF16),
-            pltpu.VMEM(before.shape, BF16),
+            pltpu.VMEM(before[0].shape, BF16),
+            pltpu.VMEM(before[1].shape, BF16),
             pltpu.VMEM(conv_taps.shape, F32),
             pltpu.VMEM(landed.shape, BF16),
             pltpu.VMEM((chunks, channels, width // chunks), BF16),
             pltpu.VMEM((chunks, rows, width // chunks), BF16),
-            pltpu.SemaphoreType.DMA((4,)),
+            pltpu.SemaphoreType.DMA((5,)),
             pltpu.SemaphoreType.DMA((chunks,)),
             pltpu.SemaphoreType.DMA((chunks,)),
         ],
         compiler_params=params(16),
         cost_estimate=cost(2 * rows * width * channels, 5 * MIB),
         name="project_out",
-    )(gate_rows, before, conv_taps, landed, *in_hbm(w_out))
+    )(gate_rows, *before, conv_taps, landed, *in_hbm(w_out))
 
 
 def solution(mesh):

time: 65.9 us -> 66.8 us (1.014)
  starting transfers between devices: 21.8 us -> 23.3 us
  waiting for transfers between devices: 18.1 us -> 17.1 us
    ppermute x1 -> x2, starting transfers between devices: 3.38 us -> 4.85 us  [on_device(): lax.ppermute(last_rows, ('far', 'near'), [pair for i, j in pairs[first::2...]
    ppermute x16, waiting for transfers between devices: 16.8 us -> 15.5 us  [exchanged(): lax.ppermute(value, axis, [(i, i ^ step) for i in range(lax.axis_size(axi...]
    ppermute x1 -> x2, waiting for transfers between devices: 1.29 us -> 1.56 us  [on_device(): lax.ppermute(last_rows, ('far', 'near'), [pair for i, j in pairs[first::2...]
  transfers between devices with their start and end apart: 17 -> 18, of which waited for: 11 -> 10; matrix products, arithmetic and copies ran while one was open for 5% -> 5% of each run, Pallas kernels for 3% -> 3%
where the time goes in v2:
time: 66.8 us; the launch traced here: 66.6 us
  starting transfers between devices  23.3 us (35%)
  waiting for transfers between devices  17.1 us (26%)
  Pallas kernels  12 us (18%)
  blocking collectives  10.9 us (16%)
  matrix products  3.24 us (5%)
    ppermute x16, starting transfers between devices, exchanged(): lax.ppermute(value, axis, [(i, i ^ step) for i in range(lax.axis_size(axi...  18.4 us
    ppermute x16, waiting for transfers between devices, exchanged(): lax.ppermute(value, axis, [(i, i ^ step) for i in range(lax.axis_size(axi...  15.5 us
    all_to_all x1, blocking collectives, on_device(): lax.all_to_all(mixed, ('dp', 'far', 'near'), 0, 0, tiled=True)  10.9 us
    ppermute x2, starting transfers between devices, on_device(): lax.ppermute(last_rows, ('far', 'near'), [pair for i, j in pairs[first::2...  4.85 us
    pallas_call x1, Pallas kernels, on_device(): pl.pallas_call(out_kernel, in_specs=[ANY] * 5 + [HBM], out_specs=HBM, out...  4.09 us
    dot_general x1, matrix products, on_device(): jnp.dot(late_tokens, w_gate, preferred_element_type=F32).astype(BF16)  3.24 us
    pallas_call x1, Pallas kernels, on_device(): pl.pallas_call(functools.partial(mix_kernel, near, far, cores, held), in_...  2.52 us
    pallas_call x1, Pallas kernels, on_device(): pl.pallas_call(functools.partial(pack_kernel, near, far), in_specs=[HBM]...  2.16 us
  transfers between devices with their start and end apart: 18, of which 10 were waited for; matrix products, arithmetic and copies ran while one was open for 5% of the time, Pallas kernels for 3%

profile of v2, /device:TPU:0, one launch (start us, length us, event | category | flops | bytes accessed | tf_op | source)
XLA Modules:
  0.0 66.6 jit_solution(10659045189440062817)
XLA Ops:
  0.0 1.0 %weights.1 = bf16[256,512]{1,0:T(8,128)(2,1)S(1)} custom-call(bf16[256,512]{1,0:T(8,128)(2,1)} %value_ref.3, bf16[256,512]{1,0:T(8,128)(2,1)} %noise_ref.3), custom_call_target="tpu_custom_call" | custom-call | bytes 524288 | tf_op jit(solution)/shard_map/weights/pallas_call | solution.py:405
  1.0 4.1 %collective-permute-start.3 = (bf16[256,512]{1,0:T(8,128)(2,1)S(1)}, bf16[256,512]{1,0:T(8,128)(2,1)S(1)}, u32[]{:S(2)}, u32[]{:S(2)}) collective-permute-start(bf16[256,512]{1,0:T(8,128)(2,1)S(1)} %weights.1), channel_id=1, source_target_pairs={{0,16},{8,24},{16,0},{24,8},{1,17},{9,25},{17,1},{25,9},{2,18},{10... | collective-permute-start | bytes 786440 | tf_op jit(solution)/shard_map/ppermute | solution.py:380
  5.1 2.2 %pack.1 = (bf16[256,512]{1,0:T(8,128)(2,1)S(1)}, bf16[128,1280]{1,0:T(8,128)(2,1)S(1)}, bf16[128,1280]{1,0:T(8,128)(2,1)S(1)}, bf16[128,1280]{1,0:T(8,128)(2,1)S(1)}, bf16[128,1280]{1,0:T(8,128)(2,1)S(1)}) custom-call(bf16[128,4096]{1,0:T(8,128)(2,1)} %tokens_ref, s32[128,256]{1,0:T(8,128)} %in_ref.1, s32[32,128]{1,0:T(8,128)} %bitcast.5, ...), custom_call_target="tpu_custom_call" | custom-call | flops 67108864 | bytes 3145728 | tf_op jit(solution)/shard_map/pack/pallas_call | solution.py:417
  7.3 1.6 %collective-permute-start.8 = (bf16[256,512]{1,0:T(8,128)(2,1)S(1)}, bf16[256,512]{1,0:T(8,128)(2,1)S(1)}, u32[]{:S(2)}, u32[]{:S(2)}) collective-permute-start(bf16[256,512]{1,0:T(8,128)(2,1)S(1)} %get-tuple-element.49.refs_8_), channel_id=1, source_target_pairs={{0,8},{8,0},{16,24},{24,16},{1,9},{9,1},{17,25},{25,17},{2,10},{10... | collective-permute-start | bytes 786440 | tf_op jit(solution)/shard_map/ppermute | solution.py:380
  8.9 2.4 %collective-permute-start = (bf16[128,1280]{1,0:T(8,128)(2,1)S(1)}, bf16[128,1280]{1,0:T(8,128)(2,1)S(1)}, u32[]{:S(2)}, u32[]{:S(2)}) collective-permute-start(bf16[128,1280]{1,0:T(8,128)(2,1)S(1)} %get-tuple-element.39), channel_id=1, source_target_pairs={{0,6},{2,4},{4,2},{6,0},{1,7},{3,5},{5,3},{7,1},{8,14},{10,12},{12... | collective-permute-start | bytes 983048 | tf_op jit(solution)/shard_map/ppermute | solution.py:380
  12.4 4.7 %collective-permute-done.3.refs_10_ = bf16[256,512]{1,0:T(8,128)(2,1)S(1)} collective-permute-done((bf16[256,512]{1,0:T(8,128)(2,1)S(1)}, bf16[256,512]{1,0:T(8,128)(2,1)S(1)}, u32[]{:S(2)}, u32[]{:S(2)}) %collective-permute-start.3) | collective-permute-done | bytes 262176 | tf_op jit(solution)/shard_map/ppermute | solution.py:380
  17.1 0.7 collective-permute-start.4
  17.8 2.3 %collective-permute-done.8.refs_9_ = bf16[256,512]{1,0:T(8,128)(2,1)S(1)} collective-permute-done((bf16[256,512]{1,0:T(8,128)(2,1)S(1)}, bf16[256,512]{1,0:T(8,128)(2,1)S(1)}, u32[]{:S(2)}, u32[]{:S(2)}) %collective-permute-start.8) | collective-permute-done | bytes 262176 | tf_op jit(solution)/shard_map/ppermute | solution.py:380
  20.1 3.2 %convolution_convert_fusion.gate_ref = bf16[128,512]{1,0:T(8,128)(2,1)S(1)} fusion(bf16[128,4096]{1,0:T(8,128)(2,1)} %tokens_ref, bf16[4096,512]{1,0:T(8,128)(2,1)} %param.14), kind=kOutput, calls=%fused_computation | convolution fusion | flops 536936448 | bytes 5373952 | tf_op jit(solution)/shard_map/dot_general | solution.py:459
  23.4 2.3 %collective-permute-done.1.refs_5_ = bf16[128,1280]{1,0:T(8,128)(2,1)S(1)} collective-permute-done((bf16[128,1280]{1,0:T(8,128)(2,1)S(1)}, bf16[128,1280]{1,0:T(8,128)(2,1)S(1)}, u32[]{:S(2)}, u32[]{:S(2)}) %collective-permute-start.1) | collective-permute-done | bytes 327712 | tf_op jit(solution)/shard_map/ppermute | solution.py:380
  26.3 1.1 %collective-permute-done.6.refs_1_ = bf16[128,1280]{1,0:T(8,128)(2,1)S(1)} collective-permute-done((bf16[128,1280]{1,0:T(8,128)(2,1)S(1)}, bf16[128,1280]{1,0:T(8,128)(2,1)S(1)}, u32[]{:S(2)}, u32[]{:S(2)}) %collective-permute-start.6) | collective-permute-done | bytes 327712 | tf_op jit(solution)/shard_map/ppermute | solution.py:380
  28.4 2.2 %project.1 = (bf16[64,1024]{1,0:T(8,128)(2,1)S(1)}, bf16[64,1024]{1,0:T(8,128)(2,1)S(1)}, bf16[64,1024]{1,0:T(8,128)(2,1)S(1)}, bf16[64,1024]{1,0:T(8,128)(2,1)S(1)}, f32[64,512]{1,0:T(8,128)S(1)}) custom-call(bf16[128,1280]{1,0:T(8,128)(2,1)S(1)} %collective-permute-done.5.refs_0_, bf16[128,1280]{1,0:T(8,128)(2,1)S(1)} %collective-permute-done.6.refs_1_, ...), custom_call_target="tpu_custom_call" | custom-call | flops 1073741824 | bytes 6291456 | tf_op jit(solution)/shard_map/project/pallas_call | solution.py:465
  30.5 1.7 %collective-permute-start.10 = (bf16[64,1024]{1,0:T(8,128)(2,1)S(1)}, bf16[64,1024]{1,0:T(8,128)(2,1)S(1)}, u32[]{:S(2)}, u32[]{:S(2)}) collective-permute-start(bf16[64,1024]{1,0:T(8,128)(2,1)S(1)} %get-tuple-element.54), channel_id=1, source_target_pairs={{0,6},{2,4},{4,2},{6,0},{1,7},{3,5},{5,3},{7,1},{8,14},{10,12},{12... | collective-permute-start | bytes 393224 | tf_op jit(solution)/shard_map/ppermute | solution.py:380
  32.3 1.3 %collective-permute-start.11 = (bf16[64,1024]{1,0:T(8,128)(2,1)S(1)}, bf16[64,1024]{1,0:T(8,128)(2,1)S(1)}, u32[]{:S(2)}, u32[]{:S(2)}) collective-permute-start(bf16[64,1024]{1,0:T(8,128)(2,1)S(1)} %get-tuple-element.55), channel_id=1, source_target_pairs={{0,4},{2,6},{4,0},{6,2},{1,5},{3,7},{5,1},{7,3},{8,12},{10,14},{12... | collective-permute-start | bytes 393224 | tf_op jit(solution)/shard_map/ppermute | solution.py:380
  34.1 0.6 collective-permute-start.13
  34.8 4.2 %collective-permute-start.14 = (bf16[2,512]{1,0:T(2,128)(2,1)S(1)}, bf16[2,512]{1,0:T(2,128)(2,1)S(1)}, u32[]{:S(2)}, u32[]{:S(2)}) collective-permute-start(bf16[2,512]{1,0:T(2,128)(2,1)S(1)} %slice.3), channel_id=1, source_target_pairs={{0,2},{2,0},{4,6},{6,4},{8,10},{10,8},{12,14},{14,12},{16,18},{18,... | collective-permute-start | bytes 6152 | tf_op jit(solution)/shard_map/ppermute | solution.py:479
  39.0 1.6 %collective-permute-done.14.odd_ref = bf16[2,512]{1,0:T(2,128)(2,1)S(1)} collective-permute-done((bf16[2,512]{1,0:T(2,128)(2,1)S(1)}, bf16[2,512]{1,0:T(2,128)(2,1)S(1)}, u32[]{:S(2)}, u32[]{:S(2)}) %collective-permute-start.14) | collective-permute-done | bytes 2080 | tf_op jit(solution)/shard_map/ppermute | solution.py:479
  40.7 3.4 %collective-permute-start.15 = (bf16[16,1536]{1,0:T(8,128)(2,1)S(1)}, bf16[16,1536]{1,0:T(8,128)(2,1)S(1)}, u32[]{:S(2)}, u32[]{:S(2)}) collective-permute-start(bf16[16,1536]{1,0:T(8,128)(2,1)S(1)} %get-tuple-element.67), channel_id=1, source_target_pairs={{0,24},{8,16},{16,8},{24,0},{1,25},{9,17},{17,9},{25,1},{2,26},{10... | collective-permute-start | bytes 147464 | tf_op jit(solution)/shard_map/ppermute | solution.py:380
  44.4 0.7 %collective-permute-start.17 = (bf16[16,1536]{1,0:T(8,128)(2,1)S(1)}, bf16[16,1536]{1,0:T(8,128)(2,1)S(1)}, u32[]{:S(2)}, u32[]{:S(2)}) collective-permute-start(bf16[16,1536]{1,0:T(8,128)(2,1)S(1)} %get-tuple-element.69), channel_id=1, source_target_pairs={{0,8},{8,0},{16,24},{24,16},{1,9},{9,1},{17,25},{25,17},{2,10},{10... | collective-permute-start | bytes 147464 | tf_op jit(solution)/shard_map/ppermute | solution.py:380
  45.1 1.6 %collective-permute-done.15.refs_0_ = bf16[16,1536]{1,0:T(8,128)(2,1)S(1)} collective-permute-done((bf16[16,1536]{1,0:T(8,128)(2,1)S(1)}, bf16[16,1536]{1,0:T(8,128)(2,1)S(1)}, u32[]{:S(2)}, u32[]{:S(2)}) %collective-permute-start.15) | collective-permute-done | bytes 49184 | tf_op jit(solution)/shard_map/ppermute | solution.py:380
  46.7 2.4 %collective-permute-done.16.refs_1_ = bf16[16,1536]{1,0:T(8,128)(2,1)S(1)} collective-permute-done((bf16[16,1536]{1,0:T(8,128)(2,1)S(1)}, bf16[16,1536]{1,0:T(8,128)(2,1)S(1)}, u32[]{:S(2)}, u32[]{:S(2)}) %collective-permute-start.16) | collective-permute-done | bytes 49184 | tf_op jit(solution)/shard_map/ppermute | solution.py:380
  49.1 2.5 %mix.1 = bf16[32,16,128]{2,1,0:T(8,128)(2,1)S(1)} custom-call(f32[3,1024]{1,0:T(4,128)S(1)} %copy-done, bf16[16,1536]{1,0:T(8,128)(2,1)S(1)} %collective-permute-done.15.refs_0_, bf16[16,1536]{1,0:T(8,128)(2,1)S(1)} %collective-permute-done.16.refs_1_, bf16[16,1536]{1,0:T(8,128)(2,1)S(1)} %collective-permute-done.17.refs_2_, ...), custom_call_target="tpu_custom_call" | custom-call | flops 536870912 | bytes 2097152 | tf_op jit(solution)/shard_map/mix/pallas_call | solution.py:508
  51.6 10.9 %all_to_all.5 = bf16[32,16,128]{2,1,0:T(8,128)(2,1)S(1)} all-to-all(bf16[32,16,128]{2,1,0:T(8,128)(2,1)S(1)} %mix.1), channel_id=1, replica_groups=mesh['far'=4,'near'=4,'dp'=2] {'dp','far','near'}, dimensions={0} | all-to-all | bytes 262144 | tf_op jit(solution)/shard_map/all_to_all | solution.py:525
  62.5 4.1 %project_out.1 = bf16[128,4096]{1,0:T(8,128)(2,1)} custom-call(bf16[128,512]{1,0:T(8,128)(2,1)S(1)} %convolution_convert_fusion.gate_ref, bf16[2,512]{1,0:T(2,128)(2,1)S(1)} %collective-permute-done.13.even_ref, bf16[2,512]{1,0:T(2,128)(2,1)S(1)} %collective-permute-done.14.odd_ref, f32[3,1024]{1,0:T(4,128)S(1)} %copy-done, bf16[512,128]{1,0:T(8,128)(2,1)S(1)} %bitcast.4, ...), custom_call_target="tpu_custom_call" | custom-call | flops 536870912 | bytes 5242880 | tf_op jit(solution)/shard_map/project_out/pallas_call | solution.py:527
  (23 shorter events, 3.6 us)
Async XLA Ops:
  1.0 16.1 %collective-permute-start.3 = (bf16[256,512]{1,0:T(8,128)(2,1)S(1)}, bf16[256,512]{1,0:T(8,128)(2,1)S(1)}, u32[]{:S(2)}, u32[]{:S(2)}) collective-permute-start(bf16[256,512]{1,0:T(8,128)(2,1)S(1)} %weights.1), channel_id=1, source_target_pairs={{0,16},{8,24},{16,0},{24,8},{1,17},{9,25},{17,1},{25,9},{2,18},{10... | collective-permute-start | bytes 786440 | tf_op jit(solution)/shard_map/ppermute | solution.py:380
  7.3 12.8 %collective-permute-start.8 = (bf16[256,512]{1,0:T(8,128)(2,1)S(1)}, bf16[256,512]{1,0:T(8,128)(2,1)S(1)}, u32[]{:S(2)}, u32[]{:S(2)}) collective-permute-start(bf16[256,512]{1,0:T(8,128)(2,1)S(1)} %get-tuple-element.49.refs_8_), channel_id=1, source_target_pairs={{0,8},{8,0},{16,24},{24,16},{1,9},{9,1},{17,25},{25,17},{2,10},{10... | collective-permute-start | bytes 786440 | tf_op jit(solution)/shard_map/ppermute | solution.py:380
  8.9 14.5 %collective-permute-start = (bf16[128,1280]{1,0:T(8,128)(2,1)S(1)}, bf16[128,1280]{1,0:T(8,128)(2,1)S(1)}, u32[]{:S(2)}, u32[]{:S(2)}) collective-permute-start(bf16[128,1280]{1,0:T(8,128)(2,1)S(1)} %get-tuple-element.39), channel_id=1, source_target_pairs={{0,6},{2,4},{4,2},{6,0},{1,7},{3,5},{5,3},{7,1},{8,14},{10,12},{12... | collective-permute-start | bytes 983048 | tf_op jit(solution)/shard_map/ppermute | solution.py:380
  11.4 14.4 %collective-permute-start.1 = (bf16[128,1280]{1,0:T(8,128)(2,1)S(1)}, bf16[128,1280]{1,0:T(8,128)(2,1)S(1)}, u32[]{:S(2)}, u32[]{:S(2)}) collective-permute-start(bf16[128,1280]{1,0:T(8,128)(2,1)S(1)} %get-tuple-element.40), channel_id=1, source_target_pairs={{0,4},{2,6},{4,0},{6,2},{1,5},{3,7},{5,1},{7,3},{8,12},{10,14},{12... | collective-permute-start | bytes 983048 | tf_op jit(solution)/shard_map/ppermute | solution.py:380
  11.9 14.0 %collective-permute-start.2 = (bf16[128,1280]{1,0:T(8,128)(2,1)S(1)}, bf16[128,1280]{1,0:T(8,128)(2,1)S(1)}, u32[]{:S(2)}, u32[]{:S(2)}) collective-permute-start(bf16[128,1280]{1,0:T(8,128)(2,1)S(1)} %get-tuple-element.41), channel_id=1, source_target_pairs={{0,2},{2,0},{4,6},{6,4},{1,3},{3,1},{5,7},{7,5},{8,10},{10,8},{12,... | collective-permute-start | bytes 983048 | tf_op jit(solution)/shard_map/ppermute | solution.py:380
  17.1 9.2 %collective-permute-start.4 = (bf16[256,512]{1,0:T(8,128)(2,1)S(1)}, bf16[256,512]{1,0:T(8,128)(2,1)S(1)}, u32[]{:S(2)}, u32[]{:S(2)}) collective-permute-start(bf16[256,512]{1,0:T(8,128)(2,1)S(1)} %collective-permute-done.3.refs_10_), channel_id=1, source_target_pairs={{0,8},{8,0},{16,24},{24,16},{1,9},{9,1},{17,25},{25,17},{2,10},{10... | collective-permute-start | bytes 786440 | tf_op jit(solution)/shard_map/ppermute | solution.py:380
  20.1 29.0 %copy-start = (f32[3,1024]{1,0:T(4,128)S(1)}, f32[3,1024]{1,0:T(4,128)}, u32[]{:S(2)}) copy-start(f32[3,1024]{1,0:T(4,128)} %taps_ref.3) | copy-start | bytes 36868
  20.1 6.2 %collective-permute-start.9 = (bf16[128,1280]{1,0:T(8,128)(2,1)S(1)}, bf16[128,1280]{1,0:T(8,128)(2,1)S(1)}, u32[]{:S(2)}, u32[]{:S(2)}) collective-permute-start(bf16[128,1280]{1,0:T(8,128)(2,1)S(1)} %get-tuple-element.51.refs_7_), channel_id=1, source_target_pairs={{0,1},{1,0},{2,3},{3,2},{4,5},{5,4},{6,7},{7,6},{8,9},{9,8},{10,11... | collective-permute-start | bytes 983048 | tf_op jit(solution)/shard_map/ppermute | solution.py:380
  25.8 1.6 %collective-permute-start.6 = (bf16[128,1280]{1,0:T(8,128)(2,1)S(1)}, bf16[128,1280]{1,0:T(8,128)(2,1)S(1)}, u32[]{:S(2)}, u32[]{:S(2)}) collective-permute-start(bf16[128,1280]{1,0:T(8,128)(2,1)S(1)} %collective-permute-done.1.refs_5_), channel_id=1, source_target_pairs={{0,1},{1,0},{2,3},{3,2},{4,5},{5,4},{6,7},{7,6},{8,9},{9,8},{10,11... | collective-permute-start | bytes 983048 | tf_op jit(solution)/shard_map/ppermute | solution.py:380
  25.8 2.1 %collective-permute-start.7 = (bf16[128,1280]{1,0:T(8,128)(2,1)S(1)}, bf16[128,1280]{1,0:T(8,128)(2,1)S(1)}, u32[]{:S(2)}, u32[]{:S(2)}) collective-permute-start(bf16[128,1280]{1,0:T(8,128)(2,1)S(1)} %collective-permute-done.2.refs_6_), channel_id=1, source_target_pairs={{0,1},{1,0},{2,3},{3,2},{4,5},{5,4},{6,7},{7,6},{8,9},{9,8},{10,11... | collective-permute-start | bytes 983048 | tf_op jit(solution)/shard_map/ppermute | solution.py:380
  26.3 2.1 %collective-permute-start.5 = (bf16[128,1280]{1,0:T(8,128)(2,1)S(1)}, bf16[128,1280]{1,0:T(8,128)(2,1)S(1)}, u32[]{:S(2)}, u32[]{:S(2)}) collective-permute-start(bf16[128,1280]{1,0:T(8,128)(2,1)S(1)} %collective-permute-done.refs_4_), channel_id=1, source_target_pairs={{0,1},{1,0},{2,3},{3,2},{4,5},{5,4},{6,7},{7,6},{8,9},{9,8},{10,11... | collective-permute-start | bytes 983048 | tf_op jit(solution)/shard_map/ppermute | solution.py:380
  30.5 10.0 %collective-permute-start.10 = (bf16[64,1024]{1,0:T(8,128)(2,1)S(1)}, bf16[64,1024]{1,0:T(8,128)(2,1)S(1)}, u32[]{:S(2)}, u32[]{:S(2)}) collective-permute-start(bf16[64,1024]{1,0:T(8,128)(2,1)S(1)} %get-tuple-element.54), channel_id=1, source_target_pairs={{0,6},{2,4},{4,2},{6,0},{1,7},{3,5},{5,3},{7,1},{8,14},{10,12},{12... | collective-permute-start | bytes 393224 | tf_op jit(solution)/shard_map/ppermute | solution.py:380
  32.3 8.3 %collective-permute-start.11 = (bf16[64,1024]{1,0:T(8,128)(2,1)S(1)}, bf16[64,1024]{1,0:T(8,128)(2,1)S(1)}, u32[]{:S(2)}, u32[]{:S(2)}) collective-permute-start(bf16[64,1024]{1,0:T(8,128)(2,1)S(1)} %get-tuple-element.55), channel_id=1, source_target_pairs={{0,4},{2,6},{4,0},{6,2},{1,5},{3,7},{5,1},{7,3},{8,12},{10,14},{12... | collective-permute-start | bytes 393224 | tf_op jit(solution)/shard_map/ppermute | solution.py:380
  33.6 7.0 %collective-permute-start.12 = (bf16[64,1024]{1,0:T(8,128)(2,1)S(1)}, bf16[64,1024]{1,0:T(8,128)(2,1)S(1)}, u32[]{:S(2)}, u32[]{:S(2)}) collective-permute-start(bf16[64,1024]{1,0:T(8,128)(2,1)S(1)} %get-tuple-element.56), channel_id=1, source_target_pairs={{0,2},{2,0},{4,6},{6,4},{1,3},{3,1},{5,7},{7,5},{8,10},{10,8},{12,... | collective-permute-start | bytes 393224 | tf_op jit(solution)/shard_map/ppermute | solution.py:380
  34.1 4.9 %collective-permute-start.13 = (bf16[2,512]{1,0:T(2,128)(2,1)S(1)}, bf16[2,512]{1,0:T(2,128)(2,1)S(1)}, u32[]{:S(2)}, u32[]{:S(2)}) collective-permute-start(bf16[2,512]{1,0:T(2,128)(2,1)S(1)} %slice.3), channel_id=1, source_target_pairs={{2,4},{4,2},{6,8},{8,6},{10,12},{12,10},{14,16},{16,14},{18,20},{2... | collective-permute-start | bytes 6152 | tf_op jit(solution)/shard_map/ppermute | solution.py:479
  34.8 5.8 %collective-permute-start.14 = (bf16[2,512]{1,0:T(2,128)(2,1)S(1)}, bf16[2,512]{1,0:T(2,128)(2,1)S(1)}, u32[]{:S(2)}, u32[]{:S(2)}) collective-permute-start(bf16[2,512]{1,0:T(2,128)(2,1)S(1)} %slice.3), channel_id=1, source_target_pairs={{0,2},{2,0},{4,6},{6,4},{8,10},{10,8},{12,14},{14,12},{16,18},{18,... | collective-permute-start | bytes 6152 | tf_op jit(solution)/shard_map/ppermute | solution.py:479
  40.7 6.1 %collective-permute-start.15 = (bf16[16,1536]{1,0:T(8,128)(2,1)S(1)}, bf16[16,1536]{1,0:T(8,128)(2,1)S(1)}, u32[]{:S(2)}, u32[]{:S(2)}) collective-permute-start(bf16[16,1536]{1,0:T(8,128)(2,1)S(1)} %get-tuple-element.67), channel_id=1, source_target_pairs={{0,24},{8,16},{16,8},{24,0},{1,25},{9,17},{17,9},{25,1},{2,26},{10... | collective-permute-start | bytes 147464 | tf_op jit(solution)/shard_map/ppermute | solution.py:380
  44.1 5.0 %collective-permute-start.16 = (bf16[16,1536]{1,0:T(8,128)(2,1)S(1)}, bf16[16,1536]{1,0:T(8,128)(2,1)S(1)}, u32[]{:S(2)}, u32[]{:S(2)}) collective-permute-start(bf16[16,1536]{1,0:T(8,128)(2,1)S(1)} %get-tuple-element.68), channel_id=1, source_target_pairs={{0,16},{8,24},{16,0},{24,8},{1,17},{9,25},{17,1},{25,9},{2,18},{10... | collective-permute-start | bytes 147464 | tf_op jit(solution)/shard_map/ppermute | solution.py:380
  44.4 4.7 %collective-permute-start.17 = (bf16[16,1536]{1,0:T(8,128)(2,1)S(1)}, bf16[16,1536]{1,0:T(8,128)(2,1)S(1)}, u32[]{:S(2)}, u32[]{:S(2)}) collective-permute-start(bf16[16,1536]{1,0:T(8,128)(2,1)S(1)} %get-tuple-element.69), channel_id=1, source_target_pairs={{0,8},{8,0},{16,24},{24,16},{1,9},{9,1},{17,25},{25,17},{2,10},{10... | collective-permute-start | bytes 147464 | tf_op jit(solution)/shard_map/ppermute | solution.py:380

commit v3 on v0

--- a/solution.py
+++ b/solution.py
@@ -135,12 +135,12 @@
     return jnp.concatenate([part for own in split for part in (own, spare)], axis=0)
 
 
-def project_kernel(near, far, cores, depth, *refs):
-    outs, (out_lags_ref, whole_ref) = refs[-2 - near : -2], refs[-2:]
-    chunks, pieces = refs[: near * cores][::-1], refs[near * cores : -2 - near]
-    core, near_at = lax.axis_index("dp"), lax.axis_index("near")
-    rows = chunks[0].shape[0]
-    half = pieces[0].shape[1] // 2
+def joined(chunks, start, stop):
+    return jnp.concatenate([chunk[:, start:stop] for chunk in chunks], axis=0)
+
+
+def flips(chunks, depth, cores, half):
+    core = lax.axis_index("dp")
     words = depth // 16
     sent_words = cores * half // 16
     sent_start = depth + 2 * words
@@ -151,30 +151,61 @@
     def out_byte(column):
         return core * (half // 16) + (column >> 4) + sent_words * ((column >> 3) & 1)
 
-    def joined(start, stop):
-        return jnp.concatenate([chunk[:, start:stop] for chunk in chunks], axis=0)
-
-    flip_in = spread_signs(joined(depth, sent_start), in_byte, depth).astype(BF16)
-    flip_out = spread_signs(joined(sent_start, sent_start + 2 * sent_words), out_byte, half)
+    flip_in = spread_signs(joined(chunks, depth, sent_start), in_byte, depth).astype(BF16)
+    sent = joined(chunks, sent_start, sent_start + 2 * sent_words)
+    return flip_in, spread_signs(sent, out_byte, half)
+
+
+def products(chunks, flip_in, pieces, half):
     mean_part, noise_part = 0.0, 0.0
-    step = depth // len(pieces)
     for at, piece in enumerate(pieces):
-        tokens = joined(at * step, (at + 1) * step)
-        flipped = tokens * flip_in[:, at * step : (at + 1) * step]
+        own = slice(at * piece.shape[0], (at + 1) * piece.shape[0])
+        tokens = joined(chunks, own.start, own.stop)
         mean_part += jnp.dot(tokens, piece[:, :half], preferred_element_type=F32)
-        noise_part += jnp.dot(flipped, piece[:, half:], preferred_element_type=F32)
+        noise_part += jnp.dot(tokens * flip_in[:, own], piece[:, half:], preferred_element_type=F32)
+    return mean_part, noise_part
+
+
+def project_kernel(near, cores, depth, *refs):
+    mean_ref, noise_ref, flip_ref, flipped_ref, lags_ref = refs[-5:]
+    count = near * cores - 1
+    chunks, pieces = refs[:count][::-1], refs[count:-5]
+    rows = chunks[0].shape[0]
+    half = pieces[0].shape[1] // 2
+    step = pieces[0].shape[0]
+    flip_in, flip_out = flips(chunks, depth, cores, half)
+    flip_ref[...] = flip_out.astype(BF16)
+    flipped_ref[...] = joined(chunks, depth - step, depth) * flip_in[:, depth - step :]
+    mean_ref[...], noise_ref[...] = products(chunks, flip_in, pieces, half)
+    for turn in range(near):
+        own_lags = chunks[turn][:, chunks[turn].shape[1] - lags_ref.shape[0] :].astype(F32).T
+        at = pl.multiple_of((lax.axis_index("near") ^ turn) * rows, rows)
+        lags_ref[:, pl.ds(at, rows)] = own_lags
+
+
+def finish_kernel(near, far, cores, depth, mean_ref, noise_ref, flip_ref, flipped_ref, *refs):
+    outs, whole_ref = refs[-1 - near : -1], refs[-1]
+    chunks, pieces = refs[: near * cores][::-1], refs[near * cores : -1 - near]
+    core, near_at = lax.axis_index("dp"), lax.axis_index("near")
+    rows = chunks[0].shape[0]
+    step, half = pieces[0].shape[0], pieces[0].shape[1] // 2
+    last = pieces[-1]
+    flip_in, flip_out = flips(chunks[-1:], depth, cores, half)
+    mean_late, noise_late = products(chunks[-1:], flip_in, pieces, half)
+    tokens = joined(chunks[:-1], depth - step, depth)
+    mean_part = mean_ref[...] + jnp.dot(tokens, last[:, :half], preferred_element_type=F32)
+    noise_part = noise_ref[...] + jnp.dot(flipped_ref[...], last[:, half:], preferred_element_type=F32)
     held = half // (near * far)
     stride = max(held, GROUP)
-    value = spaced((mean_part + flip_out * noise_part).T, held)
+    value = jnp.concatenate(
+        [mean_part + flip_ref[...].astype(F32) * noise_part, mean_late + flip_out * noise_late], axis=0
+    )
+    value = spaced(value.T, held)
     for part in range(cores):
         for turn in range(near):
             at = part * near + turn
             target = ((core ^ part) * near + (near_at ^ turn)) * rows
             whole_ref[:, pl.ds(pl.multiple_of(target, rows), rows)] = value[:, at * rows : (at + 1) * rows]
-    for turn in range(near):
-        own_lags = chunks[turn][:, sent_start + 2 * sent_words :].astype(F32).T
-        at = pl.multiple_of((near_at ^ turn) * rows, rows)
-        out_lags_ref[:, pl.ds(at, rows)] = own_lags
     for turn, out in enumerate(outs):
         for plane in range(far):
             at = pl.multiple_of((plane * near + (near_at ^ turn)) * stride, stride)
@@ -449,26 +480,45 @@
 
     late_tokens = tokens
     if len(pieces) > 1:
-        pieces[1], chunks[0] = lax.optimization_barrier((pieces[1], chunks[0]))
         late_tokens, pieces[2] = lax.optimization_barrier((tokens, pieces[2]))
         pieces[3] = exchanged(pieces[2], "far", 1)
     gate_rows = jnp.dot(late_tokens, w_gate, preferred_element_type=F32).astype(BF16)
-    *chunks[:0:-1], gate_rows = lax.optimization_barrier((*chunks[:0:-1], gate_rows))
+    late = 1 % len(pieces)
+    *chunks[::-1], gate_rows, pieces[late] = lax.optimization_barrier((*chunks[::-1], gate_rows, pieces[late]))
     pieces[-1], chunks[-1] = lax.optimization_barrier((pieces[-1], chunks[-1]))
     chunks += [exchanged(chunk, "dp", 1) for chunk in chunks]
 
+    if len(pieces) == 1:
+        pieces = [pieces[0][: depth // 2], pieces[0][depth // 2 :]]
+    step = depth // len(pieces)
+    early = (cores * near - 1) * rows
+    *kept, lags = pl.pallas_call(
+        functools.partial(project_kernel, near, cores, depth),
+        in_specs=[VMEM] * (len(chunks) + len(pieces) - 2),
+        out_specs=[VMEM] * 5,
+        out_shape=[
+            jax.ShapeDtypeStruct((early, half), F32),
+            jax.ShapeDtypeStruct((early, half), F32),
+            jax.ShapeDtypeStruct((early, half), BF16),
+            jax.ShapeDtypeStruct((early, step), BF16),
+            jax.ShapeDtypeStruct((far * held, near * rows), F32),
+        ],
+        compiler_params=params(32),
+        cost_estimate=cost(4 * early * (depth - step) * half, 5 * MIB),
+        name="project",
+    )(*chunks[-2::-1], *pieces[:-1])
     near_shape = jax.ShapeDtypeStruct((far * held, cores * near * rows), BF16)
     partial = pl.pallas_call(
-        functools.partial(project_kernel, near, far, cores, depth),
-        in_specs=[VMEM] * (len(chunks) + len(pieces)),
-        out_specs=[VMEM] * (near + 1),
-        out_shape=[near_shape] * near + [jax.ShapeDtypeStruct((far * held, near * rows), F32)],
+        functools.partial(finish_kernel, near, far, cores, depth),
+        in_specs=[VMEM] * (4 + len(chunks) + len(pieces)),
+        out_specs=[VMEM] * near,
+        out_shape=[near_shape] * near,
         scratch_shapes=[pltpu.VMEM((count * max(held, GROUP), near_shape.shape[1]), F32)],
-        compiler_params=params(40),
-        cost_estimate=cost(4 * cores * near * rows * depth * half, 6 * MIB),
-        name="project",
-    )(*chunks[::-1], *pieces)
-    *partial, lags = partial
+        compiler_params=params(32),
+        cost_estimate=cost(4 * (early * step + rows * depth) * half, 3 * MIB),
+        name="finish",
+    )(*kept, *chunks[::-1], *pieces)
+    partial = list(partial)
     last_rows, partial[0] = lax.optimization_barrier((gate_rows[rows - 2 :], partial[0]))
     before = lax.ppermute(last_rows, ("far", "near"), [(i, i + 1) for i in range(count - 1)])
     partial = all_exchanged(partial, "near")

time: 65.9 us -> 66.2 us (level)
    ppermute x16, waiting for transfers between devices: 16.8 us -> 16 us  [exchanged(): lax.ppermute(value, axis, [(i, i ^ step) for i in range(lax.axis_size(axi...]
    pallas_call x1 -> x2, Pallas kernels: 2.15 us -> 2.57 us  [the longest x1 1.73 us: on_device(): pl.pallas_call(functools.partial(project_kernel, near, cores, depth), in_...]
  transfers between devices with their start and end apart: 17 -> 17, of which waited for: 11 -> 10; matrix products, arithmetic and copies ran while one was open for 5% -> 5% of each run, Pallas kernels for 3% -> 6%
where the time goes in v3:
time: 66.2 us; the launch traced here: 66 us
  starting transfers between devices  21.9 us (33%)
  waiting for transfers between devices  17.9 us (27%)
  Pallas kernels  12.4 us (19%)
  blocking collectives  10.5 us (16%)
  matrix products  3.23 us (5%)
    ppermute x16, starting transfers between devices, exchanged(): lax.ppermute(value, axis, [(i, i ^ step) for i in range(lax.axis_size(axi...  18.4 us
    ppermute x16, waiting for transfers between devices, exchanged(): lax.ppermute(value, axis, [(i, i ^ step) for i in range(lax.axis_size(axi...  16 us
    all_to_all x1, blocking collectives, on_device(): lax.all_to_all(mixed, ('dp', 'far', 'near'), 0, 0, tiled=True)  10.5 us
    pallas_call x1, Pallas kernels, on_device(): pl.pallas_call(out_kernel, in_specs=[ANY] * 4 + [HBM], out_specs=HBM, out...  4.09 us
    ppermute x1, starting transfers between devices, on_device(): lax.ppermute(last_rows, ('far', 'near'), [(i, i + 1) for i in range(count...  3.45 us
    dot_general x1, matrix products, on_device(): jnp.dot(late_tokens, w_gate, preferred_element_type=F32).astype(BF16)  3.23 us
    pallas_call x1, Pallas kernels, on_device(): pl.pallas_call(functools.partial(mix_kernel, near, far, cores, held), in_...  2.51 us
    pallas_call x1, Pallas kernels, on_device(): pl.pallas_call(functools.partial(pack_kernel, near, far), in_specs=[HBM]...  2.16 us
  transfers between devices with their start and end apart: 17, of which 10 were waited for; matrix products, arithmetic and copies ran while one was open for 5% of the time, Pallas kernels for 6%

profile of v3, /device:TPU:0, one launch (start us, length us, event | category | flops | bytes accessed | tf_op | source)
XLA Modules:
  0.0 66.0 jit_solution(15414572909581050645)
XLA Ops:
  0.0 1.0 %weights.1 = bf16[256,512]{1,0:T(8,128)(2,1)S(1)} custom-call(bf16[256,512]{1,0:T(8,128)(2,1)} %value_ref.3, bf16[256,512]{1,0:T(8,128)(2,1)} %noise_ref.3), custom_call_target="tpu_custom_call" | custom-call | bytes 524288 | tf_op jit(solution)/shard_map/weights/pallas_call | solution.py:432
  1.0 4.1 %collective-permute-start.3 = (bf16[256,512]{1,0:T(8,128)(2,1)S(1)}, bf16[256,512]{1,0:T(8,128)(2,1)S(1)}, u32[]{:S(2)}, u32[]{:S(2)}) collective-permute-start(bf16[256,512]{1,0:T(8,128)(2,1)S(1)} %weights.1), channel_id=1, source_target_pairs={{0,16},{8,24},{16,0},{24,8},{1,17},{9,25},{17,1},{25,9},{2,18},{10... | collective-permute-start | bytes 786440 | tf_op jit(solution)/shard_map/ppermute | solution.py:407
  5.1 2.2 %pack.1 = (bf16[256,512]{1,0:T(8,128)(2,1)S(1)}, bf16[128,1280]{1,0:T(8,128)(2,1)S(1)}, bf16[128,1280]{1,0:T(8,128)(2,1)S(1)}, bf16[128,1280]{1,0:T(8,128)(2,1)S(1)}, bf16[128,1280]{1,0:T(8,128)(2,1)S(1)}) custom-call(bf16[128,4096]{1,0:T(8,128)(2,1)} %tokens_ref, s32[128,256]{1,0:T(8,128)} %in_ref.1, s32[32,128]{1,0:T(8,128)} %bitcast.5, ...), custom_call_target="tpu_custom_call" | custom-call | flops 67108864 | bytes 3145728 | tf_op jit(solution)/shard_map/pack/pallas_call | solution.py:444
  7.3 2.5 %collective-permute-start = (bf16[128,1280]{1,0:T(8,128)(2,1)S(1)}, bf16[128,1280]{1,0:T(8,128)(2,1)S(1)}, u32[]{:S(2)}, u32[]{:S(2)}) collective-permute-start(bf16[128,1280]{1,0:T(8,128)(2,1)S(1)} %get-tuple-element.42), channel_id=1, source_target_pairs={{0,6},{2,4},{4,2},{6,0},{1,7},{3,5},{5,3},{7,1},{8,14},{10,12},{12... | collective-permute-start | bytes 983048 | tf_op jit(solution)/shard_map/ppermute | solution.py:407
  10.8 1.6 %collective-permute-start.4 = (bf16[256,512]{1,0:T(8,128)(2,1)S(1)}, bf16[256,512]{1,0:T(8,128)(2,1)S(1)}, u32[]{:S(2)}, u32[]{:S(2)}) collective-permute-start(bf16[256,512]{1,0:T(8,128)(2,1)S(1)} %get-tuple-element.47.refs_7_.refs_8_), channel_id=1, source_target_pairs={{0,8},{8,0},{16,24},{24,16},{1,9},{9,1},{17,25},{25,17},{2,10},{10... | collective-permute-start | bytes 786440 | tf_op jit(solution)/shard_map/ppermute | solution.py:407
  12.4 4.7 %collective-permute-done.3.refs_9_.refs_10_ = bf16[256,512]{1,0:T(8,128)(2,1)S(1)} collective-permute-done((bf16[256,512]{1,0:T(8,128)(2,1)S(1)}, bf16[256,512]{1,0:T(8,128)(2,1)S(1)}, u32[]{:S(2)}, u32[]{:S(2)}) %collective-permute-start.3) | collective-permute-done | bytes 262176 | tf_op jit(solution)/shard_map/ppermute | solution.py:407
  17.1 0.7 %collective-permute-start.8 = (bf16[256,512]{1,0:T(8,128)(2,1)S(1)}, bf16[256,512]{1,0:T(8,128)(2,1)S(1)}, u32[]{:S(2)}, u32[]{:S(2)}) collective-permute-start(bf16[256,512]{1,0:T(8,128)(2,1)S(1)} %collective-permute-done.3.refs_9_.refs_10_), channel_id=1, source_target_pairs={{0,8},{8,0},{16,24},{24,16},{1,9},{9,1},{17,25},{25,17},{2,10},{10... | collective-permute-start | bytes 786440 | tf_op jit(solution)/shard_map/ppermute | solution.py:407
  17.8 3.2 %convolution_convert_fusion.gate_ref = bf16[128,512]{1,0:T(8,128)(2,1)S(1)} fusion(bf16[128,4096]{1,0:T(8,128)(2,1)} %tokens_ref, bf16[4096,512]{1,0:T(8,128)(2,1)} %param.14), kind=kOutput, calls=%fused_computation | convolution fusion | flops 536936448 | bytes 5373952 | tf_op jit(solution)/shard_map/dot_general | solution.py:485
  21.0 1.8 %collective-permute-done.4.refs_8_.refs_9_ = bf16[256,512]{1,0:T(8,128)(2,1)S(1)} collective-permute-done((bf16[256,512]{1,0:T(8,128)(2,1)S(1)}, bf16[256,512]{1,0:T(8,128)(2,1)S(1)}, u32[]{:S(2)}, u32[]{:S(2)}) %collective-permute-start.4) | collective-permute-done | bytes 262176 | tf_op jit(solution)/shard_map/ppermute | solution.py:407
  22.8 1.6 %collective-permute-done.1.refs_4_.refs_5_ = bf16[128,1280]{1,0:T(8,128)(2,1)S(1)} collective-permute-done((bf16[128,1280]{1,0:T(8,128)(2,1)S(1)}, bf16[128,1280]{1,0:T(8,128)(2,1)S(1)}, u32[]{:S(2)}, u32[]{:S(2)}) %collective-permute-start.1) | collective-permute-done | bytes 327712 | tf_op jit(solution)/shard_map/ppermute | solution.py:407
  25.0 2.7 %collective-permute-done.8.refs_11_ = bf16[256,512]{1,0:T(8,128)(2,1)S(1)} collective-permute-done((bf16[256,512]{1,0:T(8,128)(2,1)S(1)}, bf16[256,512]{1,0:T(8,128)(2,1)S(1)}, u32[]{:S(2)}, u32[]{:S(2)}) %collective-permute-start.8) | collective-permute-done | bytes 262176 | tf_op jit(solution)/shard_map/ppermute | solution.py:407
  27.8 1.7 %project.1 = (f32[896,256]{1,0:T(8,128)S(1)}, f32[896,256]{1,0:T(8,128)S(1)}, bf16[896,256]{1,0:T(8,128)(2,1)S(1)}, bf16[896,256]{1,0:T(8,128)(2,1)S(1)}, f32[64,512]{1,0:T(8,128)S(1)}) custom-call(bf16[128,1280]{1,0:T(8,128)(2,1)S(1)} %collective-permute-done.5.refs_0_.refs_1_, bf16[128,1280]{1,0:T(8,128)(2,1)S(1)} %collective-permute-done.6.refs_1_.refs_2_, ...), custom_call_target="tpu_custom_call" | custom-call | flops 704643072 | bytes 5242880 | tf_op jit(solution)/shard_map/project/pallas_call | solution.py:495
  29.6 0.8 %finish.1 = (bf16[64,1024]{1,0:T(8,128)(2,1)S(1)}, bf16[64,1024]{1,0:T(8,128)(2,1)S(1)}, bf16[64,1024]{1,0:T(8,128)(2,1)S(1)}, bf16[64,1024]{1,0:T(8,128)(2,1)S(1)}) custom-call(f32[896,256]{1,0:T(8,128)S(1)} %get-tuple-element.56.mean_ref, f32[896,256]{1,0:T(8,128)S(1)} %get-tuple-element.57.noise_ref, bf16[896,256]{1,0:T(8,128)(2,1)S(1)} %get-tuple-element.58.flip_ref, ...), custom_call_target="tpu_custom_call" | custom-call | flops 369098752 | bytes 3145728 | tf_op jit(solution)/shard_map/finish/pallas_call | solution.py:511
  30.4 2.6 %collective-permute-start.10 = (bf16[64,1024]{1,0:T(8,128)(2,1)S(1)}, bf16[64,1024]{1,0:T(8,128)(2,1)S(1)}, u32[]{:S(2)}, u32[]{:S(2)}) collective-permute-start(bf16[64,1024]{1,0:T(8,128)(2,1)S(1)} %get-tuple-element.61), channel_id=1, source_target_pairs={{0,6},{2,4},{4,2},{6,0},{1,7},{3,5},{5,3},{7,1},{8,14},{10,12},{12... | collective-permute-start | bytes 393224 | tf_op jit(solution)/shard_map/ppermute | solution.py:407
  34.0 3.4 %collective-permute-start.13 = (bf16[2,512]{1,0:T(2,128)(2,1)S(1)}, bf16[2,512]{1,0:T(2,128)(2,1)S(1)}, u32[]{:S(2)}, u32[]{:S(2)}) collective-permute-start(bf16[2,512]{1,0:T(2,128)(2,1)S(1)} %slice.3), channel_id=1, source_target_pairs={{0,2},{2,4},{4,6},{6,8},{8,10},{10,12},{12,14},{14,16},{16,18},{18... | collective-permute-start | bytes 6152 | tf_op jit(solution)/shard_map/ppermute | solution.py:523
  37.4 1.9 %collective-permute-done.13.before_ref = bf16[2,512]{1,0:T(2,128)(2,1)S(1)} collective-permute-done((bf16[2,512]{1,0:T(2,128)(2,1)S(1)}, bf16[2,512]{1,0:T(2,128)(2,1)S(1)}, u32[]{:S(2)}, u32[]{:S(2)}) %collective-permute-start.13) | collective-permute-done | bytes 2080 | tf_op jit(solution)/shard_map/ppermute | solution.py:523
  39.3 0.8 %collective-permute-done.11.refs_1_ = bf16[64,1024]{1,0:T(8,128)(2,1)S(1)} collective-permute-done((bf16[64,1024]{1,0:T(8,128)(2,1)S(1)}, bf16[64,1024]{1,0:T(8,128)(2,1)S(1)}, u32[]{:S(2)}, u32[]{:S(2)}) %collective-permute-start.11) | collective-permute-done | bytes 131104 | tf_op jit(solution)/shard_map/ppermute | solution.py:407
  40.4 3.5 %collective-permute-start.14 = (bf16[16,1536]{1,0:T(8,128)(2,1)S(1)}, bf16[16,1536]{1,0:T(8,128)(2,1)S(1)}, u32[]{:S(2)}, u32[]{:S(2)}) collective-permute-start(bf16[16,1536]{1,0:T(8,128)(2,1)S(1)} %get-tuple-element.73), channel_id=1, source_target_pairs={{0,24},{8,16},{16,8},{24,0},{1,25},{9,17},{17,9},{25,1},{2,26},{10... | collective-permute-start | bytes 147464 | tf_op jit(solution)/shard_map/ppermute | solution.py:407
  43.9 0.9 %collective-permute-start.16 = (bf16[16,1536]{1,0:T(8,128)(2,1)S(1)}, bf16[16,1536]{1,0:T(8,128)(2,1)S(1)}, u32[]{:S(2)}, u32[]{:S(2)}) collective-permute-start(bf16[16,1536]{1,0:T(8,128)(2,1)S(1)} %get-tuple-element.75), channel_id=1, source_target_pairs={{0,8},{8,0},{16,24},{24,16},{1,9},{9,1},{17,25},{25,17},{2,10},{10... | collective-permute-start | bytes 147464 | tf_op jit(solution)/shard_map/ppermute | solution.py:407
  44.8 1.5 %collective-permute-done.14.refs_0_ = bf16[16,1536]{1,0:T(8,128)(2,1)S(1)} collective-permute-done((bf16[16,1536]{1,0:T(8,128)(2,1)S(1)}, bf16[16,1536]{1,0:T(8,128)(2,1)S(1)}, u32[]{:S(2)}, u32[]{:S(2)}) %collective-permute-start.14) | collective-permute-done | bytes 49184 | tf_op jit(solution)/shard_map/ppermute | solution.py:407
  46.4 2.5 %collective-permute-done.15.refs_1_ = bf16[16,1536]{1,0:T(8,128)(2,1)S(1)} collective-permute-done((bf16[16,1536]{1,0:T(8,128)(2,1)S(1)}, bf16[16,1536]{1,0:T(8,128)(2,1)S(1)}, u32[]{:S(2)}, u32[]{:S(2)}) %collective-permute-start.15) | collective-permute-done | bytes 49184 | tf_op jit(solution)/shard_map/ppermute | solution.py:407
  48.9 2.5 %mix.1 = bf16[32,16,128]{2,1,0:T(8,128)(2,1)S(1)} custom-call(f32[3,1024]{1,0:T(4,128)S(1)} %copy-done, bf16[16,1536]{1,0:T(8,128)(2,1)S(1)} %collective-permute-done.14.refs_0_, bf16[16,1536]{1,0:T(8,128)(2,1)S(1)} %collective-permute-done.15.refs_1_, bf16[16,1536]{1,0:T(8,128)(2,1)S(1)} %collective-permute-done.16.refs_2_, ...), custom_call_target="tpu_custom_call" | custom-call | flops 536870912 | bytes 2097152 | tf_op jit(solution)/shard_map/mix/pallas_call | solution.py:548
  51.4 10.5 %all_to_all.5 = bf16[32,16,128]{2,1,0:T(8,128)(2,1)S(1)} all-to-all(bf16[32,16,128]{2,1,0:T(8,128)(2,1)S(1)} %mix.1), channel_id=1, replica_groups=mesh['far'=4,'near'=4,'dp'=2] {'dp','far','near'}, dimensions={0} | all-to-all | bytes 262144 | tf_op jit(solution)/shard_map/all_to_all | solution.py:565
  61.9 4.1 %project_out.1 = bf16[128,4096]{1,0:T(8,128)(2,1)} custom-call(bf16[128,512]{1,0:T(8,128)(2,1)S(1)} %convolution_convert_fusion.gate_ref, bf16[2,512]{1,0:T(2,128)(2,1)S(1)} %collective-permute-done.13.before_ref, f32[3,1024]{1,0:T(4,128)S(1)} %copy-done, bf16[512,128]{1,0:T(8,128)(2,1)S(1)} %bitcast.4, bf16[512,4096]{1,0:T(8,128)(2,1)} %source_ref.1), custom_call_target="tpu_custom_call" | custom-call | flops 536870912 | bytes 5242880 | tf_op jit(solution)/shard_map/project_out/pallas_call | solution.py:567
  (22 shorter events, 3.0 us)
Async XLA Ops:
  1.0 16.1 %collective-permute-start.3 = (bf16[256,512]{1,0:T(8,128)(2,1)S(1)}, bf16[256,512]{1,0:T(8,128)(2,1)S(1)}, u32[]{:S(2)}, u32[]{:S(2)}) collective-permute-start(bf16[256,512]{1,0:T(8,128)(2,1)S(1)} %weights.1), channel_id=1, source_target_pairs={{0,16},{8,24},{16,0},{24,8},{1,17},{9,25},{17,1},{25,9},{2,18},{10... | collective-permute-start | bytes 786440 | tf_op jit(solution)/shard_map/ppermute | solution.py:407
  7.3 15.5 %collective-permute-start = (bf16[128,1280]{1,0:T(8,128)(2,1)S(1)}, bf16[128,1280]{1,0:T(8,128)(2,1)S(1)}, u32[]{:S(2)}, u32[]{:S(2)}) collective-permute-start(bf16[128,1280]{1,0:T(8,128)(2,1)S(1)} %get-tuple-element.42), channel_id=1, source_target_pairs={{0,6},{2,4},{4,2},{6,0},{1,7},{3,5},{5,3},{7,1},{8,14},{10,12},{12... | collective-permute-start | bytes 983048 | tf_op jit(solution)/shard_map/ppermute | solution.py:407
  9.8 14.7 %collective-permute-start.1 = (bf16[128,1280]{1,0:T(8,128)(2,1)S(1)}, bf16[128,1280]{1,0:T(8,128)(2,1)S(1)}, u32[]{:S(2)}, u32[]{:S(2)}) collective-permute-start(bf16[128,1280]{1,0:T(8,128)(2,1)S(1)} %get-tuple-element.43), channel_id=1, source_target_pairs={{0,4},{2,6},{4,0},{6,2},{1,5},{3,7},{5,1},{7,3},{8,12},{10,14},{12... | collective-permute-start | bytes 983048 | tf_op jit(solution)/shard_map/ppermute | solution.py:407
  10.3 14.2 %collective-permute-start.2 = (bf16[128,1280]{1,0:T(8,128)(2,1)S(1)}, bf16[128,1280]{1,0:T(8,128)(2,1)S(1)}, u32[]{:S(2)}, u32[]{:S(2)}) collective-permute-start(bf16[128,1280]{1,0:T(8,128)(2,1)S(1)} %get-tuple-element.44), channel_id=1, source_target_pairs={{0,2},{2,0},{4,6},{6,4},{1,3},{3,1},{5,7},{7,5},{8,10},{10,8},{12,... | collective-permute-start | bytes 983048 | tf_op jit(solution)/shard_map/ppermute | solution.py:407
  10.8 12.0 %collective-permute-start.4 = (bf16[256,512]{1,0:T(8,128)(2,1)S(1)}, bf16[256,512]{1,0:T(8,128)(2,1)S(1)}, u32[]{:S(2)}, u32[]{:S(2)}) collective-permute-start(bf16[256,512]{1,0:T(8,128)(2,1)S(1)} %get-tuple-element.47.refs_7_.refs_8_), channel_id=1, source_target_pairs={{0,8},{8,0},{16,24},{24,16},{1,9},{9,1},{17,25},{25,17},{2,10},{10... | collective-permute-start | bytes 786440 | tf_op jit(solution)/shard_map/ppermute | solution.py:407
  17.1 10.7 %collective-permute-start.8 = (bf16[256,512]{1,0:T(8,128)(2,1)S(1)}, bf16[256,512]{1,0:T(8,128)(2,1)S(1)}, u32[]{:S(2)}, u32[]{:S(2)}) collective-permute-start(bf16[256,512]{1,0:T(8,128)(2,1)S(1)} %collective-permute-done.3.refs_9_.refs_10_), channel_id=1, source_target_pairs={{0,8},{8,0},{16,24},{24,16},{1,9},{9,1},{17,25},{25,17},{2,10},{10... | collective-permute-start | bytes 786440 | tf_op jit(solution)/shard_map/ppermute | solution.py:407
  24.5 3.3 %collective-permute-start.5 = (bf16[128,1280]{1,0:T(8,128)(2,1)S(1)}, bf16[128,1280]{1,0:T(8,128)(2,1)S(1)}, u32[]{:S(2)}, u32[]{:S(2)}) collective-permute-start(bf16[128,1280]{1,0:T(8,128)(2,1)S(1)} %collective-permute-done.1.refs_4_.refs_5_), channel_id=1, source_target_pairs={{0,1},{1,0},{2,3},{3,2},{4,5},{5,4},{6,7},{7,6},{8,9},{9,8},{10,11... | collective-permute-start | bytes 983048 | tf_op jit(solution)/shard_map/ppermute | solution.py:407
  24.5 3.3 %collective-permute-start.6 = (bf16[128,1280]{1,0:T(8,128)(2,1)S(1)}, bf16[128,1280]{1,0:T(8,128)(2,1)S(1)}, u32[]{:S(2)}, u32[]{:S(2)}) collective-permute-start(bf16[128,1280]{1,0:T(8,128)(2,1)S(1)} %collective-permute-done.2.refs_5_.refs_6_), channel_id=1, source_target_pairs={{0,1},{1,0},{2,3},{3,2},{4,5},{5,4},{6,7},{7,6},{8,9},{9,8},{10,11... | collective-permute-start | bytes 983048 | tf_op jit(solution)/shard_map/ppermute | solution.py:407
  25.0 2.8 %collective-permute-start.7 = (bf16[128,1280]{1,0:T(8,128)(2,1)S(1)}, bf16[128,1280]{1,0:T(8,128)(2,1)S(1)}, u32[]{:S(2)}, u32[]{:S(2)}) collective-permute-start(bf16[128,1280]{1,0:T(8,128)(2,1)S(1)} %get-tuple-element.51.refs_6_.refs_7_), channel_id=1, source_target_pairs={{0,1},{1,0},{2,3},{3,2},{4,5},{5,4},{6,7},{7,6},{8,9},{9,8},{10,11... | collective-permute-start | bytes 983048 | tf_op jit(solution)/shard_map/ppermute | solution.py:407
  27.8 1.8 %collective-permute-start.9 = (bf16[128,1280]{1,0:T(8,128)(2,1)S(1)}, bf16[128,1280]{1,0:T(8,128)(2,1)S(1)}, u32[]{:S(2)}, u32[]{:S(2)}) collective-permute-start(bf16[128,1280]{1,0:T(8,128)(2,1)S(1)} %collective-permute-done.refs_3_.refs_4_), channel_id=1, source_target_pairs={{0,1},{1,0},{2,3},{3,2},{4,5},{5,4},{6,7},{7,6},{8,9},{9,8},{10,11... | collective-permute-start | bytes 983048 | tf_op jit(solution)/shard_map/ppermute | solution.py:407
  29.5 19.4 %copy-start = (f32[3,1024]{1,0:T(4,128)S(1)}, f32[3,1024]{1,0:T(4,128)}, u32[]{:S(2)}) copy-start(f32[3,1024]{1,0:T(4,128)} %taps_ref.3) | copy-start | bytes 36868
  30.4 8.9 %collective-permute-start.10 = (bf16[64,1024]{1,0:T(8,128)(2,1)S(1)}, bf16[64,1024]{1,0:T(8,128)(2,1)S(1)}, u32[]{:S(2)}, u32[]{:S(2)}) collective-permute-start(bf16[64,1024]{1,0:T(8,128)(2,1)S(1)} %get-tuple-element.61), channel_id=1, source_target_pairs={{0,6},{2,4},{4,2},{6,0},{1,7},{3,5},{5,3},{7,1},{8,14},{10,12},{12... | collective-permute-start | bytes 393224 | tf_op jit(solution)/shard_map/ppermute | solution.py:407
  33.0 7.1 %collective-permute-start.11 = (bf16[64,1024]{1,0:T(8,128)(2,1)S(1)}, bf16[64,1024]{1,0:T(8,128)(2,1)S(1)}, u32[]{:S(2)}, u32[]{:S(2)}) collective-permute-start(bf16[64,1024]{1,0:T(8,128)(2,1)S(1)} %get-tuple-element.62), channel_id=1, source_target_pairs={{0,4},{2,6},{4,0},{6,2},{1,5},{3,7},{5,1},{7,3},{8,12},{10,14},{12... | collective-permute-start | bytes 393224 | tf_op jit(solution)/shard_map/ppermute | solution.py:407
  33.5 6.8 %collective-permute-start.12 = (bf16[64,1024]{1,0:T(8,128)(2,1)S(1)}, bf16[64,1024]{1,0:T(8,128)(2,1)S(1)}, u32[]{:S(2)}, u32[]{:S(2)}) collective-permute-start(bf16[64,1024]{1,0:T(8,128)(2,1)S(1)} %get-tuple-element.63), channel_id=1, source_target_pairs={{0,2},{2,0},{4,6},{6,4},{1,3},{3,1},{5,7},{7,5},{8,10},{10,8},{12,... | collective-permute-start | bytes 393224 | tf_op jit(solution)/shard_map/ppermute | solution.py:407
  34.0 5.3 %collective-permute-start.13 = (bf16[2,512]{1,0:T(2,128)(2,1)S(1)}, bf16[2,512]{1,0:T(2,128)(2,1)S(1)}, u32[]{:S(2)}, u32[]{:S(2)}) collective-permute-start(bf16[2,512]{1,0:T(2,128)(2,1)S(1)} %slice.3), channel_id=1, source_target_pairs={{0,2},{2,4},{4,6},{6,8},{8,10},{10,12},{12,14},{14,16},{16,18},{18... | collective-permute-start | bytes 6152 | tf_op jit(solution)/shard_map/ppermute | solution.py:523
  40.4 6.0 %collective-permute-start.14 = (bf16[16,1536]{1,0:T(8,128)(2,1)S(1)}, bf16[16,1536]{1,0:T(8,128)(2,1)S(1)}, u32[]{:S(2)}, u32[]{:S(2)}) collective-permute-start(bf16[16,1536]{1,0:T(8,128)(2,1)S(1)} %get-tuple-element.73), channel_id=1, source_target_pairs={{0,24},{8,16},{16,8},{24,0},{1,25},{9,17},{17,9},{25,1},{2,26},{10... | collective-permute-start | bytes 147464 | tf_op jit(solution)/shard_map/ppermute | solution.py:407
  43.9 5.0 %collective-permute-start.15 = (bf16[16,1536]{1,0:T(8,128)(2,1)S(1)}, bf16[16,1536]{1,0:T(8,128)(2,1)S(1)}, u32[]{:S(2)}, u32[]{:S(2)}) collective-permute-start(bf16[16,1536]{1,0:T(8,128)(2,1)S(1)} %get-tuple-element.74), channel_id=1, source_target_pairs={{0,16},{8,24},{16,0},{24,8},{1,17},{9,25},{17,1},{25,9},{2,18},{10... | collective-permute-start | bytes 147464 | tf_op jit(solution)/shard_map/ppermute | solution.py:407
  43.9 5.0 %collective-permute-start.16 = (bf16[16,1536]{1,0:T(8,128)(2,1)S(1)}, bf16[16,1536]{1,0:T(8,128)(2,1)S(1)}, u32[]{:S(2)}, u32[]{:S(2)}) collective-permute-start(bf16[16,1536]{1,0:T(8,128)(2,1)S(1)} %get-tuple-element.75), channel_id=1, source_target_pairs={{0,8},{8,0},{16,24},{24,16},{1,9},{9,1},{17,25},{25,17},{2,10},{10... | collective-permute-start | bytes 147464 | tf_op jit(solution)/shard_map/ppermute | solution.py:407

commit v4 on v3

--- a/solution.py
+++ b/solution.py
@@ -484,7 +484,7 @@
         pieces[3] = exchanged(pieces[2], "far", 1)
     gate_rows = jnp.dot(late_tokens, w_gate, preferred_element_type=F32).astype(BF16)
     late = 1 % len(pieces)
-    *chunks[::-1], gate_rows, pieces[late] = lax.optimization_barrier((*chunks[::-1], gate_rows, pieces[late]))
+    pieces[late], *chunks[::-1], gate_rows = lax.optimization_barrier((pieces[late], *chunks[::-1], gate_rows))
     pieces[-1], chunks[-1] = lax.optimization_barrier((pieces[-1], chunks[-1]))
     chunks += [exchanged(chunk, "dp", 1) for chunk in chunks]
 

time: 66.2 us -> 65.7 us (level)
  waiting for transfers between devices: 17.9 us -> 17.1 us
  transfers between devices with their start and end apart: 17 -> 17, of which waited for: 10 -> 11; matrix products, arithmetic and copies ran while one was open for 5% -> 5% of each run, Pallas kernels for 6% -> 6%
where the time goes in v4:
time: 65.7 us; the launch traced here: 65.5 us
  starting transfers between devices  22.3 us (34%)
  waiting for transfers between devices  17.1 us (26%)
  Pallas kernels  12.4 us (19%)
  blocking collectives  10.3 us (16%)
  matrix products  3.23 us (5%)
    ppermute x16, starting transfers between devices, exchanged(): lax.ppermute(value, axis, [(i, i ^ step) for i in range(lax.axis_size(axi...  18.9 us
    ppermute x16, waiting for transfers between devices, exchanged(): lax.ppermute(value, axis, [(i, i ^ step) for i in range(lax.axis_size(axi...  15.8 us
    all_to_all x1, blocking collectives, on_device(): lax.all_to_all(mixed, ('dp', 'far', 'near'), 0, 0, tiled=True)  10.3 us
    pallas_call x1, Pallas kernels, on_device(): pl.pallas_call(out_kernel, in_specs=[ANY] * 4 + [HBM], out_specs=HBM, out...  4.08 us
    ppermute x1, starting transfers between devices, on_device(): lax.ppermute(last_rows, ('far', 'near'), [(i, i + 1) for i in range(count...  3.38 us
    dot_general x1, matrix products, on_device(): jnp.dot(late_tokens, w_gate, preferred_element_type=F32).astype(BF16)  3.23 us
    pallas_call x1, Pallas kernels, on_device(): pl.pallas_call(functools.partial(mix_kernel, near, far, cores, held), in_...  2.51 us
    pallas_call x1, Pallas kernels, on_device(): pl.pallas_call(functools.partial(pack_kernel, near, far), in_specs=[HBM]...  2.16 us
  transfers between devices with their start and end apart: 17, of which 11 were waited for; matrix products, arithmetic and copies ran while one was open for 5% of the time, Pallas kernels for 6%

profile of v4, /device:TPU:0, one launch (start us, length us, event | category | flops | bytes accessed | tf_op | source)
XLA Modules:
  0.0 65.5 jit_solution(16226352143694865007)
XLA Ops:
  0.0 1.0 %weights.1 = bf16[256,512]{1,0:T(8,128)(2,1)S(1)} custom-call(bf16[256,512]{1,0:T(8,128)(2,1)} %value_ref.3, bf16[256,512]{1,0:T(8,128)(2,1)} %noise_ref.3), custom_call_target="tpu_custom_call" | custom-call | bytes 524288 | tf_op jit(solution)/shard_map/weights/pallas_call | solution.py:432
  1.0 4.1 %collective-permute-start.4 = (bf16[256,512]{1,0:T(8,128)(2,1)S(1)}, bf16[256,512]{1,0:T(8,128)(2,1)S(1)}, u32[]{:S(2)}, u32[]{:S(2)}) collective-permute-start(bf16[256,512]{1,0:T(8,128)(2,1)S(1)} %weights.1), channel_id=1, source_target_pairs={{0,16},{8,24},{16,0},{24,8},{1,17},{9,25},{17,1},{25,9},{2,18},{10... | collective-permute-start | bytes 786440 | tf_op jit(solution)/shard_map/ppermute | solution.py:407
  5.1 2.2 %pack.1 = (bf16[256,512]{1,0:T(8,128)(2,1)S(1)}, bf16[128,1280]{1,0:T(8,128)(2,1)S(1)}, bf16[128,1280]{1,0:T(8,128)(2,1)S(1)}, bf16[128,1280]{1,0:T(8,128)(2,1)S(1)}, bf16[128,1280]{1,0:T(8,128)(2,1)S(1)}) custom-call(bf16[128,4096]{1,0:T(8,128)(2,1)} %tokens_ref, s32[128,256]{1,0:T(8,128)} %in_ref.1, s32[32,128]{1,0:T(8,128)} %bitcast.5, ...), custom_call_target="tpu_custom_call" | custom-call | flops 67108864 | bytes 3145728 | tf_op jit(solution)/shard_map/pack/pallas_call | solution.py:444
  7.3 1.6 %collective-permute-start = (bf16[256,512]{1,0:T(8,128)(2,1)S(1)}, bf16[256,512]{1,0:T(8,128)(2,1)S(1)}, u32[]{:S(2)}, u32[]{:S(2)}) collective-permute-start(bf16[256,512]{1,0:T(8,128)(2,1)S(1)} %get-tuple-element.42.refs_7_.refs_8_), channel_id=1, source_target_pairs={{0,8},{8,0},{16,24},{24,16},{1,9},{9,1},{17,25},{25,17},{2,10},{10... | collective-permute-start | bytes 786440 | tf_op jit(solution)/shard_map/ppermute | solution.py:407
  8.9 2.4 %collective-permute-start.1 = (bf16[128,1280]{1,0:T(8,128)(2,1)S(1)}, bf16[128,1280]{1,0:T(8,128)(2,1)S(1)}, u32[]{:S(2)}, u32[]{:S(2)}) collective-permute-start(bf16[128,1280]{1,0:T(8,128)(2,1)S(1)} %get-tuple-element.43), channel_id=1, source_target_pairs={{0,6},{2,4},{4,2},{6,0},{1,7},{3,5},{5,3},{7,1},{8,14},{10,12},{12... | collective-permute-start | bytes 983048 | tf_op jit(solution)/shard_map/ppermute | solution.py:407
  12.4 4.7 %collective-permute-done.4.refs_9_.refs_10_ = bf16[256,512]{1,0:T(8,128)(2,1)S(1)} collective-permute-done((bf16[256,512]{1,0:T(8,128)(2,1)S(1)}, bf16[256,512]{1,0:T(8,128)(2,1)S(1)}, u32[]{:S(2)}, u32[]{:S(2)}) %collective-permute-start.4) | collective-permute-done | bytes 262176 | tf_op jit(solution)/shard_map/ppermute | solution.py:407
  17.1 0.7 %collective-permute-start.8 = (bf16[256,512]{1,0:T(8,128)(2,1)S(1)}, bf16[256,512]{1,0:T(8,128)(2,1)S(1)}, u32[]{:S(2)}, u32[]{:S(2)}) collective-permute-start(bf16[256,512]{1,0:T(8,128)(2,1)S(1)} %collective-permute-done.4.refs_9_.refs_10_), channel_id=1, source_target_pairs={{0,8},{8,0},{16,24},{24,16},{1,9},{9,1},{17,25},{25,17},{2,10},{10... | collective-permute-start | bytes 786440 | tf_op jit(solution)/shard_map/ppermute | solution.py:407
  17.8 3.2 %convolution_convert_fusion.gate_ref = bf16[128,512]{1,0:T(8,128)(2,1)S(1)} fusion(bf16[128,4096]{1,0:T(8,128)(2,1)} %tokens_ref, bf16[4096,512]{1,0:T(8,128)(2,1)} %param.14), kind=kOutput, calls=%fused_computation | convolution fusion | flops 536936448 | bytes 5373952 | tf_op jit(solution)/shard_map/dot_general | solution.py:485
  21.0 4.7 %collective-permute-done.2.refs_4_.refs_5_ = bf16[128,1280]{1,0:T(8,128)(2,1)S(1)} collective-permute-done((bf16[128,1280]{1,0:T(8,128)(2,1)S(1)}, bf16[128,1280]{1,0:T(8,128)(2,1)S(1)}, u32[]{:S(2)}, u32[]{:S(2)}) %collective-permute-start.2) | collective-permute-done | bytes 327712 | tf_op jit(solution)/shard_map/ppermute | solution.py:407
  28.4 1.7 %project.1 = (f32[896,256]{1,0:T(8,128)S(1)}, f32[896,256]{1,0:T(8,128)S(1)}, bf16[896,256]{1,0:T(8,128)(2,1)S(1)}, bf16[896,256]{1,0:T(8,128)(2,1)S(1)}, f32[64,512]{1,0:T(8,128)S(1)}) custom-call(bf16[128,1280]{1,0:T(8,128)(2,1)S(1)} %collective-permute-done.5.refs_0_.refs_1_, bf16[128,1280]{1,0:T(8,128)(2,1)S(1)} %collective-permute-done.6.refs_1_.refs_2_, ...), custom_call_target="tpu_custom_call" | custom-call | flops 704643072 | bytes 5242880 | tf_op jit(solution)/shard_map/project/pallas_call | solution.py:495
  30.1 0.8 %finish.1 = (bf16[64,1024]{1,0:T(8,128)(2,1)S(1)}, bf16[64,1024]{1,0:T(8,128)(2,1)S(1)}, bf16[64,1024]{1,0:T(8,128)(2,1)S(1)}, bf16[64,1024]{1,0:T(8,128)(2,1)S(1)}) custom-call(f32[896,256]{1,0:T(8,128)S(1)} %get-tuple-element.56.mean_ref, f32[896,256]{1,0:T(8,128)S(1)} %get-tuple-element.57.noise_ref, bf16[896,256]{1,0:T(8,128)(2,1)S(1)} %get-tuple-element.58.flip_ref, ...), custom_call_target="tpu_custom_call" | custom-call | flops 369098752 | bytes 3145728 | tf_op jit(solution)/shard_map/finish/pallas_call | solution.py:511
  31.0 1.7 %collective-permute-start.10 = (bf16[64,1024]{1,0:T(8,128)(2,1)S(1)}, bf16[64,1024]{1,0:T(8,128)(2,1)S(1)}, u32[]{:S(2)}, u32[]{:S(2)}) collective-permute-start(bf16[64,1024]{1,0:T(8,128)(2,1)S(1)} %get-tuple-element.61), channel_id=1, source_target_pairs={{0,6},{2,4},{4,2},{6,0},{1,7},{3,5},{5,3},{7,1},{8,14},{10,12},{12... | collective-permute-start | bytes 393224 | tf_op jit(solution)/shard_map/ppermute | solution.py:407
  32.7 1.3 %collective-permute-start.11 = (bf16[64,1024]{1,0:T(8,128)(2,1)S(1)}, bf16[64,1024]{1,0:T(8,128)(2,1)S(1)}, u32[]{:S(2)}, u32[]{:S(2)}) collective-permute-start(bf16[64,1024]{1,0:T(8,128)(2,1)S(1)} %get-tuple-element.62), channel_id=1, source_target_pairs={{0,4},{2,6},{4,0},{6,2},{1,5},{3,7},{5,1},{7,3},{8,12},{10,14},{12... | collective-permute-start | bytes 393224 | tf_op jit(solution)/shard_map/ppermute | solution.py:407
  34.6 3.4 %collective-permute-start.13 = (bf16[2,512]{1,0:T(2,128)(2,1)S(1)}, bf16[2,512]{1,0:T(2,128)(2,1)S(1)}, u32[]{:S(2)}, u32[]{:S(2)}) collective-permute-start(bf16[2,512]{1,0:T(2,128)(2,1)S(1)} %slice.3), channel_id=1, source_target_pairs={{0,2},{2,4},{4,6},{6,8},{8,10},{10,12},{12,14},{14,16},{16,18},{18... | collective-permute-start | bytes 6152 | tf_op jit(solution)/shard_map/ppermute | solution.py:523
  37.9 1.3 %collective-permute-done.13.before_ref = bf16[2,512]{1,0:T(2,128)(2,1)S(1)} collective-permute-done((bf16[2,512]{1,0:T(2,128)(2,1)S(1)}, bf16[2,512]{1,0:T(2,128)(2,1)S(1)}, u32[]{:S(2)}, u32[]{:S(2)}) %collective-permute-start.13) | collective-permute-done | bytes 2080 | tf_op jit(solution)/shard_map/ppermute | solution.py:523
  39.2 1.1 %collective-permute-done.11.refs_1_ = bf16[64,1024]{1,0:T(8,128)(2,1)S(1)} collective-permute-done((bf16[64,1024]{1,0:T(8,128)(2,1)S(1)}, bf16[64,1024]{1,0:T(8,128)(2,1)S(1)}, u32[]{:S(2)}, u32[]{:S(2)}) %collective-permute-start.11) | collective-permute-done | bytes 131104 | tf_op jit(solution)/shard_map/ppermute | solution.py:407
  40.4 2.1 %collective-permute-start.14 = (bf16[16,1536]{1,0:T(8,128)(2,1)S(1)}, bf16[16,1536]{1,0:T(8,128)(2,1)S(1)}, u32[]{:S(2)}, u32[]{:S(2)}) collective-permute-start(bf16[16,1536]{1,0:T(8,128)(2,1)S(1)} %get-tuple-element.73), channel_id=1, source_target_pairs={{0,24},{8,16},{16,8},{24,0},{1,25},{9,17},{17,9},{25,1},{2,26},{10... | collective-permute-start | bytes 147464 | tf_op jit(solution)/shard_map/ppermute | solution.py:407
  42.5 1.4 %collective-permute-start.15 = (bf16[16,1536]{1,0:T(8,128)(2,1)S(1)}, bf16[16,1536]{1,0:T(8,128)(2,1)S(1)}, u32[]{:S(2)}, u32[]{:S(2)}) collective-permute-start(bf16[16,1536]{1,0:T(8,128)(2,1)S(1)} %get-tuple-element.74), channel_id=1, source_target_pairs={{0,16},{8,24},{16,0},{24,8},{1,17},{9,25},{17,1},{25,9},{2,18},{10... | collective-permute-start | bytes 147464 | tf_op jit(solution)/shard_map/ppermute | solution.py:407
  43.9 1.0 %collective-permute-start.16 = (bf16[16,1536]{1,0:T(8,128)(2,1)S(1)}, bf16[16,1536]{1,0:T(8,128)(2,1)S(1)}, u32[]{:S(2)}, u32[]{:S(2)}) collective-permute-start(bf16[16,1536]{1,0:T(8,128)(2,1)S(1)} %get-tuple-element.75), channel_id=1, source_target_pairs={{0,8},{8,0},{16,24},{24,16},{1,9},{9,1},{17,25},{25,17},{2,10},{10... | collective-permute-start | bytes 147464 | tf_op jit(solution)/shard_map/ppermute | solution.py:407
  44.9 2.1 %collective-permute-done.14.refs_0_ = bf16[16,1536]{1,0:T(8,128)(2,1)S(1)} collective-permute-done((bf16[16,1536]{1,0:T(8,128)(2,1)S(1)}, bf16[16,1536]{1,0:T(8,128)(2,1)S(1)}, u32[]{:S(2)}, u32[]{:S(2)}) %collective-permute-start.14) | collective-permute-done | bytes 49184 | tf_op jit(solution)/shard_map/ppermute | solution.py:407
  46.9 1.4 %collective-permute-done.15.refs_1_ = bf16[16,1536]{1,0:T(8,128)(2,1)S(1)} collective-permute-done((bf16[16,1536]{1,0:T(8,128)(2,1)S(1)}, bf16[16,1536]{1,0:T(8,128)(2,1)S(1)}, u32[]{:S(2)}, u32[]{:S(2)}) %collective-permute-start.15) | collective-permute-done | bytes 49184 | tf_op jit(solution)/shard_map/ppermute | solution.py:407
  48.6 2.5 %mix.1 = bf16[32,16,128]{2,1,0:T(8,128)(2,1)S(1)} custom-call(f32[3,1024]{1,0:T(4,128)S(1)} %copy-done, bf16[16,1536]{1,0:T(8,128)(2,1)S(1)} %collective-permute-done.14.refs_0_, bf16[16,1536]{1,0:T(8,128)(2,1)S(1)} %collective-permute-done.15.refs_1_, bf16[16,1536]{1,0:T(8,128)(2,1)S(1)} %collective-permute-done.16.refs_2_, ...), custom_call_target="tpu_custom_call" | custom-call | flops 536870912 | bytes 2097152 | tf_op jit(solution)/shard_map/mix/pallas_call | solution.py:548
  51.1 10.3 %all_to_all.5 = bf16[32,16,128]{2,1,0:T(8,128)(2,1)S(1)} all-to-all(bf16[32,16,128]{2,1,0:T(8,128)(2,1)S(1)} %mix.1), channel_id=1, replica_groups=mesh['far'=4,'near'=4,'dp'=2] {'dp','far','near'}, dimensions={0} | all-to-all | bytes 262144 | tf_op jit(solution)/shard_map/all_to_all | solution.py:565
  61.4 4.1 %project_out.1 = bf16[128,4096]{1,0:T(8,128)(2,1)} custom-call(bf16[128,512]{1,0:T(8,128)(2,1)S(1)} %convolution_convert_fusion.gate_ref, bf16[2,512]{1,0:T(2,128)(2,1)S(1)} %collective-permute-done.13.before_ref, f32[3,1024]{1,0:T(4,128)S(1)} %copy-done, bf16[512,128]{1,0:T(8,128)(2,1)S(1)} %bitcast.4, bf16[512,4096]{1,0:T(8,128)(2,1)} %source_ref.1), custom_call_target="tpu_custom_call" | custom-call | flops 536870912 | bytes 5242880 | tf_op jit(solution)/shard_map/project_out/pallas_call | solution.py:567
  (22 shorter events, 4.5 us)
Async XLA Ops:
  1.0 16.1 %collective-permute-start.4 = (bf16[256,512]{1,0:T(8,128)(2,1)S(1)}, bf16[256,512]{1,0:T(8,128)(2,1)S(1)}, u32[]{:S(2)}, u32[]{:S(2)}) collective-permute-start(bf16[256,512]{1,0:T(8,128)(2,1)S(1)} %weights.1), channel_id=1, source_target_pairs={{0,16},{8,24},{16,0},{24,8},{1,17},{9,25},{17,1},{25,9},{2,18},{10... | collective-permute-start | bytes 786440 | tf_op jit(solution)/shard_map/ppermute | solution.py:407
  7.3 13.8 %collective-permute-start = (bf16[256,512]{1,0:T(8,128)(2,1)S(1)}, bf16[256,512]{1,0:T(8,128)(2,1)S(1)}, u32[]{:S(2)}, u32[]{:S(2)}) collective-permute-start(bf16[256,512]{1,0:T(8,128)(2,1)S(1)} %get-tuple-element.42.refs_7_.refs_8_), channel_id=1, source_target_pairs={{0,8},{8,0},{16,24},{24,16},{1,9},{9,1},{17,25},{25,17},{2,10},{10... | collective-permute-start | bytes 786440 | tf_op jit(solution)/shard_map/ppermute | solution.py:407
  8.9 12.1 %collective-permute-start.1 = (bf16[128,1280]{1,0:T(8,128)(2,1)S(1)}, bf16[128,1280]{1,0:T(8,128)(2,1)S(1)}, u32[]{:S(2)}, u32[]{:S(2)}) collective-permute-start(bf16[128,1280]{1,0:T(8,128)(2,1)S(1)} %get-tuple-element.43), channel_id=1, source_target_pairs={{0,6},{2,4},{4,2},{6,0},{1,7},{3,5},{5,3},{7,1},{8,14},{10,12},{12... | collective-permute-start | bytes 983048 | tf_op jit(solution)/shard_map/ppermute | solution.py:407
  11.4 14.4 %collective-permute-start.2 = (bf16[128,1280]{1,0:T(8,128)(2,1)S(1)}, bf16[128,1280]{1,0:T(8,128)(2,1)S(1)}, u32[]{:S(2)}, u32[]{:S(2)}) collective-permute-start(bf16[128,1280]{1,0:T(8,128)(2,1)S(1)} %get-tuple-element.44), channel_id=1, source_target_pairs={{0,4},{2,6},{4,0},{6,2},{1,5},{3,7},{5,1},{7,3},{8,12},{10,14},{12... | collective-permute-start | bytes 983048 | tf_op jit(solution)/shard_map/ppermute | solution.py:407
  11.9 14.0 %collective-permute-start.3 = (bf16[128,1280]{1,0:T(8,128)(2,1)S(1)}, bf16[128,1280]{1,0:T(8,128)(2,1)S(1)}, u32[]{:S(2)}, u32[]{:S(2)}) collective-permute-start(bf16[128,1280]{1,0:T(8,128)(2,1)S(1)} %get-tuple-element.45), channel_id=1, source_target_pairs={{0,2},{2,0},{4,6},{6,4},{1,3},{3,1},{5,7},{7,5},{8,10},{10,8},{12,... | collective-permute-start | bytes 983048 | tf_op jit(solution)/shard_map/ppermute | solution.py:407
  17.1 9.2 %collective-permute-start.8 = (bf16[256,512]{1,0:T(8,128)(2,1)S(1)}, bf16[256,512]{1,0:T(8,128)(2,1)S(1)}, u32[]{:S(2)}, u32[]{:S(2)}) collective-permute-start(bf16[256,512]{1,0:T(8,128)(2,1)S(1)} %collective-permute-done.4.refs_9_.refs_10_), channel_id=1, source_target_pairs={{0,8},{8,0},{16,24},{24,16},{1,9},{9,1},{17,25},{25,17},{2,10},{10... | collective-permute-start | bytes 786440 | tf_op jit(solution)/shard_map/ppermute | solution.py:407
  25.8 1.6 %collective-permute-start.5 = (bf16[128,1280]{1,0:T(8,128)(2,1)S(1)}, bf16[128,1280]{1,0:T(8,128)(2,1)S(1)}, u32[]{:S(2)}, u32[]{:S(2)}) collective-permute-start(bf16[128,1280]{1,0:T(8,128)(2,1)S(1)} %collective-permute-done.2.refs_4_.refs_5_), channel_id=1, source_target_pairs={{0,1},{1,0},{2,3},{3,2},{4,5},{5,4},{6,7},{7,6},{8,9},{9,8},{10,11... | collective-permute-start | bytes 983048 | tf_op jit(solution)/shard_map/ppermute | solution.py:407
  25.8 2.1 %collective-permute-start.6 = (bf16[128,1280]{1,0:T(8,128)(2,1)S(1)}, bf16[128,1280]{1,0:T(8,128)(2,1)S(1)}, u32[]{:S(2)}, u32[]{:S(2)}) collective-permute-start(bf16[128,1280]{1,0:T(8,128)(2,1)S(1)} %collective-permute-done.3.refs_5_.refs_6_), channel_id=1, source_target_pairs={{0,1},{1,0},{2,3},{3,2},{4,5},{5,4},{6,7},{7,6},{8,9},{9,8},{10,11... | collective-permute-start | bytes 983048 | tf_op jit(solution)/shard_map/ppermute | solution.py:407
  26.3 2.1 %collective-permute-start.7 = (bf16[128,1280]{1,0:T(8,128)(2,1)S(1)}, bf16[128,1280]{1,0:T(8,128)(2,1)S(1)}, u32[]{:S(2)}, u32[]{:S(2)}) collective-permute-start(bf16[128,1280]{1,0:T(8,128)(2,1)S(1)} %get-tuple-element.51.refs_6_.refs_7_), channel_id=1, source_target_pairs={{0,1},{1,0},{2,3},{3,2},{4,5},{5,4},{6,7},{7,6},{8,9},{9,8},{10,11... | collective-permute-start | bytes 983048 | tf_op jit(solution)/shard_map/ppermute | solution.py:407
  26.3 3.8 %collective-permute-start.9 = (bf16[128,1280]{1,0:T(8,128)(2,1)S(1)}, bf16[128,1280]{1,0:T(8,128)(2,1)S(1)}, u32[]{:S(2)}, u32[]{:S(2)}) collective-permute-start(bf16[128,1280]{1,0:T(8,128)(2,1)S(1)} %collective-permute-done.1.refs_3_.refs_4_), channel_id=1, source_target_pairs={{0,1},{1,0},{2,3},{3,2},{4,5},{5,4},{6,7},{7,6},{8,9},{9,8},{10,11... | collective-permute-start | bytes 983048 | tf_op jit(solution)/shard_map/ppermute | solution.py:407
  30.1 18.4 %copy-start = (f32[3,1024]{1,0:T(4,128)S(1)}, f32[3,1024]{1,0:T(4,128)}, u32[]{:S(2)}) copy-start(f32[3,1024]{1,0:T(4,128)} %taps_ref.3) | copy-start | bytes 36868
  31.0 8.2 %collective-permute-start.10 = (bf16[64,1024]{1,0:T(8,128)(2,1)S(1)}, bf16[64,1024]{1,0:T(8,128)(2,1)S(1)}, u32[]{:S(2)}, u32[]{:S(2)}) collective-permute-start(bf16[64,1024]{1,0:T(8,128)(2,1)S(1)} %get-tuple-element.61), channel_id=1, source_target_pairs={{0,6},{2,4},{4,2},{6,0},{1,7},{3,5},{5,3},{7,1},{8,14},{10,12},{12... | collective-permute-start | bytes 393224 | tf_op jit(solution)/shard_map/ppermute | solution.py:407
  32.7 7.6 %collective-permute-start.11 = (bf16[64,1024]{1,0:T(8,128)(2,1)S(1)}, bf16[64,1024]{1,0:T(8,128)(2,1)S(1)}, u32[]{:S(2)}, u32[]{:S(2)}) collective-permute-start(bf16[64,1024]{1,0:T(8,128)(2,1)S(1)} %get-tuple-element.62), channel_id=1, source_target_pairs={{0,4},{2,6},{4,0},{6,2},{1,5},{3,7},{5,1},{7,3},{8,12},{10,14},{12... | collective-permute-start | bytes 393224 | tf_op jit(solution)/shard_map/ppermute | solution.py:407
  34.0 6.3 %collective-permute-start.12 = (bf16[64,1024]{1,0:T(8,128)(2,1)S(1)}, bf16[64,1024]{1,0:T(8,128)(2,1)S(1)}, u32[]{:S(2)}, u32[]{:S(2)}) collective-permute-start(bf16[64,1024]{1,0:T(8,128)(2,1)S(1)} %get-tuple-element.63), channel_id=1, source_target_pairs={{0,2},{2,0},{4,6},{6,4},{1,3},{3,1},{5,7},{7,5},{8,10},{10,8},{12,... | collective-permute-start | bytes 393224 | tf_op jit(solution)/shard_map/ppermute | solution.py:407
  34.6 4.7 %collective-permute-start.13 = (bf16[2,512]{1,0:T(2,128)(2,1)S(1)}, bf16[2,512]{1,0:T(2,128)(2,1)S(1)}, u32[]{:S(2)}, u32[]{:S(2)}) collective-permute-start(bf16[2,512]{1,0:T(2,128)(2,1)S(1)} %slice.3), channel_id=1, source_target_pairs={{0,2},{2,4},{4,6},{6,8},{8,10},{10,12},{12,14},{14,16},{16,18},{18... | collective-permute-start | bytes 6152 | tf_op jit(solution)/shard_map/ppermute | solution.py:523
  40.4 6.5 %collective-permute-start.14 = (bf16[16,1536]{1,0:T(8,128)(2,1)S(1)}, bf16[16,1536]{1,0:T(8,128)(2,1)S(1)}, u32[]{:S(2)}, u32[]{:S(2)}) collective-permute-start(bf16[16,1536]{1,0:T(8,128)(2,1)S(1)} %get-tuple-element.73), channel_id=1, source_target_pairs={{0,24},{8,16},{16,8},{24,0},{1,25},{9,17},{17,9},{25,1},{2,26},{10... | collective-permute-start | bytes 147464 | tf_op jit(solution)/shard_map/ppermute | solution.py:407
  42.5 5.9 %collective-permute-start.15 = (bf16[16,1536]{1,0:T(8,128)(2,1)S(1)}, bf16[16,1536]{1,0:T(8,128)(2,1)S(1)}, u32[]{:S(2)}, u32[]{:S(2)}) collective-permute-start(bf16[16,1536]{1,0:T(8,128)(2,1)S(1)} %get-tuple-element.74), channel_id=1, source_target_pairs={{0,16},{8,24},{16,0},{24,8},{1,17},{9,25},{17,1},{25,9},{2,18},{10... | collective-permute-start | bytes 147464 | tf_op jit(solution)/shard_map/ppermute | solution.py:407
  43.9 4.6 %collective-permute-start.16 = (bf16[16,1536]{1,0:T(8,128)(2,1)S(1)}, bf16[16,1536]{1,0:T(8,128)(2,1)S(1)}, u32[]{:S(2)}, u32[]{:S(2)}) collective-permute-start(bf16[16,1536]{1,0:T(8,128)(2,1)S(1)} %get-tuple-element.75), channel_id=1, source_target_pairs={{0,8},{8,0},{16,24},{24,16},{1,9},{9,1},{17,25},{25,17},{2,10},{10... | collective-permute-start | bytes 147464 | tf_op jit(solution)/shard_map/ppermute | solution.py:407

commit v5 on v4

--- a/solution.py
+++ b/solution.py
@@ -484,7 +484,9 @@
         pieces[3] = exchanged(pieces[2], "far", 1)
     gate_rows = jnp.dot(late_tokens, w_gate, preferred_element_type=F32).astype(BF16)
     late = 1 % len(pieces)
-    pieces[late], *chunks[::-1], gate_rows = lax.optimization_barrier((pieces[late], *chunks[::-1], gate_rows))
+    pieces[late], chunks[0], gate_rows = lax.optimization_barrier((pieces[late], chunks[0], gate_rows))
+    for step in range(1, near):
+        chunks[step], _ = lax.optimization_barrier((chunks[step], gate_rows))
     pieces[-1], chunks[-1] = lax.optimization_barrier((pieces[-1], chunks[-1]))
     chunks += [exchanged(chunk, "dp", 1) for chunk in chunks]
 

time: 65.7 us -> 65 us (0.989)
  transfers between devices with their start and end apart: 17 -> 17, of which waited for: 11 -> 9; matrix products, arithmetic and copies ran while one was open for 5% -> 5% of each run, Pallas kernels for 6% -> 6%
where the time goes in v5:
time: 65 us; the launch traced here: 64.8 us
  starting transfers between devices  21.9 us (34%)
  waiting for transfers between devices  17.2 us (26%)
  Pallas kernels  12.4 us (19%)
  blocking collectives  9.89 us (15%)
  matrix products  3.23 us (5%)
    ppermute x16, starting transfers between devices, exchanged(): lax.ppermute(value, axis, [(i, i ^ step) for i in range(lax.axis_size(axi...  18.6 us
    ppermute x16, waiting for transfers between devices, exchanged(): lax.ppermute(value, axis, [(i, i ^ step) for i in range(lax.axis_size(axi...  15.9 us
    all_to_all x1, blocking collectives, on_device(): lax.all_to_all(mixed, ('dp', 'far', 'near'), 0, 0, tiled=True)  9.89 us
    pallas_call x1, Pallas kernels, on_device(): pl.pallas_call(out_kernel, in_specs=[ANY] * 4 + [HBM], out_specs=HBM, out...  4.09 us
    ppermute x1, starting transfers between devices, on_device(): lax.ppermute(last_rows, ('far', 'near'), [(i, i + 1) for i in range(count...  3.38 us
    dot_general x1, matrix products, on_device(): jnp.dot(late_tokens, w_gate, preferred_element_type=F32).astype(BF16)  3.23 us
    pallas_call x1, Pallas kernels, on_device(): pl.pallas_call(functools.partial(mix_kernel, near, far, cores, held), in_...  2.52 us
    pallas_call x1, Pallas kernels, on_device(): pl.pallas_call(functools.partial(pack_kernel, near, far), in_specs=[HBM]...  2.16 us
  transfers between devices with their start and end apart: 17, of which 9 were waited for; matrix products, arithmetic and copies ran while one was open for 5% of the time, Pallas kernels for 6%

profile of v5, /device:TPU:0, one launch (start us, length us, event | category | flops | bytes accessed | tf_op | source)
XLA Modules:
  0.0 64.8 jit_solution(8001968315773911598)
XLA Ops:
  0.0 1.0 %weights.1 = bf16[256,512]{1,0:T(8,128)(2,1)S(1)} custom-call(bf16[256,512]{1,0:T(8,128)(2,1)} %value_ref.3, bf16[256,512]{1,0:T(8,128)(2,1)} %noise_ref.3), custom_call_target="tpu_custom_call" | custom-call | bytes 524288 | tf_op jit(solution)/shard_map/weights/pallas_call | solution.py:432
  1.0 4.1 %collective-permute-start.1 = (bf16[256,512]{1,0:T(8,128)(2,1)S(1)}, bf16[256,512]{1,0:T(8,128)(2,1)S(1)}, u32[]{:S(2)}, u32[]{:S(2)}) collective-permute-start(bf16[256,512]{1,0:T(8,128)(2,1)S(1)} %weights.1), channel_id=1, source_target_pairs={{0,16},{8,24},{16,0},{24,8},{1,17},{9,25},{17,1},{25,9},{2,18},{10... | collective-permute-start | bytes 786440 | tf_op jit(solution)/shard_map/ppermute | solution.py:407
  5.1 2.2 %pack.1 = (bf16[256,512]{1,0:T(8,128)(2,1)S(1)}, bf16[128,1280]{1,0:T(8,128)(2,1)S(1)}, bf16[128,1280]{1,0:T(8,128)(2,1)S(1)}, bf16[128,1280]{1,0:T(8,128)(2,1)S(1)}, bf16[128,1280]{1,0:T(8,128)(2,1)S(1)}) custom-call(bf16[128,4096]{1,0:T(8,128)(2,1)} %tokens_ref, s32[128,256]{1,0:T(8,128)} %in_ref.1, s32[32,128]{1,0:T(8,128)} %bitcast.5, ...), custom_call_target="tpu_custom_call" | custom-call | flops 67108864 | bytes 3145728 | tf_op jit(solution)/shard_map/pack/pallas_call | solution.py:444
  7.3 1.6 %collective-permute-start = (bf16[256,512]{1,0:T(8,128)(2,1)S(1)}, bf16[256,512]{1,0:T(8,128)(2,1)S(1)}, u32[]{:S(2)}, u32[]{:S(2)}) collective-permute-start(bf16[256,512]{1,0:T(8,128)(2,1)S(1)} %get-tuple-element.42.refs_7_.refs_8_), channel_id=1, source_target_pairs={{0,8},{8,0},{16,24},{24,16},{1,9},{9,1},{17,25},{25,17},{2,10},{10... | collective-permute-start | bytes 786440 | tf_op jit(solution)/shard_map/ppermute | solution.py:407
  8.9 2.4 %collective-permute-start.8 = (bf16[128,1280]{1,0:T(8,128)(2,1)S(1)}, bf16[128,1280]{1,0:T(8,128)(2,1)S(1)}, u32[]{:S(2)}, u32[]{:S(2)}) collective-permute-start(bf16[128,1280]{1,0:T(8,128)(2,1)S(1)} %get-tuple-element.52), channel_id=1, source_target_pairs={{0,6},{2,4},{4,2},{6,0},{1,7},{3,5},{5,3},{7,1},{8,14},{10,12},{12... | collective-permute-start | bytes 983048 | tf_op jit(solution)/shard_map/ppermute | solution.py:407
  12.4 4.7 %collective-permute-done.1.refs_9_.refs_10_ = bf16[256,512]{1,0:T(8,128)(2,1)S(1)} collective-permute-done((bf16[256,512]{1,0:T(8,128)(2,1)S(1)}, bf16[256,512]{1,0:T(8,128)(2,1)S(1)}, u32[]{:S(2)}, u32[]{:S(2)}) %collective-permute-start.1) | collective-permute-done | bytes 262176 | tf_op jit(solution)/shard_map/ppermute | solution.py:407
  17.8 3.2 %convolution_convert_fusion.gate_ref = bf16[128,512]{1,0:T(8,128)(2,1)S(1)} fusion(bf16[128,4096]{1,0:T(8,128)(2,1)} %tokens_ref, bf16[4096,512]{1,0:T(8,128)(2,1)} %param.14), kind=kOutput, calls=%fused_computation | convolution fusion | flops 536936448 | bytes 5373952 | tf_op jit(solution)/shard_map/dot_general | solution.py:485
  21.1 4.7 %collective-permute-done.4.refs_5_.refs_6_ = bf16[128,1280]{1,0:T(8,128)(2,1)S(1)} collective-permute-done((bf16[128,1280]{1,0:T(8,128)(2,1)S(1)}, bf16[128,1280]{1,0:T(8,128)(2,1)S(1)}, u32[]{:S(2)}, u32[]{:S(2)}) %collective-permute-start.4) | collective-permute-done | bytes 327712 | tf_op jit(solution)/shard_map/ppermute | solution.py:407
  26.4 1.0 %collective-permute-done.5.refs_1_.refs_2_ = bf16[128,1280]{1,0:T(8,128)(2,1)S(1)} collective-permute-done((bf16[128,1280]{1,0:T(8,128)(2,1)S(1)}, bf16[128,1280]{1,0:T(8,128)(2,1)S(1)}, u32[]{:S(2)}, u32[]{:S(2)}) %collective-permute-start.5) | collective-permute-done | bytes 327712 | tf_op jit(solution)/shard_map/ppermute | solution.py:407
  27.9 1.7 %project.1 = (f32[896,256]{1,0:T(8,128)S(1)}, f32[896,256]{1,0:T(8,128)S(1)}, bf16[896,256]{1,0:T(8,128)(2,1)S(1)}, bf16[896,256]{1,0:T(8,128)(2,1)S(1)}, f32[64,512]{1,0:T(8,128)S(1)}) custom-call(bf16[128,1280]{1,0:T(8,128)(2,1)S(1)} %collective-permute-done.3.refs_0_.refs_1_, bf16[128,1280]{1,0:T(8,128)(2,1)S(1)} %collective-permute-done.5.refs_1_.refs_2_, ...), custom_call_target="tpu_custom_call" | custom-call | flops 704643072 | bytes 5242880 | tf_op jit(solution)/shard_map/project/pallas_call | solution.py:497
  29.7 0.8 %finish.1 = (bf16[64,1024]{1,0:T(8,128)(2,1)S(1)}, bf16[64,1024]{1,0:T(8,128)(2,1)S(1)}, bf16[64,1024]{1,0:T(8,128)(2,1)S(1)}, bf16[64,1024]{1,0:T(8,128)(2,1)S(1)}) custom-call(f32[896,256]{1,0:T(8,128)S(1)} %get-tuple-element.56.mean_ref, f32[896,256]{1,0:T(8,128)S(1)} %get-tuple-element.57.noise_ref, bf16[896,256]{1,0:T(8,128)(2,1)S(1)} %get-tuple-element.58.flip_ref, ...), custom_call_target="tpu_custom_call" | custom-call | flops 369098752 | bytes 3145728 | tf_op jit(solution)/shard_map/finish/pallas_call | solution.py:513
  30.5 1.9 %collective-permute-start.10 = (bf16[64,1024]{1,0:T(8,128)(2,1)S(1)}, bf16[64,1024]{1,0:T(8,128)(2,1)S(1)}, u32[]{:S(2)}, u32[]{:S(2)}) collective-permute-start(bf16[64,1024]{1,0:T(8,128)(2,1)S(1)} %get-tuple-element.61), channel_id=1, source_target_pairs={{0,6},{2,4},{4,2},{6,0},{1,7},{3,5},{5,3},{7,1},{8,14},{10,12},{12... | collective-permute-start | bytes 393224 | tf_op jit(solution)/shard_map/ppermute | solution.py:407
  32.5 1.1 %collective-permute-start.11 = (bf16[64,1024]{1,0:T(8,128)(2,1)S(1)}, bf16[64,1024]{1,0:T(8,128)(2,1)S(1)}, u32[]{:S(2)}, u32[]{:S(2)}) collective-permute-start(bf16[64,1024]{1,0:T(8,128)(2,1)S(1)} %get-tuple-element.62), channel_id=1, source_target_pairs={{0,4},{2,6},{4,0},{6,2},{1,5},{3,7},{5,1},{7,3},{8,12},{10,14},{12... | collective-permute-start | bytes 393224 | tf_op jit(solution)/shard_map/ppermute | solution.py:407
  34.1 3.4 %collective-permute-start.13 = (bf16[2,512]{1,0:T(2,128)(2,1)S(1)}, bf16[2,512]{1,0:T(2,128)(2,1)S(1)}, u32[]{:S(2)}, u32[]{:S(2)}) collective-permute-start(bf16[2,512]{1,0:T(2,128)(2,1)S(1)} %slice.3), channel_id=1, source_target_pairs={{0,2},{2,4},{4,6},{6,8},{8,10},{10,12},{12,14},{14,16},{16,18},{18... | collective-permute-start | bytes 6152 | tf_op jit(solution)/shard_map/ppermute | solution.py:525
  37.5 1.3 %collective-permute-done.13.before_ref = bf16[2,512]{1,0:T(2,128)(2,1)S(1)} collective-permute-done((bf16[2,512]{1,0:T(2,128)(2,1)S(1)}, bf16[2,512]{1,0:T(2,128)(2,1)S(1)}, u32[]{:S(2)}, u32[]{:S(2)}) %collective-permute-start.13) | collective-permute-done | bytes 2080 | tf_op jit(solution)/shard_map/ppermute | solution.py:525
  38.8 1.1 %collective-permute-done.11.refs_1_ = bf16[64,1024]{1,0:T(8,128)(2,1)S(1)} collective-permute-done((bf16[64,1024]{1,0:T(8,128)(2,1)S(1)}, bf16[64,1024]{1,0:T(8,128)(2,1)S(1)}, u32[]{:S(2)}, u32[]{:S(2)}) %collective-permute-start.11) | collective-permute-done | bytes 131104 | tf_op jit(solution)/shard_map/ppermute | solution.py:407
  40.0 2.5 %collective-permute-start.14 = (bf16[16,1536]{1,0:T(8,128)(2,1)S(1)}, bf16[16,1536]{1,0:T(8,128)(2,1)S(1)}, u32[]{:S(2)}, u32[]{:S(2)}) collective-permute-start(bf16[16,1536]{1,0:T(8,128)(2,1)S(1)} %get-tuple-element.73), channel_id=1, source_target_pairs={{0,24},{8,16},{16,8},{24,0},{1,25},{9,17},{17,9},{25,1},{2,26},{10... | collective-permute-start | bytes 147464 | tf_op jit(solution)/shard_map/ppermute | solution.py:407
  42.5 1.0 %collective-permute-start.15 = (bf16[16,1536]{1,0:T(8,128)(2,1)S(1)}, bf16[16,1536]{1,0:T(8,128)(2,1)S(1)}, u32[]{:S(2)}, u32[]{:S(2)}) collective-permute-start(bf16[16,1536]{1,0:T(8,128)(2,1)S(1)} %get-tuple-element.74), channel_id=1, source_target_pairs={{0,16},{8,24},{16,0},{24,8},{1,17},{9,25},{17,1},{25,9},{2,18},{10... | collective-permute-start | bytes 147464 | tf_op jit(solution)/shard_map/ppermute | solution.py:407
  43.5 1.0 %collective-permute-start.16 = (bf16[16,1536]{1,0:T(8,128)(2,1)S(1)}, bf16[16,1536]{1,0:T(8,128)(2,1)S(1)}, u32[]{:S(2)}, u32[]{:S(2)}) collective-permute-start(bf16[16,1536]{1,0:T(8,128)(2,1)S(1)} %get-tuple-element.75), channel_id=1, source_target_pairs={{0,8},{8,0},{16,24},{24,16},{1,9},{9,1},{17,25},{25,17},{2,10},{10... | collective-permute-start | bytes 147464 | tf_op jit(solution)/shard_map/ppermute | solution.py:407
  44.4 1.8 %collective-permute-done.14.refs_0_ = bf16[16,1536]{1,0:T(8,128)(2,1)S(1)} collective-permute-done((bf16[16,1536]{1,0:T(8,128)(2,1)S(1)}, bf16[16,1536]{1,0:T(8,128)(2,1)S(1)}, u32[]{:S(2)}, u32[]{:S(2)}) %collective-permute-start.14) | collective-permute-done | bytes 49184 | tf_op jit(solution)/shard_map/ppermute | solution.py:407
  46.2 1.9 %collective-permute-done.15.refs_1_ = bf16[16,1536]{1,0:T(8,128)(2,1)S(1)} collective-permute-done((bf16[16,1536]{1,0:T(8,128)(2,1)S(1)}, bf16[16,1536]{1,0:T(8,128)(2,1)S(1)}, u32[]{:S(2)}, u32[]{:S(2)}) %collective-permute-start.15) | collective-permute-done | bytes 49184 | tf_op jit(solution)/shard_map/ppermute | solution.py:407
  48.3 2.5 %mix.1 = bf16[32,16,128]{2,1,0:T(8,128)(2,1)S(1)} custom-call(f32[3,1024]{1,0:T(4,128)S(1)} %copy-done, bf16[16,1536]{1,0:T(8,128)(2,1)S(1)} %collective-permute-done.14.refs_0_, bf16[16,1536]{1,0:T(8,128)(2,1)S(1)} %collective-permute-done.15.refs_1_, bf16[16,1536]{1,0:T(8,128)(2,1)S(1)} %collective-permute-done.16.refs_2_, ...), custom_call_target="tpu_custom_call" | custom-call | flops 536870912 | bytes 2097152 | tf_op jit(solution)/shard_map/mix/pallas_call | solution.py:550
  50.9 9.9 %all_to_all.5 = bf16[32,16,128]{2,1,0:T(8,128)(2,1)S(1)} all-to-all(bf16[32,16,128]{2,1,0:T(8,128)(2,1)S(1)} %mix.1), channel_id=1, replica_groups=mesh['far'=4,'near'=4,'dp'=2] {'dp','far','near'}, dimensions={0} | all-to-all | bytes 262144 | tf_op jit(solution)/shard_map/all_to_all | solution.py:567
  60.7 4.1 %project_out.1 = bf16[128,4096]{1,0:T(8,128)(2,1)} custom-call(bf16[128,512]{1,0:T(8,128)(2,1)S(1)} %convolution_convert_fusion.gate_ref, bf16[2,512]{1,0:T(2,128)(2,1)S(1)} %collective-permute-done.13.before_ref, f32[3,1024]{1,0:T(4,128)S(1)} %copy-done, bf16[512,128]{1,0:T(8,128)(2,1)S(1)} %bitcast.4, bf16[512,4096]{1,0:T(8,128)(2,1)} %source_ref.1), custom_call_target="tpu_custom_call" | custom-call | flops 536870912 | bytes 5242880 | tf_op jit(solution)/shard_map/project_out/pallas_call | solution.py:569
  (22 shorter events, 3.7 us)
Async XLA Ops:
  1.0 16.1 %collective-permute-start.1 = (bf16[256,512]{1,0:T(8,128)(2,1)S(1)}, bf16[256,512]{1,0:T(8,128)(2,1)S(1)}, u32[]{:S(2)}, u32[]{:S(2)}) collective-permute-start(bf16[256,512]{1,0:T(8,128)(2,1)S(1)} %weights.1), channel_id=1, source_target_pairs={{0,16},{8,24},{16,0},{24,8},{1,17},{9,25},{17,1},{25,9},{2,18},{10... | collective-permute-start | bytes 786440 | tf_op jit(solution)/shard_map/ppermute | solution.py:407
  7.3 13.8 %collective-permute-start = (bf16[256,512]{1,0:T(8,128)(2,1)S(1)}, bf16[256,512]{1,0:T(8,128)(2,1)S(1)}, u32[]{:S(2)}, u32[]{:S(2)}) collective-permute-start(bf16[256,512]{1,0:T(8,128)(2,1)S(1)} %get-tuple-element.42.refs_7_.refs_8_), channel_id=1, source_target_pairs={{0,8},{8,0},{16,24},{24,16},{1,9},{9,1},{17,25},{25,17},{2,10},{10... | collective-permute-start | bytes 786440 | tf_op jit(solution)/shard_map/ppermute | solution.py:407
  8.9 17.4 %collective-permute-start.8 = (bf16[128,1280]{1,0:T(8,128)(2,1)S(1)}, bf16[128,1280]{1,0:T(8,128)(2,1)S(1)}, u32[]{:S(2)}, u32[]{:S(2)}) collective-permute-start(bf16[128,1280]{1,0:T(8,128)(2,1)S(1)} %get-tuple-element.52), channel_id=1, source_target_pairs={{0,6},{2,4},{4,2},{6,0},{1,7},{3,5},{5,3},{7,1},{8,14},{10,12},{12... | collective-permute-start | bytes 983048 | tf_op jit(solution)/shard_map/ppermute | solution.py:407
  11.4 14.5 %collective-permute-start.4 = (bf16[128,1280]{1,0:T(8,128)(2,1)S(1)}, bf16[128,1280]{1,0:T(8,128)(2,1)S(1)}, u32[]{:S(2)}, u32[]{:S(2)}) collective-permute-start(bf16[128,1280]{1,0:T(8,128)(2,1)S(1)} %get-tuple-element.48), channel_id=1, source_target_pairs={{0,2},{2,0},{4,6},{6,4},{1,3},{3,1},{5,7},{7,5},{8,10},{10,8},{12,... | collective-permute-start | bytes 983048 | tf_op jit(solution)/shard_map/ppermute | solution.py:407
  11.9 13.9 %collective-permute-start.2 = (bf16[128,1280]{1,0:T(8,128)(2,1)S(1)}, bf16[128,1280]{1,0:T(8,128)(2,1)S(1)}, u32[]{:S(2)}, u32[]{:S(2)}) collective-permute-start(bf16[128,1280]{1,0:T(8,128)(2,1)S(1)} %get-tuple-element.46), channel_id=1, source_target_pairs={{0,4},{2,6},{4,0},{6,2},{1,5},{3,7},{5,1},{7,3},{8,12},{10,14},{12... | collective-permute-start | bytes 983048 | tf_op jit(solution)/shard_map/ppermute | solution.py:407
  17.1 9.2 %collective-permute-start.7 = (bf16[256,512]{1,0:T(8,128)(2,1)S(1)}, bf16[256,512]{1,0:T(8,128)(2,1)S(1)}, u32[]{:S(2)}, u32[]{:S(2)}) collective-permute-start(bf16[256,512]{1,0:T(8,128)(2,1)S(1)} %collective-permute-done.1.refs_9_.refs_10_), channel_id=1, source_target_pairs={{0,8},{8,0},{16,24},{24,16},{1,9},{9,1},{17,25},{25,17},{2,10},{10... | collective-permute-start | bytes 786440 | tf_op jit(solution)/shard_map/ppermute | solution.py:407
  21.0 5.4 %collective-permute-start.6 = (bf16[128,1280]{1,0:T(8,128)(2,1)S(1)}, bf16[128,1280]{1,0:T(8,128)(2,1)S(1)}, u32[]{:S(2)}, u32[]{:S(2)}) collective-permute-start(bf16[128,1280]{1,0:T(8,128)(2,1)S(1)} %get-tuple-element.50.refs_6_.refs_7_), channel_id=1, source_target_pairs={{0,1},{1,0},{2,3},{3,2},{4,5},{5,4},{6,7},{7,6},{8,9},{9,8},{10,11... | collective-permute-start | bytes 983048 | tf_op jit(solution)/shard_map/ppermute | solution.py:407
  25.8 1.6 %collective-permute-start.5 = (bf16[128,1280]{1,0:T(8,128)(2,1)S(1)}, bf16[128,1280]{1,0:T(8,128)(2,1)S(1)}, u32[]{:S(2)}, u32[]{:S(2)}) collective-permute-start(bf16[128,1280]{1,0:T(8,128)(2,1)S(1)} %collective-permute-done.4.refs_5_.refs_6_), channel_id=1, source_target_pairs={{0,1},{1,0},{2,3},{3,2},{4,5},{5,4},{6,7},{7,6},{8,9},{9,8},{10,11... | collective-permute-start | bytes 983048 | tf_op jit(solution)/shard_map/ppermute | solution.py:407
  25.8 2.1 %collective-permute-start.3 = (bf16[128,1280]{1,0:T(8,128)(2,1)S(1)}, bf16[128,1280]{1,0:T(8,128)(2,1)S(1)}, u32[]{:S(2)}, u32[]{:S(2)}) collective-permute-start(bf16[128,1280]{1,0:T(8,128)(2,1)S(1)} %collective-permute-done.2.refs_4_.refs_5_), channel_id=1, source_target_pairs={{0,1},{1,0},{2,3},{3,2},{4,5},{5,4},{6,7},{7,6},{8,9},{9,8},{10,11... | collective-permute-start | bytes 983048 | tf_op jit(solution)/shard_map/ppermute | solution.py:407
  26.3 3.3 %collective-permute-start.9 = (bf16[128,1280]{1,0:T(8,128)(2,1)S(1)}, bf16[128,1280]{1,0:T(8,128)(2,1)S(1)}, u32[]{:S(2)}, u32[]{:S(2)}) collective-permute-start(bf16[128,1280]{1,0:T(8,128)(2,1)S(1)} %collective-permute-done.8.refs_3_.refs_4_), channel_id=1, source_target_pairs={{0,1},{1,0},{2,3},{3,2},{4,5},{5,4},{6,7},{7,6},{8,9},{9,8},{10,11... | collective-permute-start | bytes 983048 | tf_op jit(solution)/shard_map/ppermute | solution.py:407
  29.6 18.7 %copy-start = (f32[3,1024]{1,0:T(4,128)S(1)}, f32[3,1024]{1,0:T(4,128)}, u32[]{:S(2)}) copy-start(f32[3,1024]{1,0:T(4,128)} %taps_ref.3) | copy-start | bytes 36868
  30.5 8.2 %collective-permute-start.10 = (bf16[64,1024]{1,0:T(8,128)(2,1)S(1)}, bf16[64,1024]{1,0:T(8,128)(2,1)S(1)}, u32[]{:S(2)}, u32[]{:S(2)}) collective-permute-start(bf16[64,1024]{1,0:T(8,128)(2,1)S(1)} %get-tuple-element.61), channel_id=1, source_target_pairs={{0,6},{2,4},{4,2},{6,0},{1,7},{3,5},{5,3},{7,1},{8,14},{10,12},{12... | collective-permute-start | bytes 393224 | tf_op jit(solution)/shard_map/ppermute | solution.py:407
  32.5 7.4 %collective-permute-start.11 = (bf16[64,1024]{1,0:T(8,128)(2,1)S(1)}, bf16[64,1024]{1,0:T(8,128)(2,1)S(1)}, u32[]{:S(2)}, u32[]{:S(2)}) collective-permute-start(bf16[64,1024]{1,0:T(8,128)(2,1)S(1)} %get-tuple-element.62), channel_id=1, source_target_pairs={{0,4},{2,6},{4,0},{6,2},{1,5},{3,7},{5,1},{7,3},{8,12},{10,14},{12... | collective-permute-start | bytes 393224 | tf_op jit(solution)/shard_map/ppermute | solution.py:407
  33.5 6.3 %collective-permute-start.12 = (bf16[64,1024]{1,0:T(8,128)(2,1)S(1)}, bf16[64,1024]{1,0:T(8,128)(2,1)S(1)}, u32[]{:S(2)}, u32[]{:S(2)}) collective-permute-start(bf16[64,1024]{1,0:T(8,128)(2,1)S(1)} %get-tuple-element.63), channel_id=1, source_target_pairs={{0,2},{2,0},{4,6},{6,4},{1,3},{3,1},{5,7},{7,5},{8,10},{10,8},{12,... | collective-permute-start | bytes 393224 | tf_op jit(solution)/shard_map/ppermute | solution.py:407
  34.1 4.7 %collective-permute-start.13 = (bf16[2,512]{1,0:T(2,128)(2,1)S(1)}, bf16[2,512]{1,0:T(2,128)(2,1)S(1)}, u32[]{:S(2)}, u32[]{:S(2)}) collective-permute-start(bf16[2,512]{1,0:T(2,128)(2,1)S(1)} %slice.3), channel_id=1, source_target_pairs={{0,2},{2,4},{4,6},{6,8},{8,10},{10,12},{12,14},{14,16},{16,18},{18... | collective-permute-start | bytes 6152 | tf_op jit(solution)/shard_map/ppermute | solution.py:525
  40.0 6.3 %collective-permute-start.14 = (bf16[16,1536]{1,0:T(8,128)(2,1)S(1)}, bf16[16,1536]{1,0:T(8,128)(2,1)S(1)}, u32[]{:S(2)}, u32[]{:S(2)}) collective-permute-start(bf16[16,1536]{1,0:T(8,128)(2,1)S(1)} %get-tuple-element.73), channel_id=1, source_target_pairs={{0,24},{8,16},{16,8},{24,0},{1,25},{9,17},{17,9},{25,1},{2,26},{10... | collective-permute-start | bytes 147464 | tf_op jit(solution)/shard_map/ppermute | solution.py:407
  42.5 5.7 %collective-permute-start.15 = (bf16[16,1536]{1,0:T(8,128)(2,1)S(1)}, bf16[16,1536]{1,0:T(8,128)(2,1)S(1)}, u32[]{:S(2)}, u32[]{:S(2)}) collective-permute-start(bf16[16,1536]{1,0:T(8,128)(2,1)S(1)} %get-tuple-element.74), channel_id=1, source_target_pairs={{0,16},{8,24},{16,0},{24,8},{1,17},{9,25},{17,1},{25,9},{2,18},{10... | collective-permute-start | bytes 147464 | tf_op jit(solution)/shard_map/ppermute | solution.py:407
  43.5 4.9 %collective-permute-start.16 = (bf16[16,1536]{1,0:T(8,128)(2,1)S(1)}, bf16[16,1536]{1,0:T(8,128)(2,1)S(1)}, u32[]{:S(2)}, u32[]{:S(2)}) collective-permute-start(bf16[16,1536]{1,0:T(8,128)(2,1)S(1)} %get-tuple-element.75), channel_id=1, source_target_pairs={{0,8},{8,0},{16,24},{24,16},{1,9},{9,1},{17,25},{25,17},{2,10},{10... | collective-permute-start | bytes 147464 | tf_op jit(solution)/shard_map/ppermute | solution.py:407

commit v6 on v5

--- a/solution.py
+++ b/solution.py
@@ -15,9 +15,7 @@
 SLOTS = LANES // BLOCK
 MIB = 1 << 20
 VMEM = pl.BlockSpec(memory_space=pltpu.VMEM)
-SMEM = pl.BlockSpec(memory_space=pltpu.SMEM)
 HBM = pl.BlockSpec(memory_space=pltpu.HBM)
-ANY = pl.BlockSpec(memory_space=pl.ANY)
 
 
 def params(mib):
@@ -360,38 +358,24 @@
     out_ref[...] = done_ref[:, :held, :].astype(BF16)
 
 
-def out_kernel(
-    gate_ref, before_ref, taps_ref, mixed_ref, source_ref, target_ref,
-    gate_held, before_held, taps_held, mixed_held, weight_ref, held_ref, small_sems, read_sems, write_sems,
-):
-    chunks, channels, step = weight_ref.shape
-    small = [
-        pltpu.make_async_copy(source, target, small_sems.at[at])
-        for at, (source, target) in enumerate(
-            (
-                (gate_ref, gate_held),
-                (before_ref, before_held),
-                (taps_ref, taps_held),
-                (mixed_ref, mixed_held),
-            )
-        )
-    ]
-    reads = [
-        pltpu.make_async_copy(
-            source_ref.at[:, pl.ds(at * step, step)], weight_ref.at[at], read_sems.at[at]
-        )
-        for at in range(chunks)
-    ]
-    for copy in small + reads:
-        copy.start()
-    for copy in small:
-        copy.wait()
-    gate = gate_held[...].astype(F32)
-    extended = jnp.concatenate([before_held[...].astype(F32), gate], axis=0)
-    gate_short = taps_held[0:1, channels:] * gate
+def gate_kernel(gate_ref, before_ref, taps_ref, out_ref):
+    channels = gate_ref.shape[1]
+    gate = gate_ref[...].astype(F32)
+    extended = jnp.concatenate([before_ref[...].astype(F32), gate], axis=0)
+    gate_short = taps_ref[0:1, channels:] * gate
     for lag in range(1, 3):
-        gate_short += taps_held[lag : lag + 1, channels:] * extended[2 - lag : 2 - lag + gate.shape[0]]
-    gated = (gate_short * mixed_held[...].astype(F32).T).astype(BF16)
+        gate_short += taps_ref[lag : lag + 1, channels:] * extended[2 - lag : 2 - lag + gate.shape[0]]
+    out_ref[...] = gate_short
+
+
+def out_kernel(gate_ref, mixed_ref, source_ref, target_ref, weight_ref, held_ref, read_sems, write_sems):
+    chunks, _, step = weight_ref.shape
+    reads = []
+    for at in range(chunks):
+        columns = source_ref.at[:, pl.ds(at * step, step)]
+        reads.append(pltpu.make_async_copy(columns, weight_ref.at[at], read_sems.at[at]))
+        reads[-1].start()
+    gated = (gate_ref[...] * mixed_ref[...].astype(F32).T).astype(BF16)
     writes = []
     for at in range(chunks):
         reads[at].wait()
@@ -544,6 +528,17 @@
         parts = lax.all_to_all(jnp.take(jnp.stack(parts), order, axis=0), "far", 0, 0, tiled=True)
         parts = [parts.reshape(far * held, far_shape[1])]
 
+    gate_short = pl.pallas_call(
+        gate_kernel,
+        in_specs=[VMEM] * 3,
+        out_specs=VMEM,
+        out_shape=jax.ShapeDtypeStruct((rows, channels), F32),
+        compiler_params=params(4),
+        cost_estimate=cost(rows * channels * 6, MIB // 2),
+        name="gate",
+    )(gate_rows, before, conv_taps)
+    parts[0], gate_short = lax.optimization_barrier((parts[0], gate_short))
+
     tiles = length // LANES
     all_rows = tiles * SLOTS * cores * GROUP
     held_rows = max(held, GROUP)
@@ -568,24 +563,19 @@
     chunks = 8
     return pl.pallas_call(
         out_kernel,
-        in_specs=[ANY] * 4 + [HBM],
+        in_specs=[VMEM] * 2 + [HBM],
         out_specs=HBM,
         out_shape=jax.ShapeDtypeStruct((rows, width), BF16),
         scratch_shapes=[
-            pltpu.VMEM(gate_rows.shape, BF16),
-            pltpu.VMEM(before.shape, BF16),
-            pltpu.VMEM(conv_taps.shape, F32),
-            pltpu.VMEM(landed.shape, BF16),
             pltpu.VMEM((chunks, channels, width // chunks), BF16),
             pltpu.VMEM((chunks, rows, width // chunks), BF16),
-            pltpu.SemaphoreType.DMA((4,)),
             pltpu.SemaphoreType.DMA((chunks,)),
             pltpu.SemaphoreType.DMA((chunks,)),
         ],
         compiler_params=params(16),
         cost_estimate=cost(2 * rows * width * channels, 5 * MIB),
         name="project_out",
-    )(gate_rows, before, conv_taps, landed, *in_hbm(w_out))
+    )(gate_short, landed, *in_hbm(w_out))
 
 
 def solution(mesh):

time: 65 us -> 64.3 us (0.989)
  waiting for transfers between devices: 17.2 us -> 16.3 us
    ppermute x16, waiting for transfers between devices: 15.9 us -> 14.9 us  [exchanged(): lax.ppermute(value, axis, [(i, i ^ step) for i in range(lax.axis_size(axi...]
    pallas_call x1 -> x2, Pallas kernels: 4.09 us -> 3.82 us  [the longest x1 3.73 us: on_device(): pl.pallas_call(out_kernel, in_specs=[VMEM] * 2 + [HBM], out_specs=HBM, ou...]
  transfers between devices with their start and end apart: 17 -> 17, of which waited for: 9 -> 8; matrix products, arithmetic and copies ran while one was open for 5% -> 5% of each run, Pallas kernels for 6% -> 6%
where the time goes in v6:
time: 64.3 us; the launch traced here: 64.1 us
  starting transfers between devices  21.9 us (34%)
  waiting for transfers between devices  16.3 us (25%)
  Pallas kernels  12.2 us (19%)
  blocking collectives  10.4 us (16%)
  matrix products  3.23 us (5%)
    ppermute x16, starting transfers between devices, exchanged(): lax.ppermute(value, axis, [(i, i ^ step) for i in range(lax.axis_size(axi...  18.5 us
    ppermute x16, waiting for transfers between devices, exchanged(): lax.ppermute(value, axis, [(i, i ^ step) for i in range(lax.axis_size(axi...  14.9 us
    all_to_all x1, blocking collectives, on_device(): lax.all_to_all(mixed, ('dp', 'far', 'near'), 0, 0, tiled=True)  10.4 us
    pallas_call x1, Pallas kernels, on_device(): pl.pallas_call(out_kernel, in_specs=[VMEM] * 2 + [HBM], out_specs=HBM, ou...  3.73 us
    ppermute x1, starting transfers between devices, on_device(): lax.ppermute(last_rows, ('far', 'near'), [(i, i + 1) for i in range(count...  3.43 us
    dot_general x1, matrix products, on_device(): jnp.dot(late_tokens, w_gate, preferred_element_type=F32).astype(BF16)  3.23 us
    pallas_call x1, Pallas kernels, on_device(): pl.pallas_call(functools.partial(mix_kernel, near, far, cores, held), in_...  2.52 us
    pallas_call x1, Pallas kernels, on_device(): pl.pallas_call(functools.partial(pack_kernel, near, far), in_specs=[HBM]...  2.16 us
  transfers between devices with their start and end apart: 17, of which 8 were waited for; matrix products, arithmetic and copies ran while one was open for 5% of the time, Pallas kernels for 6%

profile of v6, /device:TPU:0, one launch (start us, length us, event | category | flops | bytes accessed | tf_op | source)
XLA Modules:
  0.0 64.1 jit_solution(14549176697191650427)
XLA Ops:
  0.0 1.0 %weights.1 = bf16[256,512]{1,0:T(8,128)(2,1)S(1)} custom-call(bf16[256,512]{1,0:T(8,128)(2,1)} %value_ref.3, bf16[256,512]{1,0:T(8,128)(2,1)} %noise_ref.3), custom_call_target="tpu_custom_call" | custom-call | bytes 524288 | tf_op jit(solution)/shard_map/weights/pallas_call | solution.py:416
  1.0 4.1 %collective-permute-start.2 = (bf16[256,512]{1,0:T(8,128)(2,1)S(1)}, bf16[256,512]{1,0:T(8,128)(2,1)S(1)}, u32[]{:S(2)}, u32[]{:S(2)}) collective-permute-start(bf16[256,512]{1,0:T(8,128)(2,1)S(1)} %weights.1), channel_id=1, source_target_pairs={{0,16},{8,24},{16,0},{24,8},{1,17},{9,25},{17,1},{25,9},{2,18},{10... | collective-permute-start | bytes 786440 | tf_op jit(solution)/shard_map/ppermute | solution.py:391
  5.1 2.2 %pack.1 = (bf16[256,512]{1,0:T(8,128)(2,1)S(1)}, bf16[128,1280]{1,0:T(8,128)(2,1)S(1)}, bf16[128,1280]{1,0:T(8,128)(2,1)S(1)}, bf16[128,1280]{1,0:T(8,128)(2,1)S(1)}, bf16[128,1280]{1,0:T(8,128)(2,1)S(1)}) custom-call(bf16[128,4096]{1,0:T(8,128)(2,1)} %tokens_ref, s32[128,256]{1,0:T(8,128)} %in_ref.1, s32[32,128]{1,0:T(8,128)} %bitcast.5, ...), custom_call_target="tpu_custom_call" | custom-call | flops 67108864 | bytes 3145728 | tf_op jit(solution)/shard_map/pack/pallas_call | solution.py:428
  7.3 1.6 %collective-permute-start = (bf16[128,1280]{1,0:T(8,128)(2,1)S(1)}, bf16[128,1280]{1,0:T(8,128)(2,1)S(1)}, u32[]{:S(2)}, u32[]{:S(2)}) collective-permute-start(bf16[128,1280]{1,0:T(8,128)(2,1)S(1)} %get-tuple-element.44), channel_id=1, source_target_pairs={{0,4},{2,6},{4,0},{6,2},{1,5},{3,7},{5,1},{7,3},{8,12},{10,14},{12... | collective-permute-start | bytes 983048 | tf_op jit(solution)/shard_map/ppermute | solution.py:391
  8.8 1.6 %collective-permute-start.1 = (bf16[256,512]{1,0:T(8,128)(2,1)S(1)}, bf16[256,512]{1,0:T(8,128)(2,1)S(1)}, u32[]{:S(2)}, u32[]{:S(2)}) collective-permute-start(bf16[256,512]{1,0:T(8,128)(2,1)S(1)} %get-tuple-element.45.refs_7_.refs_8_), channel_id=1, source_target_pairs={{0,8},{8,0},{16,24},{24,16},{1,9},{9,1},{17,25},{25,17},{2,10},{10... | collective-permute-start | bytes 786440 | tf_op jit(solution)/shard_map/ppermute | solution.py:391
  10.4 1.5 %collective-permute-start.4 = (bf16[128,1280]{1,0:T(8,128)(2,1)S(1)}, bf16[128,1280]{1,0:T(8,128)(2,1)S(1)}, u32[]{:S(2)}, u32[]{:S(2)}) collective-permute-start(bf16[128,1280]{1,0:T(8,128)(2,1)S(1)} %get-tuple-element.50), channel_id=1, source_target_pairs={{0,2},{2,0},{4,6},{6,4},{1,3},{3,1},{5,7},{7,5},{8,10},{10,8},{12,... | collective-permute-start | bytes 983048 | tf_op jit(solution)/shard_map/ppermute | solution.py:391
  12.4 4.7 %collective-permute-done.2.refs_9_.refs_10_ = bf16[256,512]{1,0:T(8,128)(2,1)S(1)} collective-permute-done((bf16[256,512]{1,0:T(8,128)(2,1)S(1)}, bf16[256,512]{1,0:T(8,128)(2,1)S(1)}, u32[]{:S(2)}, u32[]{:S(2)}) %collective-permute-start.2) | collective-permute-done | bytes 262176 | tf_op jit(solution)/shard_map/ppermute | solution.py:391
  17.8 3.2 %convolution_convert_fusion.gate_ref = bf16[128,512]{1,0:T(8,128)(2,1)S(1)} fusion(bf16[128,4096]{1,0:T(8,128)(2,1)} %tokens_ref, bf16[4096,512]{1,0:T(8,128)(2,1)} %param.14), kind=kOutput, calls=%fused_computation | convolution fusion | flops 536936448 | bytes 5373952 | tf_op jit(solution)/shard_map/dot_general | solution.py:469
  21.0 1.1 %collective-permute-done.1.refs_8_.refs_9_ = bf16[256,512]{1,0:T(8,128)(2,1)S(1)} collective-permute-done((bf16[256,512]{1,0:T(8,128)(2,1)S(1)}, bf16[256,512]{1,0:T(8,128)(2,1)S(1)}, u32[]{:S(2)}, u32[]{:S(2)}) %collective-permute-start.1) | collective-permute-done | bytes 262176 | tf_op jit(solution)/shard_map/ppermute | solution.py:391
  22.7 3.3 %collective-permute-done.8.refs_3_.refs_4_ = bf16[128,1280]{1,0:T(8,128)(2,1)S(1)} collective-permute-done((bf16[128,1280]{1,0:T(8,128)(2,1)S(1)}, bf16[128,1280]{1,0:T(8,128)(2,1)S(1)}, u32[]{:S(2)}, u32[]{:S(2)}) %collective-permute-start.8) | collective-permute-done | bytes 327712 | tf_op jit(solution)/shard_map/ppermute | solution.py:391
  26.4 1.7 %project.1 = (f32[896,256]{1,0:T(8,128)S(1)}, f32[896,256]{1,0:T(8,128)S(1)}, bf16[896,256]{1,0:T(8,128)(2,1)S(1)}, bf16[896,256]{1,0:T(8,128)(2,1)S(1)}, f32[64,512]{1,0:T(8,128)S(1)}) custom-call(bf16[128,1280]{1,0:T(8,128)(2,1)S(1)} %collective-permute-done.3.refs_0_.refs_1_, bf16[128,1280]{1,0:T(8,128)(2,1)S(1)} %collective-permute-done.5.refs_1_.refs_2_, ...), custom_call_target="tpu_custom_call" | custom-call | flops 704643072 | bytes 5242880 | tf_op jit(solution)/shard_map/project/pallas_call | solution.py:481
  28.2 0.8 %finish.1 = (bf16[64,1024]{1,0:T(8,128)(2,1)S(1)}, bf16[64,1024]{1,0:T(8,128)(2,1)S(1)}, bf16[64,1024]{1,0:T(8,128)(2,1)S(1)}, bf16[64,1024]{1,0:T(8,128)(2,1)S(1)}) custom-call(f32[896,256]{1,0:T(8,128)S(1)} %get-tuple-element.59.mean_ref, f32[896,256]{1,0:T(8,128)S(1)} %get-tuple-element.60.noise_ref, bf16[896,256]{1,0:T(8,128)(2,1)S(1)} %get-tuple-element.61.flip_ref, ...), custom_call_target="tpu_custom_call" | custom-call | flops 369098752 | bytes 3145728 | tf_op jit(solution)/shard_map/finish/pallas_call | solution.py:497
  29.0 2.1 %collective-permute-start.10 = (bf16[64,1024]{1,0:T(8,128)(2,1)S(1)}, bf16[64,1024]{1,0:T(8,128)(2,1)S(1)}, u32[]{:S(2)}, u32[]{:S(2)}) collective-permute-start(bf16[64,1024]{1,0:T(8,128)(2,1)S(1)} %get-tuple-element.64), channel_id=1, source_target_pairs={{0,6},{2,4},{4,2},{6,0},{1,7},{3,5},{5,3},{7,1},{8,14},{10,12},{12... | collective-permute-start | bytes 393224 | tf_op jit(solution)/shard_map/ppermute | solution.py:391
  31.2 0.9 %collective-permute-start.11 = (bf16[64,1024]{1,0:T(8,128)(2,1)S(1)}, bf16[64,1024]{1,0:T(8,128)(2,1)S(1)}, u32[]{:S(2)}, u32[]{:S(2)}) collective-permute-start(bf16[64,1024]{1,0:T(8,128)(2,1)S(1)} %get-tuple-element.65), channel_id=1, source_target_pairs={{0,4},{2,6},{4,0},{6,2},{1,5},{3,7},{5,1},{7,3},{8,12},{10,14},{12... | collective-permute-start | bytes 393224 | tf_op jit(solution)/shard_map/ppermute | solution.py:391
  32.6 3.4 %collective-permute-start.13 = (bf16[2,512]{1,0:T(2,128)(2,1)S(1)}, bf16[2,512]{1,0:T(2,128)(2,1)S(1)}, u32[]{:S(2)}, u32[]{:S(2)}) collective-permute-start(bf16[2,512]{1,0:T(2,128)(2,1)S(1)} %slice.3), channel_id=1, source_target_pairs={{0,2},{2,4},{4,6},{6,8},{8,10},{10,12},{12,14},{14,16},{16,18},{18... | collective-permute-start | bytes 6152 | tf_op jit(solution)/shard_map/ppermute | solution.py:509
  36.0 1.4 %collective-permute-done.13.before_ref = bf16[2,512]{1,0:T(2,128)(2,1)S(1)} collective-permute-done((bf16[2,512]{1,0:T(2,128)(2,1)S(1)}, bf16[2,512]{1,0:T(2,128)(2,1)S(1)}, u32[]{:S(2)}, u32[]{:S(2)}) %collective-permute-start.13) | collective-permute-done | bytes 2080 | tf_op jit(solution)/shard_map/ppermute | solution.py:509
  37.5 1.2 %collective-permute-done.11.refs_1_ = bf16[64,1024]{1,0:T(8,128)(2,1)S(1)} collective-permute-done((bf16[64,1024]{1,0:T(8,128)(2,1)S(1)}, bf16[64,1024]{1,0:T(8,128)(2,1)S(1)}, u32[]{:S(2)}, u32[]{:S(2)}) %collective-permute-start.11) | collective-permute-done | bytes 131104 | tf_op jit(solution)/shard_map/ppermute | solution.py:391
  38.8 3.6 %collective-permute-start.14 = (bf16[16,1536]{1,0:T(8,128)(2,1)S(1)}, bf16[16,1536]{1,0:T(8,128)(2,1)S(1)}, u32[]{:S(2)}, u32[]{:S(2)}) collective-permute-start(bf16[16,1536]{1,0:T(8,128)(2,1)S(1)} %get-tuple-element.77), channel_id=1, source_target_pairs={{0,24},{8,16},{16,8},{24,0},{1,25},{9,17},{17,9},{25,1},{2,26},{10... | collective-permute-start | bytes 147464 | tf_op jit(solution)/shard_map/ppermute | solution.py:391
  42.5 0.8 %collective-permute-start.16 = (bf16[16,1536]{1,0:T(8,128)(2,1)S(1)}, bf16[16,1536]{1,0:T(8,128)(2,1)S(1)}, u32[]{:S(2)}, u32[]{:S(2)}) collective-permute-start(bf16[16,1536]{1,0:T(8,128)(2,1)S(1)} %get-tuple-element.79), channel_id=1, source_target_pairs={{0,8},{8,0},{16,24},{24,16},{1,9},{9,1},{17,25},{25,17},{2,10},{10... | collective-permute-start | bytes 147464 | tf_op jit(solution)/shard_map/ppermute | solution.py:391
  43.4 1.6 %collective-permute-done.14.refs_0_ = bf16[16,1536]{1,0:T(8,128)(2,1)S(1)} collective-permute-done((bf16[16,1536]{1,0:T(8,128)(2,1)S(1)}, bf16[16,1536]{1,0:T(8,128)(2,1)S(1)}, u32[]{:S(2)}, u32[]{:S(2)}) %collective-permute-start.14) | collective-permute-done | bytes 49184 | tf_op jit(solution)/shard_map/ppermute | solution.py:391
  45.0 2.5 %collective-permute-done.15.refs_1_ = bf16[16,1536]{1,0:T(8,128)(2,1)S(1)} collective-permute-done((bf16[16,1536]{1,0:T(8,128)(2,1)S(1)}, bf16[16,1536]{1,0:T(8,128)(2,1)S(1)}, u32[]{:S(2)}, u32[]{:S(2)}) %collective-permute-start.15) | collective-permute-done | bytes 49184 | tf_op jit(solution)/shard_map/ppermute | solution.py:391
  47.5 2.5 %mix.1 = bf16[32,16,128]{2,1,0:T(8,128)(2,1)S(1)} custom-call(f32[3,1024]{1,0:T(4,128)S(1)} %copy-done, bf16[16,1536]{1,0:T(8,128)(2,1)S(1)} %collective-permute-done.14.refs_0_, bf16[16,1536]{1,0:T(8,128)(2,1)S(1)} %collective-permute-done.15.refs_1_, bf16[16,1536]{1,0:T(8,128)(2,1)S(1)} %collective-permute-done.16.refs_2_, ...), custom_call_target="tpu_custom_call" | custom-call | flops 536870912 | bytes 2097152 | tf_op jit(solution)/shard_map/mix/pallas_call | solution.py:545
  50.0 10.4 %all_to_all.5 = bf16[32,16,128]{2,1,0:T(8,128)(2,1)S(1)} all-to-all(bf16[32,16,128]{2,1,0:T(8,128)(2,1)S(1)} %mix.1), channel_id=1, replica_groups=mesh['far'=4,'near'=4,'dp'=2] {'dp','far','near'}, dimensions={0} | all-to-all | bytes 262144 | tf_op jit(solution)/shard_map/all_to_all | solution.py:562
  60.4 3.7 %project_out.1 = bf16[128,4096]{1,0:T(8,128)(2,1)} custom-call(f32[128,512]{1,0:T(8,128)S(1)} %gate.1.gate_ref, bf16[512,128]{1,0:T(8,128)(2,1)S(1)} %bitcast.4, bf16[512,4096]{1,0:T(8,128)(2,1)} %source_ref.1), custom_call_target="tpu_custom_call" | custom-call | flops 536870912 | bytes 5242880 | tf_op jit(solution)/shard_map/project_out/pallas_call | solution.py:564
  (23 shorter events, 2.9 us)
Async XLA Ops:
  1.0 16.1 %collective-permute-start.2 = (bf16[256,512]{1,0:T(8,128)(2,1)S(1)}, bf16[256,512]{1,0:T(8,128)(2,1)S(1)}, u32[]{:S(2)}, u32[]{:S(2)}) collective-permute-start(bf16[256,512]{1,0:T(8,128)(2,1)S(1)} %weights.1), channel_id=1, source_target_pairs={{0,16},{8,24},{16,0},{24,8},{1,17},{9,25},{17,1},{25,9},{2,18},{10... | collective-permute-start | bytes 786440 | tf_op jit(solution)/shard_map/ppermute | solution.py:391
  7.3 14.8 %collective-permute-start = (bf16[128,1280]{1,0:T(8,128)(2,1)S(1)}, bf16[128,1280]{1,0:T(8,128)(2,1)S(1)}, u32[]{:S(2)}, u32[]{:S(2)}) collective-permute-start(bf16[128,1280]{1,0:T(8,128)(2,1)S(1)} %get-tuple-element.44), channel_id=1, source_target_pairs={{0,4},{2,6},{4,0},{6,2},{1,5},{3,7},{5,1},{7,3},{8,12},{10,14},{12... | collective-permute-start | bytes 983048 | tf_op jit(solution)/shard_map/ppermute | solution.py:391
  8.8 13.2 %collective-permute-start.1 = (bf16[256,512]{1,0:T(8,128)(2,1)S(1)}, bf16[256,512]{1,0:T(8,128)(2,1)S(1)}, u32[]{:S(2)}, u32[]{:S(2)}) collective-permute-start(bf16[256,512]{1,0:T(8,128)(2,1)S(1)} %get-tuple-element.45.refs_7_.refs_8_), channel_id=1, source_target_pairs={{0,8},{8,0},{16,24},{24,16},{1,9},{9,1},{17,25},{25,17},{2,10},{10... | collective-permute-start | bytes 786440 | tf_op jit(solution)/shard_map/ppermute | solution.py:391
  10.4 12.2 %collective-permute-start.4 = (bf16[128,1280]{1,0:T(8,128)(2,1)S(1)}, bf16[128,1280]{1,0:T(8,128)(2,1)S(1)}, u32[]{:S(2)}, u32[]{:S(2)}) collective-permute-start(bf16[128,1280]{1,0:T(8,128)(2,1)S(1)} %get-tuple-element.50), channel_id=1, source_target_pairs={{0,2},{2,0},{4,6},{6,4},{1,3},{3,1},{5,7},{7,5},{8,10},{10,8},{12,... | collective-permute-start | bytes 983048 | tf_op jit(solution)/shard_map/ppermute | solution.py:391
  11.9 14.1 %collective-permute-start.8 = (bf16[128,1280]{1,0:T(8,128)(2,1)S(1)}, bf16[128,1280]{1,0:T(8,128)(2,1)S(1)}, u32[]{:S(2)}, u32[]{:S(2)}) collective-permute-start(bf16[128,1280]{1,0:T(8,128)(2,1)S(1)} %get-tuple-element.54), channel_id=1, source_target_pairs={{0,6},{2,4},{4,2},{6,0},{1,7},{3,5},{5,3},{7,1},{8,14},{10,12},{12... | collective-permute-start | bytes 983048 | tf_op jit(solution)/shard_map/ppermute | solution.py:391
  17.1 9.3 %collective-permute-start.7 = (bf16[256,512]{1,0:T(8,128)(2,1)S(1)}, bf16[256,512]{1,0:T(8,128)(2,1)S(1)}, u32[]{:S(2)}, u32[]{:S(2)}) collective-permute-start(bf16[256,512]{1,0:T(8,128)(2,1)S(1)} %collective-permute-done.2.refs_9_.refs_10_), channel_id=1, source_target_pairs={{0,8},{8,0},{16,24},{24,16},{1,9},{9,1},{17,25},{25,17},{2,10},{10... | collective-permute-start | bytes 786440 | tf_op jit(solution)/shard_map/ppermute | solution.py:391
  22.1 4.3 %collective-permute-start.6 = (bf16[128,1280]{1,0:T(8,128)(2,1)S(1)}, bf16[128,1280]{1,0:T(8,128)(2,1)S(1)}, u32[]{:S(2)}, u32[]{:S(2)}) collective-permute-start(bf16[128,1280]{1,0:T(8,128)(2,1)S(1)} %get-tuple-element.52.refs_6_.refs_7_), channel_id=1, source_target_pairs={{0,1},{1,0},{2,3},{3,2},{4,5},{5,4},{6,7},{7,6},{8,9},{9,8},{10,11... | collective-permute-start | bytes 983048 | tf_op jit(solution)/shard_map/ppermute | solution.py:391
  22.1 4.3 %collective-permute-start.3 = (bf16[128,1280]{1,0:T(8,128)(2,1)S(1)}, bf16[128,1280]{1,0:T(8,128)(2,1)S(1)}, u32[]{:S(2)}, u32[]{:S(2)}) collective-permute-start(bf16[128,1280]{1,0:T(8,128)(2,1)S(1)} %collective-permute-done.refs_4_.refs_5_), channel_id=1, source_target_pairs={{0,1},{1,0},{2,3},{3,2},{4,5},{5,4},{6,7},{7,6},{8,9},{9,8},{10,11... | collective-permute-start | bytes 983048 | tf_op jit(solution)/shard_map/ppermute | solution.py:391
  22.6 3.8 %collective-permute-start.5 = (bf16[128,1280]{1,0:T(8,128)(2,1)S(1)}, bf16[128,1280]{1,0:T(8,128)(2,1)S(1)}, u32[]{:S(2)}, u32[]{:S(2)}) collective-permute-start(bf16[128,1280]{1,0:T(8,128)(2,1)S(1)} %collective-permute-done.4.refs_5_.refs_6_), channel_id=1, source_target_pairs={{0,1},{1,0},{2,3},{3,2},{4,5},{5,4},{6,7},{7,6},{8,9},{9,8},{10,11... | collective-permute-start | bytes 983048 | tf_op jit(solution)/shard_map/ppermute | solution.py:391
  26.4 1.8 %collective-permute-start.9 = (bf16[128,1280]{1,0:T(8,128)(2,1)S(1)}, bf16[128,1280]{1,0:T(8,128)(2,1)S(1)}, u32[]{:S(2)}, u32[]{:S(2)}) collective-permute-start(bf16[128,1280]{1,0:T(8,128)(2,1)S(1)} %collective-permute-done.8.refs_3_.refs_4_), channel_id=1, source_target_pairs={{0,1},{1,0},{2,3},{3,2},{4,5},{5,4},{6,7},{7,6},{8,9},{9,8},{10,11... | collective-permute-start | bytes 983048 | tf_op jit(solution)/shard_map/ppermute | solution.py:391
  28.2 15.1 %copy-start = (f32[3,1024]{1,0:T(4,128)S(1)}, f32[3,1024]{1,0:T(4,128)}, u32[]{:S(2)}) copy-start(f32[3,1024]{1,0:T(4,128)} %taps_ref.3) | copy-start | bytes 36868
  29.0 8.4 %collective-permute-start.10 = (bf16[64,1024]{1,0:T(8,128)(2,1)S(1)}, bf16[64,1024]{1,0:T(8,128)(2,1)S(1)}, u32[]{:S(2)}, u32[]{:S(2)}) collective-permute-start(bf16[64,1024]{1,0:T(8,128)(2,1)S(1)} %get-tuple-element.64), channel_id=1, source_target_pairs={{0,6},{2,4},{4,2},{6,0},{1,7},{3,5},{5,3},{7,1},{8,14},{10,12},{12... | collective-permute-start | bytes 393224 | tf_op jit(solution)/shard_map/ppermute | solution.py:391
  31.2 7.6 %collective-permute-start.11 = (bf16[64,1024]{1,0:T(8,128)(2,1)S(1)}, bf16[64,1024]{1,0:T(8,128)(2,1)S(1)}, u32[]{:S(2)}, u32[]{:S(2)}) collective-permute-start(bf16[64,1024]{1,0:T(8,128)(2,1)S(1)} %get-tuple-element.65), channel_id=1, source_target_pairs={{0,4},{2,6},{4,0},{6,2},{1,5},{3,7},{5,1},{7,3},{8,12},{10,14},{12... | collective-permute-start | bytes 393224 | tf_op jit(solution)/shard_map/ppermute | solution.py:391
  32.1 6.6 %collective-permute-start.12 = (bf16[64,1024]{1,0:T(8,128)(2,1)S(1)}, bf16[64,1024]{1,0:T(8,128)(2,1)S(1)}, u32[]{:S(2)}, u32[]{:S(2)}) collective-permute-start(bf16[64,1024]{1,0:T(8,128)(2,1)S(1)} %get-tuple-element.66), channel_id=1, source_target_pairs={{0,2},{2,0},{4,6},{6,4},{1,3},{3,1},{5,7},{7,5},{8,10},{10,8},{12,... | collective-permute-start | bytes 393224 | tf_op jit(solution)/shard_map/ppermute | solution.py:391
  32.6 4.9 %collective-permute-start.13 = (bf16[2,512]{1,0:T(2,128)(2,1)S(1)}, bf16[2,512]{1,0:T(2,128)(2,1)S(1)}, u32[]{:S(2)}, u32[]{:S(2)}) collective-permute-start(bf16[2,512]{1,0:T(2,128)(2,1)S(1)} %slice.3), channel_id=1, source_target_pairs={{0,2},{2,4},{4,6},{6,8},{8,10},{10,12},{12,14},{14,16},{16,18},{18... | collective-permute-start | bytes 6152 | tf_op jit(solution)/shard_map/ppermute | solution.py:509
  38.8 6.2 %collective-permute-start.14 = (bf16[16,1536]{1,0:T(8,128)(2,1)S(1)}, bf16[16,1536]{1,0:T(8,128)(2,1)S(1)}, u32[]{:S(2)}, u32[]{:S(2)}) collective-permute-start(bf16[16,1536]{1,0:T(8,128)(2,1)S(1)} %get-tuple-element.77), channel_id=1, source_target_pairs={{0,24},{8,16},{16,8},{24,0},{1,25},{9,17},{17,9},{25,1},{2,26},{10... | collective-permute-start | bytes 147464 | tf_op jit(solution)/shard_map/ppermute | solution.py:391
  42.5 5.0 %collective-permute-start.15 = (bf16[16,1536]{1,0:T(8,128)(2,1)S(1)}, bf16[16,1536]{1,0:T(8,128)(2,1)S(1)}, u32[]{:S(2)}, u32[]{:S(2)}) collective-permute-start(bf16[16,1536]{1,0:T(8,128)(2,1)S(1)} %get-tuple-element.78), channel_id=1, source_target_pairs={{0,16},{8,24},{16,0},{24,8},{1,17},{9,25},{17,1},{25,9},{2,18},{10... | collective-permute-start | bytes 147464 | tf_op jit(solution)/shard_map/ppermute | solution.py:391
  42.5 5.0 %collective-permute-start.16 = (bf16[16,1536]{1,0:T(8,128)(2,1)S(1)}, bf16[16,1536]{1,0:T(8,128)(2,1)S(1)}, u32[]{:S(2)}, u32[]{:S(2)}) collective-permute-start(bf16[16,1536]{1,0:T(8,128)(2,1)S(1)} %get-tuple-element.79), channel_id=1, source_target_pairs={{0,8},{8,0},{16,24},{24,16},{1,9},{9,1},{17,25},{25,17},{2,10},{10... | collective-permute-start | bytes 147464 | tf_op jit(solution)/shard_map/ppermute | solution.py:391

commit v7 on v6

--- a/solution.py
+++ b/solution.py
@@ -311,7 +311,6 @@
             kept = jnp.where(owner == lane // BLOCK + half * SLOTS, spread, 0.0)
             left_ref[:, half * LANES : (half + 1) * LANES] = kept.astype(BF16)
 
-        sums_ref[...] = jnp.zeros_like(sums_ref)
         if tiles <= 16:
             for at in range(tiles // 2):
                 start = 2 * at * tile_rows
@@ -320,9 +319,13 @@
                     table_ref[:, at * pair : (at + 1) * pair],
                     preferred_element_type=F32,
                 )
-                sums_ref[start:rows, :] += partial[:, :LANES]
+                if at == 0:
+                    sums_ref[...] = partial[:, :LANES]
+                else:
+                    sums_ref[start:rows, :] += partial[:, :LANES]
                 sums_ref[start + tile_rows : rows, :] += partial[: rows - start - tile_rows, LANES:]
         else:
+            sums_ref[...] = jnp.zeros_like(sums_ref)
 
             def add(at, _):
                 partial = jnp.dot(

time: 64.3 us -> 64.3 us (level)
  no operation moved by 1% of the time
where the time goes in v7:
time: 64.3 us; the launch traced here: 64.1 us
  starting transfers between devices  21.9 us (34%)
  waiting for transfers between devices  16.3 us (25%)
  Pallas kernels  12.2 us (19%)
  blocking collectives  10.4 us (16%)
  matrix products  3.23 us (5%)
    ppermute x16, starting transfers between devices, exchanged(): lax.ppermute(value, axis, [(i, i ^ step) for i in range(lax.axis_size(axi...  18.5 us
    ppermute x16, waiting for transfers between devices, exchanged(): lax.ppermute(value, axis, [(i, i ^ step) for i in range(lax.axis_size(axi...  14.9 us
    all_to_all x1, blocking collectives, on_device(): lax.all_to_all(mixed, ('dp', 'far', 'near'), 0, 0, tiled=True)  10.4 us
    pallas_call x1, Pallas kernels, on_device(): pl.pallas_call(out_kernel, in_specs=[VMEM] * 2 + [HBM], out_specs=HBM, ou...  3.73 us
    ppermute x1, starting transfers between devices, on_device(): lax.ppermute(last_rows, ('far', 'near'), [(i, i + 1) for i in range(count...  3.43 us
    dot_general x1, matrix products, on_device(): jnp.dot(late_tokens, w_gate, preferred_element_type=F32).astype(BF16)  3.23 us
    pallas_call x1, Pallas kernels, on_device(): pl.pallas_call(functools.partial(mix_kernel, near, far, cores, held), in_...  2.52 us
    pallas_call x1, Pallas kernels, on_device(): pl.pallas_call(functools.partial(pack_kernel, near, far), in_specs=[HBM]...  2.16 us
  transfers between devices with their start and end apart: 17, of which 8 were waited for; matrix products, arithmetic and copies ran while one was open for 5% of the time, Pallas kernels for 6%

profile of v7, /device:TPU:0, one launch (start us, length us, event | category | flops | bytes accessed | tf_op | source)
XLA Modules:
  0.0 64.1 jit_solution(14549176697191650427)
XLA Ops:
  0.0 1.0 %weights.1 = bf16[256,512]{1,0:T(8,128)(2,1)S(1)} custom-call(bf16[256,512]{1,0:T(8,128)(2,1)} %value_ref.3, bf16[256,512]{1,0:T(8,128)(2,1)} %noise_ref.3), custom_call_target="tpu_custom_call" | custom-call | bytes 524288 | tf_op jit(solution)/shard_map/weights/pallas_call | solution.py:419
  1.0 4.1 %collective-permute-start.2 = (bf16[256,512]{1,0:T(8,128)(2,1)S(1)}, bf16[256,512]{1,0:T(8,128)(2,1)S(1)}, u32[]{:S(2)}, u32[]{:S(2)}) collective-permute-start(bf16[256,512]{1,0:T(8,128)(2,1)S(1)} %weights.1), channel_id=1, source_target_pairs={{0,16},{8,24},{16,0},{24,8},{1,17},{9,25},{17,1},{25,9},{2,18},{10... | collective-permute-start | bytes 786440 | tf_op jit(solution)/shard_map/ppermute | solution.py:394
  5.1 2.2 %pack.1 = (bf16[256,512]{1,0:T(8,128)(2,1)S(1)}, bf16[128,1280]{1,0:T(8,128)(2,1)S(1)}, bf16[128,1280]{1,0:T(8,128)(2,1)S(1)}, bf16[128,1280]{1,0:T(8,128)(2,1)S(1)}, bf16[128,1280]{1,0:T(8,128)(2,1)S(1)}) custom-call(bf16[128,4096]{1,0:T(8,128)(2,1)} %tokens_ref, s32[128,256]{1,0:T(8,128)} %in_ref.1, s32[32,128]{1,0:T(8,128)} %bitcast.5, ...), custom_call_target="tpu_custom_call" | custom-call | flops 67108864 | bytes 3145728 | tf_op jit(solution)/shard_map/pack/pallas_call | solution.py:431
  7.3 1.6 %collective-permute-start = (bf16[128,1280]{1,0:T(8,128)(2,1)S(1)}, bf16[128,1280]{1,0:T(8,128)(2,1)S(1)}, u32[]{:S(2)}, u32[]{:S(2)}) collective-permute-start(bf16[128,1280]{1,0:T(8,128)(2,1)S(1)} %get-tuple-element.44), channel_id=1, source_target_pairs={{0,4},{2,6},{4,0},{6,2},{1,5},{3,7},{5,1},{7,3},{8,12},{10,14},{12... | collective-permute-start | bytes 983048 | tf_op jit(solution)/shard_map/ppermute | solution.py:394
  8.8 1.6 %collective-permute-start.1 = (bf16[256,512]{1,0:T(8,128)(2,1)S(1)}, bf16[256,512]{1,0:T(8,128)(2,1)S(1)}, u32[]{:S(2)}, u32[]{:S(2)}) collective-permute-start(bf16[256,512]{1,0:T(8,128)(2,1)S(1)} %get-tuple-element.45.refs_7_.refs_8_), channel_id=1, source_target_pairs={{0,8},{8,0},{16,24},{24,16},{1,9},{9,1},{17,25},{25,17},{2,10},{10... | collective-permute-start | bytes 786440 | tf_op jit(solution)/shard_map/ppermute | solution.py:394
  10.4 1.5 %collective-permute-start.4 = (bf16[128,1280]{1,0:T(8,128)(2,1)S(1)}, bf16[128,1280]{1,0:T(8,128)(2,1)S(1)}, u32[]{:S(2)}, u32[]{:S(2)}) collective-permute-start(bf16[128,1280]{1,0:T(8,128)(2,1)S(1)} %get-tuple-element.50), channel_id=1, source_target_pairs={{0,2},{2,0},{4,6},{6,4},{1,3},{3,1},{5,7},{7,5},{8,10},{10,8},{12,... | collective-permute-start | bytes 983048 | tf_op jit(solution)/shard_map/ppermute | solution.py:394
  12.4 4.7 %collective-permute-done.2.refs_9_.refs_10_ = bf16[256,512]{1,0:T(8,128)(2,1)S(1)} collective-permute-done((bf16[256,512]{1,0:T(8,128)(2,1)S(1)}, bf16[256,512]{1,0:T(8,128)(2,1)S(1)}, u32[]{:S(2)}, u32[]{:S(2)}) %collective-permute-start.2) | collective-permute-done | bytes 262176 | tf_op jit(solution)/shard_map/ppermute | solution.py:394
  17.8 3.2 %convolution_convert_fusion.gate_ref = bf16[128,512]{1,0:T(8,128)(2,1)S(1)} fusion(bf16[128,4096]{1,0:T(8,128)(2,1)} %tokens_ref, bf16[4096,512]{1,0:T(8,128)(2,1)} %param.14), kind=kOutput, calls=%fused_computation | convolution fusion | flops 536936448 | bytes 5373952 | tf_op jit(solution)/shard_map/dot_general | solution.py:472
  21.0 1.1 %collective-permute-done.1.refs_8_.refs_9_ = bf16[256,512]{1,0:T(8,128)(2,1)S(1)} collective-permute-done((bf16[256,512]{1,0:T(8,128)(2,1)S(1)}, bf16[256,512]{1,0:T(8,128)(2,1)S(1)}, u32[]{:S(2)}, u32[]{:S(2)}) %collective-permute-start.1) | collective-permute-done | bytes 262176 | tf_op jit(solution)/shard_map/ppermute | solution.py:394
  22.7 3.3 %collective-permute-done.8.refs_3_.refs_4_ = bf16[128,1280]{1,0:T(8,128)(2,1)S(1)} collective-permute-done((bf16[128,1280]{1,0:T(8,128)(2,1)S(1)}, bf16[128,1280]{1,0:T(8,128)(2,1)S(1)}, u32[]{:S(2)}, u32[]{:S(2)}) %collective-permute-start.8) | collective-permute-done | bytes 327712 | tf_op jit(solution)/shard_map/ppermute | solution.py:394
  26.4 1.7 %project.1 = (f32[896,256]{1,0:T(8,128)S(1)}, f32[896,256]{1,0:T(8,128)S(1)}, bf16[896,256]{1,0:T(8,128)(2,1)S(1)}, bf16[896,256]{1,0:T(8,128)(2,1)S(1)}, f32[64,512]{1,0:T(8,128)S(1)}) custom-call(bf16[128,1280]{1,0:T(8,128)(2,1)S(1)} %collective-permute-done.3.refs_0_.refs_1_, bf16[128,1280]{1,0:T(8,128)(2,1)S(1)} %collective-permute-done.5.refs_1_.refs_2_, ...), custom_call_target="tpu_custom_call" | custom-call | flops 704643072 | bytes 5242880 | tf_op jit(solution)/shard_map/project/pallas_call | solution.py:484
  28.2 0.8 %finish.1 = (bf16[64,1024]{1,0:T(8,128)(2,1)S(1)}, bf16[64,1024]{1,0:T(8,128)(2,1)S(1)}, bf16[64,1024]{1,0:T(8,128)(2,1)S(1)}, bf16[64,1024]{1,0:T(8,128)(2,1)S(1)}) custom-call(f32[896,256]{1,0:T(8,128)S(1)} %get-tuple-element.59.mean_ref, f32[896,256]{1,0:T(8,128)S(1)} %get-tuple-element.60.noise_ref, bf16[896,256]{1,0:T(8,128)(2,1)S(1)} %get-tuple-element.61.flip_ref, ...), custom_call_target="tpu_custom_call" | custom-call | flops 369098752 | bytes 3145728 | tf_op jit(solution)/shard_map/finish/pallas_call | solution.py:500
  29.0 2.1 %collective-permute-start.10 = (bf16[64,1024]{1,0:T(8,128)(2,1)S(1)}, bf16[64,1024]{1,0:T(8,128)(2,1)S(1)}, u32[]{:S(2)}, u32[]{:S(2)}) collective-permute-start(bf16[64,1024]{1,0:T(8,128)(2,1)S(1)} %get-tuple-element.64), channel_id=1, source_target_pairs={{0,6},{2,4},{4,2},{6,0},{1,7},{3,5},{5,3},{7,1},{8,14},{10,12},{12... | collective-permute-start | bytes 393224 | tf_op jit(solution)/shard_map/ppermute | solution.py:394
  31.2 0.9 %collective-permute-start.11 = (bf16[64,1024]{1,0:T(8,128)(2,1)S(1)}, bf16[64,1024]{1,0:T(8,128)(2,1)S(1)}, u32[]{:S(2)}, u32[]{:S(2)}) collective-permute-start(bf16[64,1024]{1,0:T(8,128)(2,1)S(1)} %get-tuple-element.65), channel_id=1, source_target_pairs={{0,4},{2,6},{4,0},{6,2},{1,5},{3,7},{5,1},{7,3},{8,12},{10,14},{12... | collective-permute-start | bytes 393224 | tf_op jit(solution)/shard_map/ppermute | solution.py:394
  32.6 3.4 %collective-permute-start.13 = (bf16[2,512]{1,0:T(2,128)(2,1)S(1)}, bf16[2,512]{1,0:T(2,128)(2,1)S(1)}, u32[]{:S(2)}, u32[]{:S(2)}) collective-permute-start(bf16[2,512]{1,0:T(2,128)(2,1)S(1)} %slice.3), channel_id=1, source_target_pairs={{0,2},{2,4},{4,6},{6,8},{8,10},{10,12},{12,14},{14,16},{16,18},{18... | collective-permute-start | bytes 6152 | tf_op jit(solution)/shard_map/ppermute | solution.py:512
  36.0 1.4 %collective-permute-done.13.before_ref = bf16[2,512]{1,0:T(2,128)(2,1)S(1)} collective-permute-done((bf16[2,512]{1,0:T(2,128)(2,1)S(1)}, bf16[2,512]{1,0:T(2,128)(2,1)S(1)}, u32[]{:S(2)}, u32[]{:S(2)}) %collective-permute-start.13) | collective-permute-done | bytes 2080 | tf_op jit(solution)/shard_map/ppermute | solution.py:512
  37.5 1.2 %collective-permute-done.11.refs_1_ = bf16[64,1024]{1,0:T(8,128)(2,1)S(1)} collective-permute-done((bf16[64,1024]{1,0:T(8,128)(2,1)S(1)}, bf16[64,1024]{1,0:T(8,128)(2,1)S(1)}, u32[]{:S(2)}, u32[]{:S(2)}) %collective-permute-start.11) | collective-permute-done | bytes 131104 | tf_op jit(solution)/shard_map/ppermute | solution.py:394
  38.8 3.6 %collective-permute-start.14 = (bf16[16,1536]{1,0:T(8,128)(2,1)S(1)}, bf16[16,1536]{1,0:T(8,128)(2,1)S(1)}, u32[]{:S(2)}, u32[]{:S(2)}) collective-permute-start(bf16[16,1536]{1,0:T(8,128)(2,1)S(1)} %get-tuple-element.77), channel_id=1, source_target_pairs={{0,24},{8,16},{16,8},{24,0},{1,25},{9,17},{17,9},{25,1},{2,26},{10... | collective-permute-start | bytes 147464 | tf_op jit(solution)/shard_map/ppermute | solution.py:394
  42.5 0.8 %collective-permute-start.16 = (bf16[16,1536]{1,0:T(8,128)(2,1)S(1)}, bf16[16,1536]{1,0:T(8,128)(2,1)S(1)}, u32[]{:S(2)}, u32[]{:S(2)}) collective-permute-start(bf16[16,1536]{1,0:T(8,128)(2,1)S(1)} %get-tuple-element.79), channel_id=1, source_target_pairs={{0,8},{8,0},{16,24},{24,16},{1,9},{9,1},{17,25},{25,17},{2,10},{10... | collective-permute-start | bytes 147464 | tf_op jit(solution)/shard_map/ppermute | solution.py:394
  43.4 1.6 %collective-permute-done.14.refs_0_ = bf16[16,1536]{1,0:T(8,128)(2,1)S(1)} collective-permute-done((bf16[16,1536]{1,0:T(8,128)(2,1)S(1)}, bf16[16,1536]{1,0:T(8,128)(2,1)S(1)}, u32[]{:S(2)}, u32[]{:S(2)}) %collective-permute-start.14) | collective-permute-done | bytes 49184 | tf_op jit(solution)/shard_map/ppermute | solution.py:394
  45.0 2.5 %collective-permute-done.15.refs_1_ = bf16[16,1536]{1,0:T(8,128)(2,1)S(1)} collective-permute-done((bf16[16,1536]{1,0:T(8,128)(2,1)S(1)}, bf16[16,1536]{1,0:T(8,128)(2,1)S(1)}, u32[]{:S(2)}, u32[]{:S(2)}) %collective-permute-start.15) | collective-permute-done | bytes 49184 | tf_op jit(solution)/shard_map/ppermute | solution.py:394
  47.5 2.5 %mix.1 = bf16[32,16,128]{2,1,0:T(8,128)(2,1)S(1)} custom-call(f32[3,1024]{1,0:T(4,128)S(1)} %copy-done, bf16[16,1536]{1,0:T(8,128)(2,1)S(1)} %collective-permute-done.14.refs_0_, bf16[16,1536]{1,0:T(8,128)(2,1)S(1)} %collective-permute-done.15.refs_1_, bf16[16,1536]{1,0:T(8,128)(2,1)S(1)} %collective-permute-done.16.refs_2_, ...), custom_call_target="tpu_custom_call" | custom-call | flops 536870912 | bytes 2097152 | tf_op jit(solution)/shard_map/mix/pallas_call | solution.py:548
  50.0 10.4 %all_to_all.5 = bf16[32,16,128]{2,1,0:T(8,128)(2,1)S(1)} all-to-all(bf16[32,16,128]{2,1,0:T(8,128)(2,1)S(1)} %mix.1), channel_id=1, replica_groups=mesh['far'=4,'near'=4,'dp'=2] {'dp','far','near'}, dimensions={0} | all-to-all | bytes 262144 | tf_op jit(solution)/shard_map/all_to_all | solution.py:565
  60.4 3.7 %project_out.1 = bf16[128,4096]{1,0:T(8,128)(2,1)} custom-call(f32[128,512]{1,0:T(8,128)S(1)} %gate.1.gate_ref, bf16[512,128]{1,0:T(8,128)(2,1)S(1)} %bitcast.4, bf16[512,4096]{1,0:T(8,128)(2,1)} %source_ref.1), custom_call_target="tpu_custom_call" | custom-call | flops 536870912 | bytes 5242880 | tf_op jit(solution)/shard_map/project_out/pallas_call | solution.py:567
  (23 shorter events, 2.9 us)
Async XLA Ops:
  1.0 16.1 %collective-permute-start.2 = (bf16[256,512]{1,0:T(8,128)(2,1)S(1)}, bf16[256,512]{1,0:T(8,128)(2,1)S(1)}, u32[]{:S(2)}, u32[]{:S(2)}) collective-permute-start(bf16[256,512]{1,0:T(8,128)(2,1)S(1)} %weights.1), channel_id=1, source_target_pairs={{0,16},{8,24},{16,0},{24,8},{1,17},{9,25},{17,1},{25,9},{2,18},{10... | collective-permute-start | bytes 786440 | tf_op jit(solution)/shard_map/ppermute | solution.py:394
  7.3 14.8 %collective-permute-start = (bf16[128,1280]{1,0:T(8,128)(2,1)S(1)}, bf16[128,1280]{1,0:T(8,128)(2,1)S(1)}, u32[]{:S(2)}, u32[]{:S(2)}) collective-permute-start(bf16[128,1280]{1,0:T(8,128)(2,1)S(1)} %get-tuple-element.44), channel_id=1, source_target_pairs={{0,4},{2,6},{4,0},{6,2},{1,5},{3,7},{5,1},{7,3},{8,12},{10,14},{12... | collective-permute-start | bytes 983048 | tf_op jit(solution)/shard_map/ppermute | solution.py:394
  8.8 13.2 %collective-permute-start.1 = (bf16[256,512]{1,0:T(8,128)(2,1)S(1)}, bf16[256,512]{1,0:T(8,128)(2,1)S(1)}, u32[]{:S(2)}, u32[]{:S(2)}) collective-permute-start(bf16[256,512]{1,0:T(8,128)(2,1)S(1)} %get-tuple-element.45.refs_7_.refs_8_), channel_id=1, source_target_pairs={{0,8},{8,0},{16,24},{24,16},{1,9},{9,1},{17,25},{25,17},{2,10},{10... | collective-permute-start | bytes 786440 | tf_op jit(solution)/shard_map/ppermute | solution.py:394
  10.4 12.2 %collective-permute-start.4 = (bf16[128,1280]{1,0:T(8,128)(2,1)S(1)}, bf16[128,1280]{1,0:T(8,128)(2,1)S(1)}, u32[]{:S(2)}, u32[]{:S(2)}) collective-permute-start(bf16[128,1280]{1,0:T(8,128)(2,1)S(1)} %get-tuple-element.50), channel_id=1, source_target_pairs={{0,2},{2,0},{4,6},{6,4},{1,3},{3,1},{5,7},{7,5},{8,10},{10,8},{12,... | collective-permute-start | bytes 983048 | tf_op jit(solution)/shard_map/ppermute | solution.py:394
  11.9 14.1 %collective-permute-start.8 = (bf16[128,1280]{1,0:T(8,128)(2,1)S(1)}, bf16[128,1280]{1,0:T(8,128)(2,1)S(1)}, u32[]{:S(2)}, u32[]{:S(2)}) collective-permute-start(bf16[128,1280]{1,0:T(8,128)(2,1)S(1)} %get-tuple-element.54), channel_id=1, source_target_pairs={{0,6},{2,4},{4,2},{6,0},{1,7},{3,5},{5,3},{7,1},{8,14},{10,12},{12... | collective-permute-start | bytes 983048 | tf_op jit(solution)/shard_map/ppermute | solution.py:394
  17.1 9.3 %collective-permute-start.7 = (bf16[256,512]{1,0:T(8,128)(2,1)S(1)}, bf16[256,512]{1,0:T(8,128)(2,1)S(1)}, u32[]{:S(2)}, u32[]{:S(2)}) collective-permute-start(bf16[256,512]{1,0:T(8,128)(2,1)S(1)} %collective-permute-done.2.refs_9_.refs_10_), channel_id=1, source_target_pairs={{0,8},{8,0},{16,24},{24,16},{1,9},{9,1},{17,25},{25,17},{2,10},{10... | collective-permute-start | bytes 786440 | tf_op jit(solution)/shard_map/ppermute | solution.py:394
  22.1 4.3 %collective-permute-start.6 = (bf16[128,1280]{1,0:T(8,128)(2,1)S(1)}, bf16[128,1280]{1,0:T(8,128)(2,1)S(1)}, u32[]{:S(2)}, u32[]{:S(2)}) collective-permute-start(bf16[128,1280]{1,0:T(8,128)(2,1)S(1)} %get-tuple-element.52.refs_6_.refs_7_), channel_id=1, source_target_pairs={{0,1},{1,0},{2,3},{3,2},{4,5},{5,4},{6,7},{7,6},{8,9},{9,8},{10,11... | collective-permute-start | bytes 983048 | tf_op jit(solution)/shard_map/ppermute | solution.py:394
  22.1 4.3 %collective-permute-start.3 = (bf16[128,1280]{1,0:T(8,128)(2,1)S(1)}, bf16[128,1280]{1,0:T(8,128)(2,1)S(1)}, u32[]{:S(2)}, u32[]{:S(2)}) collective-permute-start(bf16[128,1280]{1,0:T(8,128)(2,1)S(1)} %collective-permute-done.refs_4_.refs_5_), channel_id=1, source_target_pairs={{0,1},{1,0},{2,3},{3,2},{4,5},{5,4},{6,7},{7,6},{8,9},{9,8},{10,11... | collective-permute-start | bytes 983048 | tf_op jit(solution)/shard_map/ppermute | solution.py:394
  22.6 3.8 %collective-permute-start.5 = (bf16[128,1280]{1,0:T(8,128)(2,1)S(1)}, bf16[128,1280]{1,0:T(8,128)(2,1)S(1)}, u32[]{:S(2)}, u32[]{:S(2)}) collective-permute-start(bf16[128,1280]{1,0:T(8,128)(2,1)S(1)} %collective-permute-done.4.refs_5_.refs_6_), channel_id=1, source_target_pairs={{0,1},{1,0},{2,3},{3,2},{4,5},{5,4},{6,7},{7,6},{8,9},{9,8},{10,11... | collective-permute-start | bytes 983048 | tf_op jit(solution)/shard_map/ppermute | solution.py:394
  26.4 1.8 %collective-permute-start.9 = (bf16[128,1280]{1,0:T(8,128)(2,1)S(1)}, bf16[128,1280]{1,0:T(8,128)(2,1)S(1)}, u32[]{:S(2)}, u32[]{:S(2)}) collective-permute-start(bf16[128,1280]{1,0:T(8,128)(2,1)S(1)} %collective-permute-done.8.refs_3_.refs_4_), channel_id=1, source_target_pairs={{0,1},{1,0},{2,3},{3,2},{4,5},{5,4},{6,7},{7,6},{8,9},{9,8},{10,11... | collective-permute-start | bytes 983048 | tf_op jit(solution)/shard_map/ppermute | solution.py:394
  28.2 15.1 %copy-start = (f32[3,1024]{1,0:T(4,128)S(1)}, f32[3,1024]{1,0:T(4,128)}, u32[]{:S(2)}) copy-start(f32[3,1024]{1,0:T(4,128)} %taps_ref.3) | copy-start | bytes 36868
  29.0 8.4 %collective-permute-start.10 = (bf16[64,1024]{1,0:T(8,128)(2,1)S(1)}, bf16[64,1024]{1,0:T(8,128)(2,1)S(1)}, u32[]{:S(2)}, u32[]{:S(2)}) collective-permute-start(bf16[64,1024]{1,0:T(8,128)(2,1)S(1)} %get-tuple-element.64), channel_id=1, source_target_pairs={{0,6},{2,4},{4,2},{6,0},{1,7},{3,5},{5,3},{7,1},{8,14},{10,12},{12... | collective-permute-start | bytes 393224 | tf_op jit(solution)/shard_map/ppermute | solution.py:394
  31.2 7.6 %collective-permute-start.11 = (bf16[64,1024]{1,0:T(8,128)(2,1)S(1)}, bf16[64,1024]{1,0:T(8,128)(2,1)S(1)}, u32[]{:S(2)}, u32[]{:S(2)}) collective-permute-start(bf16[64,1024]{1,0:T(8,128)(2,1)S(1)} %get-tuple-element.65), channel_id=1, source_target_pairs={{0,4},{2,6},{4,0},{6,2},{1,5},{3,7},{5,1},{7,3},{8,12},{10,14},{12... | collective-permute-start | bytes 393224 | tf_op jit(solution)/shard_map/ppermute | solution.py:394
  32.1 6.6 %collective-permute-start.12 = (bf16[64,1024]{1,0:T(8,128)(2,1)S(1)}, bf16[64,1024]{1,0:T(8,128)(2,1)S(1)}, u32[]{:S(2)}, u32[]{:S(2)}) collective-permute-start(bf16[64,1024]{1,0:T(8,128)(2,1)S(1)} %get-tuple-element.66), channel_id=1, source_target_pairs={{0,2},{2,0},{4,6},{6,4},{1,3},{3,1},{5,7},{7,5},{8,10},{10,8},{12,... | collective-permute-start | bytes 393224 | tf_op jit(solution)/shard_map/ppermute | solution.py:394
  32.6 4.9 %collective-permute-start.13 = (bf16[2,512]{1,0:T(2,128)(2,1)S(1)}, bf16[2,512]{1,0:T(2,128)(2,1)S(1)}, u32[]{:S(2)}, u32[]{:S(2)}) collective-permute-start(bf16[2,512]{1,0:T(2,128)(2,1)S(1)} %slice.3), channel_id=1, source_target_pairs={{0,2},{2,4},{4,6},{6,8},{8,10},{10,12},{12,14},{14,16},{16,18},{18... | collective-permute-start | bytes 6152 | tf_op jit(solution)/shard_map/ppermute | solution.py:512
  38.8 6.2 %collective-permute-start.14 = (bf16[16,1536]{1,0:T(8,128)(2,1)S(1)}, bf16[16,1536]{1,0:T(8,128)(2,1)S(1)}, u32[]{:S(2)}, u32[]{:S(2)}) collective-permute-start(bf16[16,1536]{1,0:T(8,128)(2,1)S(1)} %get-tuple-element.77), channel_id=1, source_target_pairs={{0,24},{8,16},{16,8},{24,0},{1,25},{9,17},{17,9},{25,1},{2,26},{10... | collective-permute-start | bytes 147464 | tf_op jit(solution)/shard_map/ppermute | solution.py:394
  42.5 5.0 %collective-permute-start.15 = (bf16[16,1536]{1,0:T(8,128)(2,1)S(1)}, bf16[16,1536]{1,0:T(8,128)(2,1)S(1)}, u32[]{:S(2)}, u32[]{:S(2)}) collective-permute-start(bf16[16,1536]{1,0:T(8,128)(2,1)S(1)} %get-tuple-element.78), channel_id=1, source_target_pairs={{0,16},{8,24},{16,0},{24,8},{1,17},{9,25},{17,1},{25,9},{2,18},{10... | collective-permute-start | bytes 147464 | tf_op jit(solution)/shard_map/ppermute | solution.py:394
  42.5 5.0 %collective-permute-start.16 = (bf16[16,1536]{1,0:T(8,128)(2,1)S(1)}, bf16[16,1536]{1,0:T(8,128)(2,1)S(1)}, u32[]{:S(2)}, u32[]{:S(2)}) collective-permute-start(bf16[16,1536]{1,0:T(8,128)(2,1)S(1)} %get-tuple-element.79), channel_id=1, source_target_pairs={{0,8},{8,0},{16,24},{24,16},{1,9},{9,1},{17,25},{25,17},{2,10},{10... | collective-permute-start | bytes 147464 | tf_op jit(solution)/shard_map/ppermute | solution.py:394
